TPU v7x, 128 devices: a whole 4x4x4 slice. The times are simulated.
128 devices in a mesh: section: 2 (over y_lo), ctx: 32 (over z, x, core), shard: 2 (over y_hi).
Axes of the slice: x: 4, y: 4 (y_hi: 2, y_lo: 2; y = y_hi * 2 + y_lo), z: 4, core: 2. Of those that a mesh axis runs over, the one named last changes fastest.
Arguments:
- ends: float32 [2, 2, 2048, 1536], P('section', None, 'ctx'), may hold values from -6 to 6
- w_query: bfloat16 [2, 1536, 1536], P('section', 'ctx', 'shard'), may hold values from -0.15625 to 0.15625
- w_kv: bfloat16 [2, 1536, 2, 256], P('section', 'ctx', None, 'shard'), may hold values from -0.15625 to 0.15625
- w_out: bfloat16 [2, 1536, 1536], P('section', 'ctx', 'shard'), may hold values from -1.25 to 1.25
- w_gate_up: bfloat16 [2, 1536, 2, 8960], P('section', 'ctx', None, 'shard'), may hold values from -0.15625 to 0.15625
- w_down: bfloat16 [2, 1536, 8960], P('section', 'ctx', 'shard'), may hold values from -0.0625 to 0.0625
- gains: bfloat16 [2, 2, 1536], P('section', None, 'ctx'), may hold values from 0.5 to 1.5
- bias_query: bfloat16 [2, 12, 128], P('section', 'shard', 'ctx'), may hold values from -3 to 3
- bias_kv: bfloat16 [2, 2, 2, 128], P('section', None, 'shard', 'ctx'), may hold values from -3 to 3
Outputs:
- boundary: float32 [2, 2, 2048, 1536], P('section', None, 'ctx')
- grad_query: float32 [2, 1536, 1536], P('section', 'ctx', 'shard')
- grad_kv: float32 [2, 1536, 2, 256], P('section', 'ctx', None, 'shard')
- grad_out: float32 [2, 1536, 1536], P('section', 'ctx', 'shard')
- grad_gate_up: float32 [2, 1536, 2, 8960], P('section', 'ctx', None, 'shard')
- grad_down: float32 [2, 1536, 8960], P('section', 'ctx', 'shard')
- grad_gains: float32 [2, 2, 1536], P('section', None, 'ctx')
- grad_bias_query: float32 [2, 12, 128], P('section', 'shard', 'ctx')
- grad_bias_kv: float32 [2, 2, 2, 128], P('section', None, 'shard', 'ctx')
All inputs are finite; a program needn't handle non-finite values.
Results may differ from a plain program's by a relative error of at most 0.038.
Values may be sent and summed in bfloat16 or wider, within the bound.
A program may use at most 192 MiB of HBM per device.

v0:
```python
import jax
import jax.numpy as jnp
from jax import lax
from jax.sharding import PartitionSpec as P

HD = 128


EPS = 1e-06
THETA = 1000000.0


def shifted(shard, axis, by):
    count = lax.axis_size(axis)
    pairs = [(i, i + by) for i in range(count) if 0 <= i + by < count]
    return lax.ppermute(shard, axis, pairs)


def tables(offset, length, width):
    positions = (offset * length + jnp.arange(length, dtype=jnp.int32)).astype(jnp.float32)
    inverse = 1.0 / THETA ** (jnp.arange(0, width, 2, dtype=jnp.float32) / width)
    angles = positions[:, None] * inverse[None, :]
    angles = jnp.concatenate([angles, angles], axis=1)
    return (jnp.cos(angles), jnp.sin(angles))


def rotate(values, cos_table, sine_table):
    half_width = values.shape[-1] // 2
    turned = jnp.concatenate([-values[..., half_width:], values[..., :half_width]], axis=-1)
    return values * cos_table[:, None, :] + turned * sine_table[:, None, :]


def rotate_back(grad_rot, cos_table, sine_table):
    half_width = grad_rot.shape[-1] // 2
    scaled = grad_rot * sine_table[:, None, :]
    turned = jnp.concatenate([scaled[..., half_width:], -scaled[..., :half_width]], axis=-1)
    return grad_rot * cos_table[:, None, :] + turned


def contract_rows(left_side, right_side):
    return lax.dot_general(
        left_side, right_side, (((0,), (0,)), ((), ())), preferred_element_type=jnp.float32
    )


def contract_cols(left_side, right_side):
    return lax.dot_general(
        left_side, right_side, (((1,), (1,)), ((), ())), preferred_element_type=jnp.float32
    )


def scores_of(queries, all_keys, offset):
    row_count = queries.shape[0]
    scale = queries.shape[2] ** (-0.5)
    raw_scores = (
        jnp.einsum("qhd,kd->hqk", queries, all_keys, preferred_element_type=jnp.float32) * scale
    )
    query_pos = offset * row_count + jnp.arange(row_count, dtype=jnp.int32)
    key_pos = jnp.arange(all_keys.shape[0], dtype=jnp.int32)
    allowed = key_pos[None, :] <= query_pos[:, None]
    return jnp.where(allowed[None], raw_scores, -1e30)


def branch_total(partial_value):
    return lax.psum(partial_value.astype(jnp.bfloat16), "shard").astype(jnp.float32)


def input_total(partial_value):
    return lax.psum(partial_value.astype(jnp.bfloat16), "shard").astype(jnp.float32)


def layer_forward(inputs, gathered, cos_table, sine_table, offset):
    w_query, w_kv, w_out, w_gate_up, w_down, gains, bias_query, bias_kv = gathered
    row_count, model_width = inputs.shape
    size_head = cos_table.shape[1]
    head_count = w_query.shape[1] // size_head
    first_scale = lax.rsqrt(jnp.mean(inputs * inputs, axis=1, keepdims=True) + EPS)
    first_normed = inputs * first_scale
    hidden = (first_normed * gains[0].astype(jnp.float32)).astype(jnp.bfloat16)
    query_proj = jnp.dot(hidden, w_query, preferred_element_type=jnp.float32) + bias_query.reshape(
        -1
    ).astype(jnp.float32)
    key_value = jnp.dot(
        hidden, w_kv.reshape(model_width, -1), preferred_element_type=jnp.float32
    ) + bias_kv.reshape(-1).astype(jnp.float32)
    queries = rotate(
        query_proj.reshape(row_count, head_count, size_head), cos_table, sine_table
    ).astype(jnp.bfloat16)
    own_keys = (
        rotate(key_value[:, :size_head].reshape(row_count, 1, size_head), cos_table, sine_table)
        .reshape(row_count, size_head)
        .astype(jnp.bfloat16)
    )
    own_values = key_value[:, size_head:].astype(jnp.bfloat16)
    all_keys, all_values = (
        lax.all_gather(own_keys, "ctx", axis=0, tiled=True),
        lax.all_gather(own_values, "ctx", axis=0, tiled=True),
    )
    scores = scores_of(queries, all_keys, offset)
    row_max = jnp.max(scores, axis=2, keepdims=True)
    log_total = row_max + jnp.log(jnp.sum(jnp.exp(scores - row_max), axis=2, keepdims=True))
    soft_low = jnp.exp(scores - log_total).astype(jnp.bfloat16)
    attended = jnp.einsum("hqk,kd->qhd", soft_low, all_values, preferred_element_type=jnp.float32)
    attended = attended.reshape(row_count, -1).astype(jnp.bfloat16)
    residual_mid = inputs + branch_total(contract_cols(attended, w_out))
    second_scale = lax.rsqrt(jnp.mean(residual_mid * residual_mid, axis=1, keepdims=True) + EPS)
    second_normed = residual_mid * second_scale
    hidden2 = (second_normed * gains[1].astype(jnp.float32)).astype(jnp.bfloat16)
    gate_up = jnp.einsum("td,dcf->tcf", hidden2, w_gate_up, preferred_element_type=jnp.float32)
    gate_part = gate_up[:, 0]
    up_part = gate_up[:, 1]
    product = (jax.nn.silu(gate_part) * up_part).astype(jnp.bfloat16)
    result = residual_mid + branch_total(contract_cols(product, w_down))
    saved_state = (
        first_normed,
        first_scale,
        hidden,
        queries,
        all_keys,
        all_values,
        log_total,
        attended,
        second_normed,
        second_scale,
        hidden2,
        gate_part,
        up_part,
        product,
    )
    return (result, saved_state)


def layer_backward(grad_out, saved_state, gathered, cos_table, sine_table, offset):
    w_query, w_kv, w_out, w_gate_up, w_down, gains, bias_query, bias_kv = gathered
    (
        first_normed,
        first_scale,
        hidden,
        queries,
        all_keys,
        all_values,
        log_total,
        attended,
        second_normed,
        second_scale,
        hidden2,
        gate_part,
        up_part,
        product,
    ) = saved_state
    row_count, model_width = grad_out.shape
    size_head = cos_table.shape[1]
    head_count = queries.shape[1]
    grad_low = grad_out.astype(jnp.bfloat16)
    grad_product = jnp.dot(grad_low, w_down, preferred_element_type=jnp.float32)
    sigma = jax.nn.sigmoid(gate_part)
    grad_gate = grad_product * up_part * sigma * (1.0 + gate_part * (1.0 - sigma))
    grad_up = grad_product * gate_part * sigma
    grad_gate_up = jnp.stack([grad_gate, grad_up], axis=1).astype(jnp.bfloat16)
    grad_hidden2 = input_total(
        jnp.einsum("tcf,dcf->td", grad_gate_up, w_gate_up, preferred_element_type=jnp.float32)
    )
    scaled_second = grad_hidden2 * gains[1].astype(jnp.float32)
    grad_mid = grad_out + second_scale * (
        scaled_second
        - second_normed * jnp.mean(scaled_second * second_normed, axis=1, keepdims=True)
    )
    grad_mid_low = grad_mid.astype(jnp.bfloat16)
    grad_attended = jnp.dot(grad_mid_low, w_out, preferred_element_type=jnp.float32).astype(
        jnp.bfloat16
    )
    grad_attended = grad_attended.reshape(row_count, head_count, size_head)
    scores = scores_of(queries, all_keys, offset)
    soft_full = jnp.exp(scores - log_total)
    grad_soft = jnp.einsum(
        "qhd,kd->hqk", grad_attended, all_values, preferred_element_type=jnp.float32
    )
    grad_scores = (
        soft_full * (grad_soft - jnp.sum(soft_full * grad_soft, axis=2, keepdims=True))
    ).astype(jnp.bfloat16)
    scale = size_head ** (-0.5)
    grad_queries = (
        jnp.einsum("hqk,kd->qhd", grad_scores, all_keys, preferred_element_type=jnp.float32) * scale
    )
    grad_keys = (
        jnp.einsum("hqk,qhd->kd", grad_scores, queries, preferred_element_type=jnp.float32) * scale
    )
    grad_values = jnp.einsum(
        "hqk,qhd->kd",
        soft_full.astype(jnp.bfloat16),
        grad_attended,
        preferred_element_type=jnp.float32,
    )
    own_grad_keys, own_grad_values = (
        lax.psum_scatter(
            grad_keys.astype(jnp.bfloat16), "ctx", scatter_dimension=0, tiled=True
        ).astype(jnp.float32),
        lax.psum_scatter(
            grad_values.astype(jnp.bfloat16), "ctx", scatter_dimension=0, tiled=True
        ).astype(jnp.float32),
    )
    grad_query_low = (
        rotate_back(grad_queries, cos_table, sine_table).reshape(row_count, -1).astype(jnp.bfloat16)
    )
    grad_key_rot = rotate_back(
        own_grad_keys.reshape(row_count, 1, size_head), cos_table, sine_table
    ).reshape(row_count, size_head)
    grad_kv_low = jnp.concatenate([grad_key_rot, own_grad_values], axis=1).astype(jnp.bfloat16)
    grad_hidden = input_total(
        contract_cols(grad_query_low, w_query)
        + contract_cols(grad_kv_low, w_kv.reshape(model_width, -1))
    )
    scaled_first = grad_hidden * gains[0].astype(jnp.float32)
    grad_in = grad_mid + first_scale * (
        scaled_first - first_normed * jnp.mean(scaled_first * first_normed, axis=1, keepdims=True)
    )
    gain_terms = jnp.stack(
        [jnp.sum(grad_hidden * first_normed, axis=0), jnp.sum(grad_hidden2 * second_normed, axis=0)]
    )
    bias_terms = jnp.concatenate(
        [
            jnp.sum(grad_query_low.astype(jnp.float32), axis=0).reshape(-1, size_head),
            jnp.sum(grad_kv_low.astype(jnp.float32), axis=0).reshape(-1, size_head),
        ],
        axis=0,
    )
    products = (
        hidden,
        grad_query_low,
        grad_kv_low,
        grad_mid_low,
        attended,
        hidden2,
        grad_gate_up.reshape(row_count, -1),
        grad_low,
        product,
    )
    return (grad_in, (products, gain_terms, bias_terms))


def pairs_of(fields):
    (
        hidden_all,
        grad_query_all,
        grad_kv_all,
        grad_mid_all,
        attended_all,
        hidden2_all,
        grad_gate_up_all,
        grad_low_all,
        product_all,
    ) = fields
    return (
        (hidden_all, grad_query_all),
        (hidden_all, grad_kv_all),
        (grad_mid_all, attended_all),
        (hidden2_all, grad_gate_up_all),
        (grad_low_all, product_all),
    )


def term_maker(pairs):
    blocks = [contract_rows(left_side, right_side) for left_side, right_side in pairs]
    return jnp.concatenate(blocks, axis=1)


def body(ends, w_query, w_kv, w_out, w_gate_up, w_down, gains, bias_query, bias_kv):
    pieces = (
        w_query[0],
        w_kv[0],
        w_out[0],
        w_gate_up[0],
        w_down[0],
        gains[0],
        bias_query[0],
        bias_kv[0],
    )
    gathered = (
        lax.all_gather(pieces[0], "ctx", axis=0, tiled=True),
        lax.all_gather(pieces[1], "ctx", axis=0, tiled=True),
        lax.all_gather(pieces[2], "ctx", axis=0, tiled=True),
        lax.all_gather(pieces[3], "ctx", axis=0, tiled=True),
        lax.all_gather(pieces[4], "ctx", axis=0, tiled=True),
        lax.all_gather(pieces[5], "ctx", axis=1, tiled=True),
        lax.all_gather(pieces[6], "ctx", axis=1, tiled=True),
        lax.all_gather(pieces[7], "ctx", axis=2, tiled=True),
    )
    section = lax.axis_index("section")
    offset = lax.axis_index("ctx")
    local = ends[0]
    micro_count, row_count, model_width = local.shape
    cos_table, sine_table = tables(offset, row_count, HD)
    first_section = section == 0
    received = jnp.zeros((row_count, model_width), jnp.float32)
    states = []
    outputs = []
    for tick in range(micro_count + 1):
        inputs = jnp.where(first_section, local[min(tick, micro_count - 1)], received)
        result, saved_state = layer_forward(inputs, gathered, cos_table, sine_table, offset)
        states.append(saved_state)
        outputs.append(result)
        if tick < micro_count:
            received = shifted(result.astype(jnp.bfloat16), "section", 1).astype(jnp.float32)
    gathered = (
        lax.all_gather(pieces[0], "ctx", axis=0, tiled=True),
        lax.all_gather(pieces[1], "ctx", axis=0, tiled=True),
        lax.all_gather(pieces[2], "ctx", axis=0, tiled=True),
        lax.all_gather(pieces[3], "ctx", axis=0, tiled=True),
        lax.all_gather(pieces[4], "ctx", axis=0, tiled=True),
        lax.all_gather(pieces[5], "ctx", axis=1, tiled=True),
        lax.all_gather(pieces[6], "ctx", axis=1, tiled=True),
        lax.all_gather(pieces[7], "ctx", axis=2, tiled=True),
    )
    returned = jnp.zeros((row_count, model_width), jnp.float32)
    grads_in = []
    collected = []
    chosen = [None] * micro_count
    for tick in range(micro_count + 1):
        grad_out = jnp.where(first_section, returned, local[max(micro_count - 1 - tick, 0)])
        grad_in, terms = layer_backward(
            grad_out, states[micro_count - tick], gathered, cos_table, sine_table, offset
        )
        grads_in.append(grad_in)
        collected.append(terms)
        if tick >= 1:
            entry = jax.tree.map(
                lambda early, late: jnp.where(first_section, early, late),
                collected[tick],
                collected[tick - 1],
            )
            chosen[micro_count - tick] = entry
        if tick < micro_count:
            returned = shifted(grad_in.astype(jnp.bfloat16), "section", -1).astype(jnp.float32)
    boundary = jnp.stack(
        [
            jnp.where(first_section, grads_in[micro_count - index], outputs[index + 1])
            for index in range(micro_count)
        ]
    )[None]
    gain_sum = chosen[0][1]
    bias_sum = chosen[0][2]
    for entry in chosen[1:]:
        gain_sum = gain_sum + entry[1]
        bias_sum = bias_sum + entry[2]
    stacked = tuple(
        (jnp.concatenate([entry[0][field] for entry in chosen], axis=0) for field in range(9))
    )
    own_rows = lax.psum_scatter(
        term_maker(pairs_of(stacked)).astype(jnp.bfloat16), "ctx", scatter_dimension=0, tiled=True
    ).astype(jnp.float32)
    row_part = own_rows.shape[0]
    width_query = w_query.shape[2]
    width_kv = w_kv.shape[2] * w_kv.shape[3]
    width_out = w_out.shape[2]
    width_gate_up = w_gate_up.shape[2] * w_gate_up.shape[3]
    edge_two = width_query + width_kv
    edge_three = edge_two + width_out
    edge_four = edge_three + width_gate_up
    grad_query = own_rows[:, :width_query][None]
    grad_kv = own_rows[:, width_query:edge_two].reshape(1, row_part, w_kv.shape[2], w_kv.shape[3])
    grad_out = own_rows[:, edge_two:edge_three][None]
    grad_gate_up = own_rows[:, edge_three:edge_four].reshape(
        1, row_part, w_gate_up.shape[2], w_gate_up.shape[3]
    )
    grad_down = own_rows[:, edge_four:][None]
    gain_part, bias_part = (
        lax.psum_scatter(gain_sum, "ctx", scatter_dimension=1, tiled=True),
        lax.psum_scatter(bias_sum, "ctx", scatter_dimension=1, tiled=True),
    )
    head_count = bias_query.shape[1]
    grad_gains = gain_part[None]
    grad_bias_query = bias_part[:head_count][None]
    grad_bias_kv = bias_part[head_count:].reshape(1, 2, 1, -1)
    return (
        boundary,
        grad_query,
        grad_kv,
        grad_out,
        grad_gate_up,
        grad_down,
        grad_gains,
        grad_bias_query,
        grad_bias_kv,
    )


def solution(mesh):
    placed = (
        P("section", None, "ctx", None),
        P("section", "ctx", "shard"),
        P("section", "ctx", None, "shard"),
        P("section", "ctx", "shard"),
        P("section", "ctx", None, "shard"),
        P("section", "ctx", "shard"),
        P("section", None, "ctx"),
        P("section", "shard", "ctx"),
        P("section", None, "shard", "ctx"),
    )
    return jax.shard_map(
        body,
        mesh=mesh,
        in_specs=placed,
        out_specs=(
            P("section", None, "ctx", None),
            P("section", "ctx", "shard"),
            P("section", "ctx", None, "shard"),
            P("section", "ctx", "shard"),
            P("section", "ctx", None, "shard"),
            P("section", "ctx", "shard"),
            P("section", None, "ctx"),
            P("section", "shard", "ctx"),
            P("section", None, "shard", "ctx"),
        ),
        check_vma=False,
    )
```

profile of v0, /device:TPU:1, one launch (start us, length us, event | category | flops | bytes accessed | tf_op | source)
XLA Modules:
  0.0 1789.6 jit_solution(3728853374332114934)
XLA Ops:
  12.1 26.8 %all-gather.2 = bf16[1,2,1,128]{2,1,0,3:T(2,128)(2,1)S(1)} all-gather(bf16[1,2,1,4]{2,1,0,3:T(2,128)(2,1)S(1)} %copy.131), channel_id=4, replica_groups=mesh['section'=2,'ctx'=32,'shard'=2] {'ctx'}, dimensions={3}, use_global_device_ids=true | all-gather | bytes 528 | tf_op jit(solution)/shard_map/all_gather | solution.py:286
  39.0 23.5 %all-gather.4 = bf16[1,6,128]{1,0,2:T(2,128)(2,1)S(1)} all-gather(bf16[1,6,4]{1,0,2:T(2,128)(2,1)S(1)} %copy.133), channel_id=6, replica_groups=mesh['section'=2,'ctx'=32,'shard'=2] {'ctx'}, dimensions={2}, use_global_device_ids=true | all-gather | bytes 1584 | tf_op jit(solution)/shard_map/all_gather | solution.py:285
  62.6 22.7 %all-gather = bf16[1,2,1536]{1,0,2:T(2,128)(2,1)S(1)} all-gather(bf16[1,2,48]{1,0,2:T(2,128)(2,1)S(1)} %copy.129), channel_id=2, replica_groups=mesh['section'=2,'ctx'=32,'shard'=2] {'ctx'}, dimensions={2}, use_global_device_ids=true | all-gather | bytes 6336 | tf_op jit(solution)/shard_map/all_gather | solution.py:284
  85.3 24.8 %all-gather.1 = bf16[1,1536,2,128]{3,2,0,1:T(2,128)(2,1)S(1)} all-gather(bf16[1,48,2,128]{3,2,0,1:T(2,128)(2,1)} %bitcast.572), channel_id=3, replica_groups=mesh['section'=2,'ctx'=32,'shard'=2] {'ctx'}, dimensions={1}, use_global_device_ids=true | all-gather | bytes 811008 | tf_op jit(solution)/shard_map/all_gather | solution.py:280
  110.1 25.1 %fusion.170 = (f32[1536]{0:T(1024)S(1)}, f32[1536]{0:T(1024)S(1)}) fusion(bf16[1,2,1536]{1,0,2:T(2,128)(2,1)S(1)} %all-gather), kind=kLoop, calls=%fused_computation.176 | loop fusion | flops 3072 | bytes 18432 | tf_op jit(solution)/shard_map/mul | solution.py:108
  136.4 22.7 %all_gather.52 = bf16[2048,128]{1,0:T(8,128)(2,1)S(1)} all-gather(bf16[64,128]{1,0:T(8,128)(2,1)S(1)} %get-tuple-element.147), channel_id=1, replica_groups=mesh['section'=2,'ctx'=32,'shard'=2] {'ctx'}, dimensions={0}, use_global_device_ids=true | all-gather | bytes 540672 | tf_op jit(solution)/shard_map/all_gather | solution.py:96
  159.0 24.2 %all_gather.51 = bf16[2048,128]{1,0:T(8,128)(2,1)S(1)} all-gather(bf16[64,128]{1,0:T(8,128)(2,1)S(1)} %slice.376), channel_id=1, replica_groups=mesh['section'=2,'ctx'=32,'shard'=2] {'ctx'}, dimensions={0}, use_global_device_ids=true | all-gather | bytes 540672 | tf_op jit(solution)/shard_map/all_gather | solution.py:97
  194.1 26.5 %all-reduce.14.cloned.1.call-done = bf16[64,1536]{1,0:T(8,128)(2,1)} async-done(((bf16[64,1536]{1,0:T(8,128)(2,1)}), bf16[64,1536]{1,0:T(8,128)(2,1)}) %all-reduce.14.cloned.1.call-update) | async-done | bytes 196624 | tf_op jit(solution)/shard_map/psum | solution.py:65
  221.7 100.2 %all-gather.17.cloned.1.call-done = bf16[1,1536,2,4480]{3,1,2,0:T(8,128)(2,1)} async-done(((bf16[1,48,2,4480]{3,1,2,0:T(8,128)(2,1)}), bf16[1,1536,2,4480]{3,1,2,0:T(8,128)(2,1)}) %all-gather.17.cloned.1.call-update) | async-done | bytes 27525136 | tf_op jit(solution)/shard_map/all_gather | solution.py:282
  321.9 11.4 fusion.11
  333.3 55.8 %all-gather.19.cloned.1.call-done = bf16[1,1536,4480]{2,1,0:T(8,128)(2,1)} async-done(((bf16[1,48,4480]{2,1,0:T(8,128)(2,1)}), bf16[1,1536,4480]{2,1,0:T(8,128)(2,1)}) %all-gather.19.cloned.1.call-update) | async-done | bytes 13762576 | tf_op jit(solution)/shard_map/all_gather | solution.py:283
  389.2 9.8 fusion.116
  399.1 29.0 %all-reduce.16.cloned.1.call-done = bf16[64,1536]{1,0:T(8,128)(2,1)} async-done(((bf16[64,1536]{1,0:T(8,128)(2,1)}), bf16[64,1536]{1,0:T(8,128)(2,1)}) %all-reduce.16.cloned.1.call-update) | async-done | bytes 196624 | tf_op jit(solution)/shard_map/psum | solution.py:65
  437.7 27.1 %all_gather.59 = bf16[2048,128]{1,0:T(8,128)(2,1)S(1)} all-gather(bf16[64,128]{1,0:T(8,128)(2,1)S(1)} %fusion.330), channel_id=1, replica_groups=mesh['section'=2,'ctx'=32,'shard'=2] {'ctx'}, dimensions={0}, use_global_device_ids=true | all-gather | bytes 540672 | tf_op jit(solution)/shard_map/all_gather | solution.py:96
  464.7 24.1 %all_gather.58 = bf16[2048,128]{1,0:T(8,128)(2,1)S(1)} all-gather(bf16[64,128]{1,0:T(8,128)(2,1)S(1)} %slice.375), channel_id=1, replica_groups=mesh['section'=2,'ctx'=32,'shard'=2] {'ctx'}, dimensions={0}, use_global_device_ids=true | all-gather | bytes 540672 | tf_op jit(solution)/shard_map/all_gather | solution.py:97
  494.3 28.1 %all-reduce.18.cloned.1.call-done = bf16[64,1536]{1,0:T(8,128)(2,1)} async-done(((bf16[64,1536]{1,0:T(8,128)(2,1)}), bf16[64,1536]{1,0:T(8,128)(2,1)}) %all-reduce.18.cloned.1.call-update) | async-done | bytes 196624 | tf_op jit(solution)/shard_map/psum | solution.py:65
  525.1 11.5 fusion.9
  539.1 4.9 fusion.119
  544.1 29.9 %all-reduce.20.cloned.1.call-done = bf16[64,1536]{1,0:T(8,128)(2,1)} async-done(((bf16[64,1536]{1,0:T(8,128)(2,1)}), bf16[64,1536]{1,0:T(8,128)(2,1)}) %all-reduce.20.cloned.1.call-update) | async-done | bytes 196624 | tf_op jit(solution)/shard_map/psum | solution.py:65
  586.4 27.3 %all_gather.61 = bf16[2048,128]{1,0:T(8,128)(2,1)S(1)} all-gather(bf16[64,128]{1,0:T(8,128)(2,1)S(1)} %fusion.332), channel_id=1, replica_groups=mesh['section'=2,'ctx'=32,'shard'=2] {'ctx'}, dimensions={0}, use_global_device_ids=true | all-gather | bytes 540672 | tf_op jit(solution)/shard_map/all_gather | solution.py:96
  613.6 24.1 %all_gather.60 = bf16[2048,128]{1,0:T(8,128)(2,1)S(1)} all-gather(bf16[64,128]{1,0:T(8,128)(2,1)S(1)} %slice.374), channel_id=1, replica_groups=mesh['section'=2,'ctx'=32,'shard'=2] {'ctx'}, dimensions={0}, use_global_device_ids=true | all-gather | bytes 540672 | tf_op jit(solution)/shard_map/all_gather | solution.py:97
  643.2 27.2 %all-reduce.22.cloned.1.call-done = bf16[64,1536]{1,0:T(8,128)(2,1)} async-done(((bf16[64,1536]{1,0:T(8,128)(2,1)}), bf16[64,1536]{1,0:T(8,128)(2,1)}) %all-reduce.22.cloned.1.call-update) | async-done | bytes 196624 | tf_op jit(solution)/shard_map/psum | solution.py:65
  671.7 13.0 fusion.7
  685.3 5.6 multiply_bitcast_fusion.5
  690.9 14.4 fusion.95
  705.6 29.7 %all-reduce.24.cloned.1.call-done = bf16[64,1536]{1,0:T(8,128)(2,1)} async-done(((bf16[64,1536]{1,0:T(8,128)(2,1)}), bf16[64,1536]{1,0:T(8,128)(2,1)}) %all-reduce.24.cloned.1.call-update) | async-done | bytes 196624 | tf_op jit(solution)/shard_map/psum | solution.py:69
  749.1 71.6 %reduce-scatter.12.cloned.1.call-done = bf16[64,128]{1,0:T(8,128)(2,1)} async-done(((bf16[2048,128]{1,0:T(8,128)(2,1)}), bf16[64,128]{1,0:T(8,128)(2,1)}) %reduce-scatter.12.cloned.1.call-update) | async-done | bytes 16400 | tf_op jit(solution)/shard_map/reduce_scatter | solution.py:195
  826.9 73.6 %reduce-scatter.14.cloned.1.call-done = bf16[64,128]{1,0:T(8,128)(2,1)} async-done(((bf16[2048,128]{1,0:T(8,128)(2,1)}), bf16[64,128]{1,0:T(8,128)(2,1)}) %reduce-scatter.14.cloned.1.call-update) | async-done | bytes 16400 | tf_op jit(solution)/shard_map/reduce_scatter | solution.py:198
  904.4 31.1 %all-reduce.26.cloned.1.call-done = bf16[64,1536]{1,0:T(8,128)(2,1)} async-done(((bf16[64,1536]{1,0:T(8,128)(2,1)}), bf16[64,1536]{1,0:T(8,128)(2,1)}) %all-reduce.26.cloned.1.call-update) | async-done | bytes 196624 | tf_op jit(solution)/shard_map/psum | solution.py:69
  940.0 5.9 collective-permute-done.2
  946.6 8.6 multiply_bitcast_fusion.3
  955.2 14.6 fusion.92
  970.0 30.0 %all-reduce.28.cloned.1.call-done = bf16[64,1536]{1,0:T(8,128)(2,1)} async-done(((bf16[64,1536]{1,0:T(8,128)(2,1)}), bf16[64,1536]{1,0:T(8,128)(2,1)}) %all-reduce.28.cloned.1.call-update) | async-done | bytes 196624 | tf_op jit(solution)/shard_map/psum | solution.py:69
  1018.8 67.4 %reduce-scatter.16.cloned.1.call-done = bf16[64,128]{1,0:T(8,128)(2,1)} async-done(((bf16[2048,128]{1,0:T(8,128)(2,1)}), bf16[64,128]{1,0:T(8,128)(2,1)}) %reduce-scatter.16.cloned.1.call-update) | async-done | bytes 16400 | tf_op jit(solution)/shard_map/reduce_scatter | solution.py:195
  1088.7 77.7 %reduce-scatter.18.cloned.1.call-done = bf16[64,128]{1,0:T(8,128)(2,1)} async-done(((bf16[2048,128]{1,0:T(8,128)(2,1)}), bf16[64,128]{1,0:T(8,128)(2,1)}) %reduce-scatter.18.cloned.1.call-update) | async-done | bytes 16400 | tf_op jit(solution)/shard_map/reduce_scatter | solution.py:198
  1172.1 29.2 %all-reduce.30.cloned.1.call-done = bf16[64,1536]{1,0:T(8,128)(2,1)} async-done(((bf16[64,1536]{1,0:T(8,128)(2,1)}), bf16[64,1536]{1,0:T(8,128)(2,1)}) %all-reduce.30.cloned.1.call-update) | async-done | bytes 196624 | tf_op jit(solution)/shard_map/psum | solution.py:69
  1205.1 10.2 fusion.122
  1217.7 8.5 multiply_bitcast_fusion.1
  1226.3 14.5 fusion.89
  1245.7 26.5 %all-reduce.32.cloned.1.call-done = bf16[64,1536]{1,0:T(8,128)(2,1)} async-done(((bf16[64,1536]{1,0:T(8,128)(2,1)}), bf16[64,1536]{1,0:T(8,128)(2,1)}) %all-reduce.32.cloned.1.call-update) | async-done | bytes 196624 | tf_op jit(solution)/shard_map/psum | solution.py:69
  1301.6 4.4 copy.158
  1306.0 51.6 %reduce-scatter.20.cloned.1.call-done = bf16[64,128]{1,0:T(8,128)(2,1)} async-done(((bf16[2048,128]{1,0:T(8,128)(2,1)}), bf16[64,128]{1,0:T(8,128)(2,1)}) %reduce-scatter.20.cloned.1.call-update) | async-done | bytes 16400 | tf_op jit(solution)/shard_map/reduce_scatter | solution.py:195
  1359.5 78.3 %reduce-scatter.22.cloned.1.call-done = bf16[64,128]{1,0:T(8,128)(2,1)} async-done(((bf16[2048,128]{1,0:T(8,128)(2,1)}), bf16[64,128]{1,0:T(8,128)(2,1)}) %reduce-scatter.22.cloned.1.call-update) | async-done | bytes 16400 | tf_op jit(solution)/shard_map/reduce_scatter | solution.py:198
  1453.0 12.9 fusion
  1466.0 16.4 all-reduce.34.cloned.1.call-done
  1485.0 7.0 fusion.13
  1494.0 62.9 %all-reduce = f32[8,128]{1,0:T(8,128)S(1)} all-reduce(f32[8,128]{1,0:T(8,128)S(1)} %fusion.336), channel_id=18, replica_groups=mesh['section'=2,'ctx'=32,'shard'=2] {'ctx'}, use_global_device_ids=true, to_apply=%region_53.54.clone | all-reduce | flops 1024 | bytes 8192
  1563.5 213.0 %reduce-scatter.24.cloned.1.call-done = bf16[48,15232]{1,0:T(8,128)(2,1)} async-done(((bf16[1536,15232]{1,0:T(8,128)(2,1)}), bf16[48,15232]{1,0:T(8,128)(2,1)}) %reduce-scatter.24.cloned.1.call-update) | async-done | bytes 1462288 | tf_op jit(solution)/shard_map/reduce_scatter | solution.py:348
  (560 shorter events, 187.4 us)
Async XLA Ops:
  7.2 128.1 %copy-start.14 = (f32[1,2,64,1536]{3,2,1,0:T(8,128)S(1)}, f32[1,2,64,1536]{3,2,1,0:T(8,128)}, u32[]{:S(2)}) copy-start(f32[1,2,64,1536]{3,2,1,0:T(8,128)} %param.9) | copy-start | bytes 2359300
  7.2 176.2 %all-gather.13.cloned.1.call-start = ((), (), s32[]{:S(2)}) async-start(), calls=%async_computation.25 | async-start | bytes 2433024 | tf_op jit(solution)/shard_map/all_gather | solution.py:279
  7.9 181.2 %all-gather.15.cloned.1.call-start = ((), (), s32[]{:S(2)}) async-start(), calls=%async_computation.26 | async-start | bytes 2433024 | tf_op jit(solution)/shard_map/all_gather | solution.py:281
  8.7 211.9 %all-reduce.14.cloned.1.call-start = ((), (), s32[]{:S(2)}) async-start(), calls=%async_computation.8 | async-start | bytes 393216 | tf_op jit(solution)/shard_map/psum | solution.py:65
  9.9 173.5 %copy-start.148 = (f32[64]{0:T(128)}, f32[64]{0:T(128)S(1)}, u32[]{:S(2)}) copy-start(f32[64]{0:T(128)S(1)} %add_rsqrt_fusion.5) | copy-start | bytes 772
  39.0 96.6 %copy-start.154 = (f32[256]{0:T(256)}, f32[256]{0:T(256)S(1)}, u32[]{:S(2)}) copy-start(f32[256]{0:T(256)S(1)} %bitcast_convert_fusion.1) | copy-start | bytes 3076
  192.4 129.5 %all-gather.17.cloned.1.call-start = ((), (), s32[]{:S(2)}) async-start(), calls=%async_computation.27 | async-start | bytes 28385280 | tf_op jit(solution)/shard_map/all_gather | solution.py:282
  193.5 195.7 %all-gather.19.cloned.1.call-start = ((), (), s32[]{:S(2)}) async-start(), calls=%async_computation.28 | async-start | bytes 14192640 | tf_op jit(solution)/shard_map/all_gather | solution.py:283
  194.1 234.1 %all-reduce.16.cloned.1.call-start = ((), (), s32[]{:S(2)}) async-start(), calls=%async_computation.9 | async-start | bytes 393216 | tf_op jit(solution)/shard_map/psum | solution.py:65
  221.7 301.9 %copy-start.22 = (f32[64,1536]{1,0:T(8,128)}, f32[64,1536]{1,0:T(8,128)S(1)}, u32[]{:S(2)}) copy-start(f32[64,1536]{1,0:T(8,128)S(1)} %get-tuple-element.101) | copy-start | bytes 1179652
  221.7 111.6 %copy-start.143 = (f32[64]{0:T(128)}, f32[64]{0:T(128)S(1)}, u32[]{:S(2)}) copy-start(f32[64]{0:T(128)S(1)} %add_rsqrt_fusion.4) | copy-start | bytes 772
  399.0 123.4 %all-reduce.18.cloned.1.call-start = ((), (), s32[]{:S(2)}) async-start(), calls=%async_computation.10 | async-start | bytes 393216 | tf_op jit(solution)/shard_map/psum | solution.py:65
  429.2 5.3 collective-permute-start
  494.3 79.7 %all-reduce.20.cloned.1.call-start = ((), (), s32[]{:S(2)}) async-start(), calls=%async_computation.11 | async-start | bytes 393216 | tf_op jit(solution)/shard_map/psum | solution.py:65
  544.0 126.4 %all-reduce.22.cloned.1.call-start = ((), (), s32[]{:S(2)}) async-start(), calls=%async_computation.12 | async-start | bytes 393216 | tf_op jit(solution)/shard_map/psum | solution.py:65
  575.1 5.3 collective-permute-start.1
  643.1 92.2 %all-reduce.24.cloned.1.call-start = ((), (), s32[]{:S(2)}) async-start(), calls=%async_computation.13 | async-start | bytes 393216 | tf_op jit(solution)/shard_map/psum | solution.py:69
  705.4 115.3 %reduce-scatter.12.cloned.1.call-start = ((), (), s32[]{:S(2)}) async-start(), calls=%async_computation.14 | async-start | bytes 540672 | tf_op jit(solution)/shard_map/reduce_scatter | solution.py:195
  745.4 75.2 %copy-start.62 = (f32[64,64]{1,0:T(8,128)S(1)}, f32[64,64]{1,0:T(8,128)}, u32[]{:S(2)}) copy-start(f32[64,64]{1,0:T(8,128)} %copy-done.59) | copy-start | bytes 49156
  745.4 155.0 %reduce-scatter.14.cloned.1.call-start = ((), (), s32[]{:S(2)}) async-start(), calls=%async_computation.15 | async-start | bytes 540672 | tf_op jit(solution)/shard_map/reduce_scatter | solution.py:198
  749.0 186.5 %all-reduce.26.cloned.1.call-start = ((), (), s32[]{:S(2)}) async-start(), calls=%async_computation.16 | async-start | bytes 393216 | tf_op jit(solution)/shard_map/psum | solution.py:69
  826.9 108.7 %copy-start.37 = (f32[64,1536]{1,0:T(8,128)S(1)}, f32[64,1536]{1,0:T(8,128)}, u32[]{:S(2)}) copy-start(f32[64,1536]{1,0:T(8,128)} %copy-done.36) | copy-start | bytes 1179652
  904.4 95.7 %all-reduce.28.cloned.1.call-start = ((), (), s32[]{:S(2)}) async-start(), calls=%async_computation.17 | async-start | bytes 393216 | tf_op jit(solution)/shard_map/psum | solution.py:69
  938.7 7.2 collective-permute-start.2
  969.8 116.4 %reduce-scatter.16.cloned.1.call-start = ((), (), s32[]{:S(2)}) async-start(), calls=%async_computation.18 | async-start | bytes 540672 | tf_op jit(solution)/shard_map/reduce_scatter | solution.py:195
  1010.7 155.8 %reduce-scatter.18.cloned.1.call-start = ((), (), s32[]{:S(2)}) async-start(), calls=%async_computation.19 | async-start | bytes 540672 | tf_op jit(solution)/shard_map/reduce_scatter | solution.py:198
  1013.8 72.4 %copy-start.63 = (f32[64,64]{1,0:T(8,128)S(1)}, f32[64,64]{1,0:T(8,128)}, u32[]{:S(2)}) copy-start(f32[64,64]{1,0:T(8,128)} %copy-done.59) | copy-start | bytes 49156
  1016.3 185.0 %all-reduce.30.cloned.1.call-start = ((), (), s32[]{:S(2)}) async-start(), calls=%async_computation.20 | async-start | bytes 393216 | tf_op jit(solution)/shard_map/psum | solution.py:69
  1088.7 112.6 %copy-start.29 = (f32[64,1536]{1,0:T(8,128)S(1)}, f32[64,1536]{1,0:T(8,128)}, u32[]{:S(2)}) copy-start(f32[64,1536]{1,0:T(8,128)} %copy-done.27) | copy-start | bytes 1179652
  1170.4 101.8 %all-reduce.32.cloned.1.call-start = ((), (), s32[]{:S(2)}) async-start(), calls=%async_computation.21 | async-start | bytes 393216 | tf_op jit(solution)/shard_map/psum | solution.py:69
  1203.8 13.9 collective-permute-start.3
  1240.8 116.8 %reduce-scatter.20.cloned.1.call-start = ((), (), s32[]{:S(2)}) async-start(), calls=%async_computation.22 | async-start | bytes 540672 | tf_op jit(solution)/shard_map/reduce_scatter | solution.py:195
  1282.4 155.5 %reduce-scatter.22.cloned.1.call-start = ((), (), s32[]{:S(2)}) async-start(), calls=%async_computation.23 | async-start | bytes 540672 | tf_op jit(solution)/shard_map/reduce_scatter | solution.py:198
  1298.3 184.1 %all-reduce.34.cloned.1.call-start = ((), (), s32[]{:S(2)}) async-start(), calls=%async_computation.30 | async-start | bytes 786432 | tf_op jit(solution)/shard_map/psum | solution.py:65
  1301.6 136.2 %copy-start.110 = (bf16[64,128]{1,0:T(8,128)(2,1)S(1)}, bf16[64,128]{1,0:T(8,128)(2,1)}, u32[]{:S(2)}) copy-start(bf16[64,128]{1,0:T(8,128)(2,1)} %fusion.313) | copy-start | bytes 49156
  1301.6 136.2 %copy-start.112 = (bf16[64,128]{1,0:T(8,128)(2,1)S(1)}, bf16[64,128]{1,0:T(8,128)(2,1)}, u32[]{:S(2)}) copy-start(bf16[64,128]{1,0:T(8,128)(2,1)} %fusion.316) | copy-start | bytes 49156
  1301.6 136.2 %copy-start.116 = (bf16[64,128]{1,0:T(8,128)(2,1)S(1)}, bf16[64,128]{1,0:T(8,128)(2,1)}, u32[]{:S(2)}) copy-start(bf16[64,128]{1,0:T(8,128)(2,1)} %reduce-scatter.14.cloned.1.call-done) | copy-start | bytes 49156
  1301.6 136.2 %copy-start.118 = (bf16[64,128]{1,0:T(8,128)(2,1)S(1)}, bf16[64,128]{1,0:T(8,128)(2,1)}, u32[]{:S(2)}) copy-start(bf16[64,128]{1,0:T(8,128)(2,1)} %reduce-scatter.18.cloned.1.call-done) | copy-start | bytes 49156
  1359.5 81.3 %copy-start.114 = (bf16[64,128]{1,0:T(8,128)(2,1)}, bf16[64,128]{1,0:T(8,128)(2,1)S(1)}, u32[]{:S(2)}) copy-start(bf16[64,128]{1,0:T(8,128)(2,1)S(1)} %fusion.319) | copy-start | bytes 49156
  1447.1 115.1 %reduce-scatter.26.cloned.1.call-start = ((), (), s32[]{:S(2)}) async-start(), calls=%async_computation.29 | async-start | bytes 811008
  1484.9 291.6 %reduce-scatter.24.cloned.1.call-start = ((), (), s32[]{:S(2)}) async-start(), calls=%async_computation.24 | async-start | bytes 48254976 | tf_op jit(solution)/shard_map/reduce_scatter | solution.py:348
  1492.0 66.2 %copy-start.26 = (f32[64,1536]{1,0:T(8,128)S(1)}, f32[64,1536]{1,0:T(8,128)}, u32[]{:S(2)}) copy-start(f32[64,1536]{1,0:T(8,128)} %copy-done.24) | copy-start | bytes 1179652
  1492.0 66.2 %copy-start.30 = (f32[64,1536]{1,0:T(8,128)S(1)}, f32[64,1536]{1,0:T(8,128)}, u32[]{:S(2)}) copy-start(f32[64,1536]{1,0:T(8,128)} %copy-done.27) | copy-start | bytes 1179652
  1492.0 66.2 %copy-start.33 = (f32[64,1536]{1,0:T(8,128)S(1)}, f32[64,1536]{1,0:T(8,128)}, u32[]{:S(2)}) copy-start(f32[64,1536]{1,0:T(8,128)} %copy-done.31) | copy-start | bytes 1179652
  1492.0 66.2 %copy-start.39 = (f32[64,1536]{1,0:T(8,128)S(1)}, f32[64,1536]{1,0:T(8,128)}, u32[]{:S(2)}) copy-start(f32[64,1536]{1,0:T(8,128)} %copy-done.38) | copy-start | bytes 1179652
  1492.1 66.2 %copy-start.58 = (f32[64,1536]{1,0:T(8,128)S(1)}, f32[64,1536]{1,0:T(8,128)}, u32[]{:S(2)}) copy-start(f32[64,1536]{1,0:T(8,128)} %copy-done.57) | copy-start | bytes 1179652
  1492.1 66.2 %copy-start.74 = (bf16[64,1536]{1,0:T(8,128)(2,1)S(1)}, bf16[64,1536]{1,0:T(8,128)(2,1)}, u32[]{:S(2)}) copy-start(bf16[64,1536]{1,0:T(8,128)(2,1)} %all-reduce.30.cloned.1.call-done) | copy-start | bytes 589828
  1492.1 66.2 %copy-start.87 = (bf16[64,1536]{1,0:T(8,128)(2,1)S(1)}, bf16[64,1536]{1,0:T(8,128)(2,1)}, u32[]{:S(2)}) copy-start(bf16[64,1536]{1,0:T(8,128)(2,1)} %all-reduce.20.cloned.1.call-done) | copy-start | bytes 589828
  (145 other events, 1987.6 us)
Sparse Core Ops, SparseCore 0:
  10.3 47.9 all-gather.12
  60.5 44.3 all-gather.14
  192.5 28.0 all-reduce.13
  223.4 98.5 all-gather.16
  324.1 65.0 all-gather.18
  399.1 28.9 all-reduce.15
  494.4 28.0 all-reduce.17
  544.1 29.7 all-reduce.19
  643.2 27.0 all-reduce.21
  705.5 29.7 all-reduce.23
  745.6 75.0 reduce-scatter.11
  824.0 76.3 reduce-scatter.13
  904.5 30.9 all-reduce.25
  969.9 30.1 all-reduce.27
  1010.8 75.3 reduce-scatter.15
  1090.0 76.3 reduce-scatter.17
  1170.5 30.7 all-reduce.29
  1240.9 31.2 all-reduce.31
  1282.5 75.0 reduce-scatter.19
  1361.5 76.3 reduce-scatter.21
  1447.2 35.1 all-reduce.33
  1486.8 75.2 reduce-scatter.25
  1566.8 209.6 reduce-scatter.23
where the time goes:
time: 1790 us
  waiting for transfers between devices  1110 us (62%)
  blocking collectives  310 us (17%)
  matrix products  207 us (12%)
  other arithmetic  86.8 us (5%)
  local copies, waits for them, and re-layouts  50.6 us (3%)
    reduce_scatter x3, waiting for transfers between devices, layer_backward(): lax.psum_scatter(grad_values.astype(jnp.bfloat16), 'ctx', scatter_dimensi...  230 us
    reduce_scatter x1, waiting for transfers between devices, body(): lax.psum_scatter(term_maker(pairs_of(stacked)).astype(jnp.bfloat16), 'ctx...  213 us
    reduce_scatter x3, waiting for transfers between devices, layer_backward(): lax.psum_scatter(grad_keys.astype(jnp.bfloat16), 'ctx', scatter_dimension...  191 us
    psum x6, waiting for transfers between devices, branch_total(): lax.psum(partial_value.astype(jnp.bfloat16), 'shard').astype(jnp.float32)  157 us
    psum x5, waiting for transfers between devices, input_total(): lax.psum(partial_value.astype(jnp.bfloat16), 'shard').astype(jnp.float32)  147 us
    all_gather x1, waiting for transfers between devices, body(): lax.all_gather(pieces[3], 'ctx', axis=0, tiled=True)  100 us
    all_gather x3, blocking collectives, layer_forward(): lax.all_gather(own_keys, 'ctx', axis=0, tiled=True)  77 us
    all_gather x3, blocking collectives, layer_forward(): lax.all_gather(own_values, 'ctx', axis=0, tiled=True)  72.4 us
  transfers between devices with their start and end apart: 27, of which 24 were waited for; matrix products, arithmetic and copies ran while one was open for 8% of the time, Pallas kernels for 0%

commit v1 on v0

v1 whole, which is shorter than its diff:
```python
import jax
import jax.numpy as jnp
from jax import lax
from jax.experimental import pallas as pl
from jax.experimental.pallas import tpu as pltpu
from jax.sharding import PartitionSpec as P

MESH = pl.DeviceIdType.MESH
BF = jnp.bfloat16
F32 = jnp.float32
EPS = 1e-06
THETA = 1000000.0
D = 1536
HD = 128
HEADS = 3
UNITS = 1152
CHUNK = 384
TOK = 64
OWN = 32
QKW = 512
ANY = pl.BlockSpec(memory_space=pl.ANY)
VM = pl.BlockSpec(memory_space=pltpu.VMEM)


class Place:
    def __init__(self):
        self.ctx = lax.axis_index("ctx")
        self.s = lax.axis_index("section")
        self.h = lax.axis_index("shard")
        self.z = self.ctx // 8
        self.x = (self.ctx // 2) % 4
        self.c = self.ctx % 2
        self.y = self.h * 2 + self.s

    def yp(self, k):
        other = (self.y + k) % 4
        return {"section": other % 2, "shard": other // 2}

    def xp(self, k):
        return {"ctx": self.z * 8 + ((self.x + k) % 4) * 2 + self.c}

    def zp(self, k):
        return {"ctx": (self.ctx + 8 * k) % 32}

    def cp(self):
        return {"ctx": self.ctx + 1 - 2 * self.c}


def greet(peers):
    barrier = pltpu.get_barrier_semaphore()
    for peer in peers:
        pl.semaphore_signal(barrier, 1, device_id=peer, device_id_type=MESH)
    pl.semaphore_wait(barrier, len(peers))


class Links:
    def __init__(self, send, recv):
        self.send, self.recv, self.count = send, recv, 0

    def go(self, src, dst, peer):
        index = self.count
        self.count += 1
        copy = pltpu.make_async_remote_copy(
            src, dst, self.send.at[index], self.recv.at[index], device_id=peer, device_id_type=MESH
        )
        copy.start()
        return copy


def landed(copies):
    for copy in copies:
        copy.wait_recv()


def left(copies):
    for copy in copies:
        copy.wait_send()


def dot(a, b, ca=1, cb=0):
    return lax.dot_general(a, b, (((ca,), (cb,)), ((), ())), preferred_element_type=F32)


ORDER = (1, 3, 2)


def unit_rms(u):
    scale = lax.rsqrt(jnp.mean(u * u, axis=1, keepdims=True) + EPS)
    return u * scale, scale


def norm_back(u, gain, dy):
    n, scale = unit_rms(u)
    sd = dy * gain
    return scale * (sd - n * jnp.mean(sd * n, axis=1, keepdims=True)), jnp.sum(dy * n, axis=0, keepdims=True)


def turned(u, cos, sin):
    return u * cos + pltpu.roll(u, 64, 1) * sin


def turned_back(w, cos, sin):
    return w * cos - pltpu.roll(w, 64, 1) * sin


def twice(table):
    return jnp.concatenate([table, table], axis=0)


def key_places(micro_rows):
    j = lax.broadcasted_iota(jnp.int32, (micro_rows, 2048), 1)
    core = j // 1024
    chip = (j % 1024) // TOK
    return chip * (2 * TOK) + core * TOK + j % TOK


def masked(raw, ctx):
    rows = raw.shape[0]
    query = ctx * TOK + lax.broadcasted_iota(jnp.int32, (rows, 2048), 0) % TOK
    return jnp.where(key_places(rows) <= query, raw * (HD**-0.5), -1e30)


def attn_forward_kernel(
    x_ref, gain_ref, w_ref, bias_ref, cos_ref, sin_ref,
    mid_ref, hid_ref, q_ref, kv_ref, att_ref, wf_ref,
    part_ref, got_ref, wsem, send, recv,
):
    me = Place()
    greet([me.yp(1), me.yp(2), me.yp(3), me.xp(1), me.xp(2), me.xp(3), me.zp(1), me.zp(2), me.zp(3), me.cp()])
    net = Links(send, recv)
    weights_over = net.go(w_ref, wf_ref.at[me.c], me.cp())
    weights_here = pltpu.make_async_copy(w_ref, wf_ref.at[me.c], wsem)
    weights_here.start()
    x = x_ref[...]
    normed, _ = unit_rms(x)
    hid_ref[me.y] = (normed * gain_ref[...]).astype(BF)
    hid_copies = [net.go(hid_ref.at[me.y], hid_ref.at[me.y], me.yp(k)) for k in ORDER]
    cos, sin = twice(cos_ref[...]), twice(sin_ref[...])
    weights_here.wait()
    weights_over.wait()
    landed(hid_copies)
    hidden = hid_ref[...].reshape(2 * TOK, D)
    keyval = []
    proj = dot(hidden, wf_ref[0]) + bias_ref[:, :QKW]
    key = turned(proj[:, 384:], cos, sin).astype(BF)
    value = (dot(hidden, wf_ref[1, :, 384:]) + bias_ref[:, QKW:]).astype(BF)
    keyval = jnp.concatenate([key, value], axis=1)
    for m in range(2):
        kv_ref[me.c, m, me.z, me.x] = keyval[m * TOK : (m + 1) * TOK]
    first0 = [net.go(kv_ref.at[me.c, 0, me.z, me.x], kv_ref.at[me.c, 0, me.z, me.x], me.xp(k)) for k in ORDER]
    first1 = [net.go(kv_ref.at[me.c, 1, me.z, me.x], kv_ref.at[me.c, 1, me.z, me.x], me.zp(k)) for k in ORDER]
    for head in range(HEADS):
        query = turned(proj[:, head * HD : (head + 1) * HD], cos, sin).astype(BF)
        for m in range(2):
            q_ref[m, head] = query[m * TOK : (m + 1) * TOK]
    landed(first0)
    second0 = [net.go(kv_ref.at[me.c, 0, me.z], kv_ref.at[me.c, 0, me.z], me.zp(k)) for k in ORDER]
    landed(first1)
    second1 = [net.go(kv_ref.at[me.c, 1, :, me.x], kv_ref.at[me.c, 1, :, me.x], me.xp(k)) for k in ORDER]
    landed(second0)
    third0 = net.go(kv_ref.at[me.c, 0], kv_ref.at[me.c, 0], me.cp())
    landed(second1)
    third1 = net.go(kv_ref.at[me.c, 1], kv_ref.at[me.c, 1], me.cp())
    for m, third in ((0, third0), (1, third1)):
        third.wait_recv()
        queries = q_ref[m].reshape(HEADS * TOK, HD)
        keys = kv_ref[:, m, :, :, :, :HD].reshape(2048, HD)
        values = kv_ref[:, m, :, :, :, HD:].reshape(2048, HD)
        scores = masked(dot(queries, keys, 1, 1), me.ctx)
        weight = jnp.exp(scores - jnp.max(scores, axis=1, keepdims=True))
        total = jnp.sum(weight, axis=1, keepdims=True)
        out = (dot(weight.astype(BF), values) / total).astype(BF)
        for head in range(HEADS):
            att_ref[m * TOK : (m + 1) * TOK, head * HD : (head + 1) * HD] = out[head * TOK : (head + 1) * TOK]
    part_ref[...] = dot(att_ref[...], wf_ref[1, :, :384], 1, 1).astype(BF).reshape(4, OWN, D)
    back = [net.go(part_ref.at[(me.y + k) % 4], got_ref.at[k - 1], me.yp(k)) for k in ORDER]
    total = x + part_ref[me.y].astype(F32)
    landed(back)
    for k in range(3):
        total = total + got_ref[k].astype(F32)
    mid_ref[...] = total
    left(hid_copies + first0 + first1 + second0 + second1 + [third0, third1] + back)


def attn_forward(x, gain, w_half, bias, cos, sin):
    return pl.pallas_call(
        attn_forward_kernel,
        out_shape=(
            jax.ShapeDtypeStruct((OWN, D), F32),
            jax.ShapeDtypeStruct((4, OWN, D), BF),
            jax.ShapeDtypeStruct((2, HEADS, TOK, HD), BF),
            jax.ShapeDtypeStruct((2, 2, 4, 4, TOK, 2 * HD), BF),
            jax.ShapeDtypeStruct((2 * TOK, HEADS * HD), BF),
            jax.ShapeDtypeStruct((2, D, QKW), BF),
        ),
        in_specs=[VM, VM, ANY, VM, VM, VM],
        out_specs=(VM,) * 6,
        scratch_shapes=[
            pltpu.VMEM((4, OWN, D), BF),
            pltpu.VMEM((3, OWN, D), BF),
            pltpu.SemaphoreType.DMA,
            pltpu.SemaphoreType.DMA((21,)),
            pltpu.SemaphoreType.DMA((21,)),
        ],
        compiler_params=pltpu.CompilerParams(collective_id=0, has_side_effects=True, vmem_limit_bytes=48 << 20),
        name="attn_forward",
    )(x, gain, w_half, bias, cos, sin)


def fetch_mlp(w_ref, w_vmem, sems):
    copies = []
    for part in range(3):
        copy = pltpu.make_async_copy(w_ref.at[:, part * UNITS : (part + 1) * UNITS], w_vmem.at[part], sems.at[part])
        copy.start()
        copies.append(copy)
    return copies


def gather_yc(net, me, buf):
    sent = [net.go(buf.at[me.c, me.y], buf.at[me.c, me.y], me.yp(k)) for k in ORDER]
    crossed = [net.go(buf.at[me.c, me.y], buf.at[me.c, me.y], me.cp())]
    for k, copy in zip(ORDER, sent):
        copy.wait_recv()
        slot = (me.y + 4 - k) % 4
        crossed.append(net.go(buf.at[me.c, slot], buf.at[me.c, slot], me.cp()))
    landed(crossed)
    return sent + crossed


def scatter_yc_start(net, me, part, mate):
    return net.go(part.at[1 - me.c], mate, me.cp())


def scatter_yc_middle(net, me, part, mate, got, swap):
    swap.wait_recv()
    mate[...] = (part[me.c].astype(F32) + mate[...].astype(F32)).astype(BF)
    return [net.go(mate.at[(me.y + k) % 4], got.at[k - 1], me.yp(k)) for k in ORDER]


def scatter_yc_end(me, mate, got, back):
    total = mate[me.y].astype(F32)
    landed(back)
    for k in range(3):
        total = total + got[k].astype(F32)
    return total


def mlp_forward_kernel(
    mid_ref, gain_ref, w_ref,
    out_ref, hid_ref, gate_ref, up_ref, prod_ref,
    w_vmem, acc, part, mate, got, wsem, send, recv,
):
    me = Place()
    weights = fetch_mlp(w_ref, w_vmem, wsem)
    greet([me.yp(1), me.yp(2), me.yp(3), me.cp()])
    net = Links(send, recv)
    normed, _ = unit_rms(mid_ref[...])
    hid_ref[me.c, me.y] = (normed * gain_ref[...]).astype(BF)
    gathered = gather_yc(net, me, hid_ref)
    for copy in weights:
        copy.wait()
    hidden = hid_ref[...].reshape(256, D)
    acc[...] = jnp.zeros_like(acc)

    def step(i, _):
        cols = pl.ds(pl.multiple_of(i * CHUNK, CHUNK), CHUNK)
        gate = dot(hid_ref[...].reshape(256, D), w_vmem[0, :, cols])
        up = dot(hid_ref[...].reshape(256, D), w_vmem[1, :, cols])
        product = (gate * jax.nn.sigmoid(gate) * up).astype(BF)
        gate_ref[:, cols] = gate
        up_ref[:, cols] = up
        prod_ref[:, cols] = product
        acc[...] += dot(product, w_vmem[2, :, cols], 1, 1)
        return 0

    lax.fori_loop(0, UNITS // CHUNK, step, 0)
    part[...] = acc[...].astype(BF).reshape(2, 4, OWN, D)
    swap = scatter_yc_start(net, me, part, mate)
    back = scatter_yc_middle(net, me, part, mate, got, swap)
    out_ref[...] = mid_ref[...] + scatter_yc_end(me, mate, got, back)
    left(gathered + [swap] + back)


def mlp_forward(mid, gain, w):
    return pl.pallas_call(
        mlp_forward_kernel,
        out_shape=(
            jax.ShapeDtypeStruct((OWN, D), F32),
            jax.ShapeDtypeStruct((2, 4, OWN, D), BF),
            jax.ShapeDtypeStruct((256, UNITS), F32),
            jax.ShapeDtypeStruct((256, UNITS), F32),
            jax.ShapeDtypeStruct((256, UNITS), BF),
        ),
        in_specs=[VM, VM, ANY],
        out_specs=(VM,) * 5,
        scratch_shapes=[
            pltpu.VMEM((3, D, UNITS), BF),
            pltpu.VMEM((256, D), F32),
            pltpu.VMEM((2, 4, OWN, D), BF),
            pltpu.VMEM((4, OWN, D), BF),
            pltpu.VMEM((3, OWN, D), BF),
            pltpu.SemaphoreType.DMA((3,)),
            pltpu.SemaphoreType.DMA((11,)),
            pltpu.SemaphoreType.DMA((11,)),
        ],
        compiler_params=pltpu.CompilerParams(collective_id=1, has_side_effects=True, vmem_limit_bytes=48 << 20),
        name="mlp_forward",
    )(mid, gain, w)


def mlp_backward_kernel(
    g_ref, mid_ref, gain_ref, w_ref, hid_ref, gate_ref, up_ref, prod_ref,
    gmid_ref, ggain_ref, dw_ref,
    w_vmem, low, dgate, dup, acc, part, mate, got, wsem, send, recv,
):
    me = Place()
    weights = fetch_mlp(w_ref, w_vmem, wsem)
    greet([me.yp(1), me.yp(2), me.yp(3), me.cp()])
    net = Links(send, recv)
    low[me.c, me.y] = g_ref[...].astype(BF)
    gathered = gather_yc(net, me, low)
    for copy in weights:
        copy.wait()
    acc[...] = jnp.zeros_like(acc)

    def step(i, _):
        cols = pl.ds(pl.multiple_of(i * CHUNK, CHUNK), CHUNK)
        dprod = dot(low[...].reshape(256, D), w_vmem[2, :, cols])
        gate, up = gate_ref[:, cols], up_ref[:, cols]
        sigma = jax.nn.sigmoid(gate)
        dg = (dprod * up * sigma * (1.0 + gate * (1.0 - sigma))).astype(BF)
        du = (dprod * gate * sigma).astype(BF)
        dgate[:, cols] = dg
        dup[:, cols] = du
        acc[...] += dot(dg, w_vmem[0, :, cols], 1, 1) + dot(du, w_vmem[1, :, cols], 1, 1)
        return 0

    lax.fori_loop(0, UNITS // CHUNK, step, 0)
    part[...] = acc[...].astype(BF).reshape(2, 4, OWN, D)
    swap = scatter_yc_start(net, me, part, mate)

    def weight_grads(index, left_ref, right_ref):
        def step_w(i, _):
            cols = pl.ds(pl.multiple_of(i * CHUNK, CHUNK), CHUNK)
            where = pl.ds(pl.multiple_of(index * UNITS + i * CHUNK, CHUNK), CHUNK)
            dw_ref[:, where] = dot(left_ref[...].reshape(256, D), right_ref[:, cols], 0, 0).astype(BF)
            return 0

        lax.fori_loop(0, UNITS // CHUNK, step_w, 0)

    back = scatter_yc_middle(net, me, part, mate, got, swap)
    weight_grads(0, hid_ref, dgate)
    weight_grads(1, hid_ref, dup)
    weight_grads(2, low, prod_ref)
    dy = scatter_yc_end(me, mate, got, back)
    du, ggain_ref[...] = norm_back(mid_ref[...], gain_ref[...], dy)
    gmid_ref[...] = g_ref[...] + du
    left(gathered + [swap] + back)


def mlp_backward(g, mid, gain, w, hid, gate, up, prod):
    return pl.pallas_call(
        mlp_backward_kernel,
        out_shape=(
            jax.ShapeDtypeStruct((OWN, D), F32),
            jax.ShapeDtypeStruct((1, D), F32),
            jax.ShapeDtypeStruct((D, 3 * UNITS), BF),
        ),
        in_specs=[VM, VM, VM, ANY, VM, VM, VM, VM],
        out_specs=(VM,) * 3,
        scratch_shapes=[
            pltpu.VMEM((3, D, UNITS), BF),
            pltpu.VMEM((2, 4, OWN, D), BF),
            pltpu.VMEM((256, UNITS), BF),
            pltpu.VMEM((256, UNITS), BF),
            pltpu.VMEM((256, D), F32),
            pltpu.VMEM((2, 4, OWN, D), BF),
            pltpu.VMEM((4, OWN, D), BF),
            pltpu.VMEM((3, OWN, D), BF),
            pltpu.SemaphoreType.DMA((3,)),
            pltpu.SemaphoreType.DMA((11,)),
            pltpu.SemaphoreType.DMA((11,)),
        ],
        compiler_params=pltpu.CompilerParams(collective_id=2, has_side_effects=True, vmem_limit_bytes=56 << 20),
        name="mlp_backward",
    )(g, mid, gain, w, hid, gate, up, prod)


def attn_backward_kernel(
    gm_ref, x_ref, gain_ref, w_ref, hid_ref, q_ref, kv_ref, att_ref, cos_ref, sin_ref,
    gin_ref, ggain_ref, gbias_ref, dw_ref,
    low, dkv, kmate, kz, kx, k2, k3, kpair, kpair_got, dqs, dws, dw_got, part, got, send, recv,
):
    me = Place()
    greet([me.yp(1), me.yp(2), me.yp(3), me.xp(1), me.xp(2), me.xp(3), me.zp(1), me.zp(2), me.zp(3), me.cp()])
    net = Links(send, recv)
    low[me.y] = gm_ref[...].astype(BF)
    gathered = [net.go(low.at[me.y], low.at[me.y], me.yp(k)) for k in ORDER]
    cos, sin = twice(cos_ref[...]), twice(sin_ref[...])
    landed(gathered)
    grad_mid = low[...].reshape(2 * TOK, D)
    grad_att = dot(grad_mid, w_ref[1, :, :384]).astype(BF)
    for m in range(2):
        rows = slice(m * TOK, (m + 1) * TOK)
        queries = q_ref[m].reshape(HEADS * TOK, HD)
        keys = kv_ref[:, m, :, :, :, :HD].reshape(2048, HD)
        values = kv_ref[:, m, :, :, :, HD:].reshape(2048, HD)
        grad_out = jnp.concatenate([grad_att[rows, h * HD : (h + 1) * HD] for h in range(HEADS)], axis=0)
        scores = masked(dot(queries, keys, 1, 1), me.ctx)
        weight = jnp.exp(scores - jnp.max(scores, axis=1, keepdims=True))
        soft = weight / jnp.sum(weight, axis=1, keepdims=True)
        grad_soft = dot(grad_out, values, 1, 1)
        delta = jnp.sum(soft * grad_soft, axis=1, keepdims=True)
        grad_scores = (soft * (grad_soft - delta)).astype(BF)
        grad_values = dot(soft.astype(BF), grad_out, 0, 0)
        grad_keys = dot(grad_scores, queries, 0, 0) * (HD**-0.5)
        dkv[:, m] = jnp.concatenate([grad_keys, grad_values], axis=1).astype(BF).reshape(2, 4, 4, TOK, 2 * HD)
        dq = dot(grad_scores, keys) * (HD**-0.5)
        for h in range(HEADS):
            dqs[rows, h * HD : (h + 1) * HD] = dq[h * TOK : (h + 1) * TOK]
    swap = net.go(dkv.at[1 - me.c], kmate, me.cp())
    dq_low = jnp.concatenate(
        [turned_back(dqs[:, h * HD : (h + 1) * HD], cos, sin).astype(BF) for h in range(HEADS)], axis=1
    )
    hidden = hid_ref[...].reshape(2 * TOK, D)
    swap.wait_recv()
    kmate[...] = (kmate[...].astype(F32) + dkv[me.c].astype(F32)).astype(BF)
    first0 = [net.go(kmate.at[0, (me.z + k) % 4], kz.at[k - 1], me.zp(k)) for k in ORDER]
    first1 = [net.go(kmate.at[1, :, (me.x + k) % 4], kx.at[k - 1], me.xp(k)) for k in ORDER]
    dws[0, :, :384] = dot(hidden, dq_low, 0, 0).astype(BF)
    dws[1, :, :384] = dot(grad_mid, att_ref[...], 0, 0).astype(BF)
    dws[1, :, 384:] = jnp.zeros((D, HD), BF)
    landed(first0)
    total0 = kmate[0, me.z].astype(F32)
    for k in range(3):
        total0 = total0 + kz[k].astype(F32)
    k2[0] = total0.astype(BF)
    second0 = [net.go(k2.at[0, (me.x + k) % 4], k3.at[0, k - 1], me.xp(k)) for k in ORDER]
    landed(first1)
    total1 = kmate[1, :, me.x].astype(F32)
    for k in range(3):
        total1 = total1 + kx[k].astype(F32)
    k2[1] = total1.astype(BF)
    second1 = [net.go(k2.at[1, (me.z + k) % 4], k3.at[1, k - 1], me.zp(k)) for k in ORDER]
    landed(second0 + second1)
    for m, place in ((0, me.x), (1, me.z)):
        total = k2[m, place].astype(F32)
        for k in range(3):
            total = total + k3[m, k].astype(F32)
        kpair[0, m * TOK : (m + 1) * TOK] = total[:, :HD].astype(BF)
        kpair[1, m * TOK : (m + 1) * TOK] = total[:, HD:].astype(BF)
    pair = net.go(kpair.at[1 - me.s], kpair_got, {"section": 1 - me.s})
    pair.wait_recv()
    total = kpair[me.s].astype(F32) + kpair_got[...].astype(F32)
    dk_low = jnp.where(me.s == 0, turned_back(total, cos, sin), total).astype(BF)
    part[...] = (
        (dot(dq_low, w_ref[0, :, :384], 1, 1) + dot(dk_low, w_ref[me.s, :, 384:], 1, 1)).astype(BF).reshape(4, OWN, D)
    )
    back = [net.go(part.at[(me.y + k) % 4], got.at[k - 1], me.yp(k)) for k in ORDER]
    dws[0, :, 384:] = dot(hidden, dk_low, 0, 0).astype(BF)
    dw_swap = net.go(dws.at[1 - me.c], dw_got, me.cp())
    gbias_ref[:, :384] = jnp.sum(dq_low.astype(F32), axis=0, keepdims=True)
    gbias_ref[:, 384:] = jnp.sum(dk_low.astype(F32), axis=0, keepdims=True)
    dy = part[me.y].astype(F32)
    landed(back)
    for k in range(3):
        dy = dy + got[k].astype(F32)
    dx, ggain_ref[...] = norm_back(x_ref[...], gain_ref[...], dy)
    gin_ref[...] = gm_ref[...] + dx
    dw_swap.wait_recv()
    dw_ref[...] = (dws[me.c].astype(F32) + dw_got[...].astype(F32)).astype(BF)
    left(gathered + [swap] + first0 + first1 + second0 + second1 + [pair] + back + [dw_swap])


def attn_backward(gm, x, gain, w, hid, q, kv, att, cos, sin):
    return pl.pallas_call(
        attn_backward_kernel,
        out_shape=(
            jax.ShapeDtypeStruct((OWN, D), F32),
            jax.ShapeDtypeStruct((1, D), F32),
            jax.ShapeDtypeStruct((1, QKW), F32),
            jax.ShapeDtypeStruct((D, QKW), BF),
        ),
        in_specs=[VM] * 10,
        out_specs=(VM,) * 4,
        scratch_shapes=[
            pltpu.VMEM((4, OWN, D), BF),
            pltpu.VMEM((2, 2, 4, 4, TOK, 2 * HD), BF),
            pltpu.VMEM((2, 4, 4, TOK, 2 * HD), BF),
            pltpu.VMEM((3, 4, TOK, 2 * HD), BF),
            pltpu.VMEM((3, 4, TOK, 2 * HD), BF),
            pltpu.VMEM((2, 4, TOK, 2 * HD), BF),
            pltpu.VMEM((2, 3, TOK, 2 * HD), BF),
            pltpu.VMEM((2, 2 * TOK, HD), BF),
            pltpu.VMEM((2 * TOK, HD), BF),
            pltpu.VMEM((2 * TOK, HEADS * HD), F32),
            pltpu.VMEM((2, D, QKW), BF),
            pltpu.VMEM((D, QKW), BF),
            pltpu.VMEM((4, OWN, D), BF),
            pltpu.VMEM((3, OWN, D), BF),
            pltpu.SemaphoreType.DMA((21,)),
            pltpu.SemaphoreType.DMA((21,)),
        ],
        compiler_params=pltpu.CompilerParams(collective_id=3, has_side_effects=True, vmem_limit_bytes=48 << 20),
        name="attn_backward",
    )(gm, x, gain, w, hid, q, kv, att, cos, sin)


def quad(me):
    return (
        (me.c, 1 - me.s, {"section": 1 - me.s}),
        (1 - me.c, me.s, me.cp()),
        (1 - me.c, 1 - me.s, {"section": 1 - me.s, "ctx": me.ctx + 1 - 2 * me.c}),
    )


def spread_kernel(attn_ref, mlp_ref, attn_out, mlp_out, lsem, send, recv):
    me = Place()
    peers = quad(me)
    greet([peer for _, _, peer in peers])
    net = Links(send, recv)
    copies = []
    for src, dst in ((attn_ref, attn_out), (mlp_ref, mlp_out)):
        for core, section, peer in peers:
            copies.append(net.go(src.at[section, core], dst.at[me.s, me.c], peer))
    here = []
    for i, (src, dst) in enumerate(((attn_ref, attn_out), (mlp_ref, mlp_out))):
        copy = pltpu.make_async_copy(src.at[me.s, me.c], dst.at[me.s, me.c], lsem.at[i])
        copy.start()
        here.append(copy)
    for copy in here + copies:
        copy.wait()


def spread(attn, mlp):
    return pl.pallas_call(
        spread_kernel,
        out_shape=(jax.ShapeDtypeStruct(attn.shape, BF), jax.ShapeDtypeStruct(mlp.shape, BF)),
        in_specs=[ANY, ANY],
        out_specs=(ANY, ANY),
        scratch_shapes=[
            pltpu.SemaphoreType.DMA((2,)),
            pltpu.SemaphoreType.DMA((6,)),
            pltpu.SemaphoreType.DMA((6,)),
        ],
        compiler_params=pltpu.CompilerParams(collective_id=4, has_side_effects=True),
        name="spread",
    )(attn, mlp)


def gather_back_kernel(attn_ref, mlp_ref, ends_ref, attn_out, mlp_out, ends_out, lsem, send, recv):
    me = Place()
    peers = quad(me)
    far = {"section": me.s, "shard": 1 - me.h}
    cross = {"section": 1 - me.s, "shard": 1 - me.h}
    greet([peer for _, _, peer in peers] + [far, cross])
    net = Links(send, recv)
    copies = []
    for src, dst in ((attn_ref, attn_out), (mlp_ref, mlp_out)):
        for core, section, peer in peers:
            copies.append(net.go(src.at[section, core], dst.at[me.s, me.c], peer))
    for k in ORDER:
        copies.append(net.go(ends_ref.at[((me.y + k) % 4) % 2], ends_out.at[me.y], me.yp(k)))
    here = []
    pairs = (
        (attn_ref.at[me.s, me.c], attn_out.at[me.s, me.c]),
        (mlp_ref.at[me.s, me.c], mlp_out.at[me.s, me.c]),
        (ends_ref.at[me.s], ends_out.at[me.y]),
    )
    for i, (src, dst) in enumerate(pairs):
        copy = pltpu.make_async_copy(src, dst, lsem.at[i])
        copy.start()
        here.append(copy)
    for copy in here + copies:
        copy.wait()


def gather_back(attn, mlp, ends):
    return pl.pallas_call(
        gather_back_kernel,
        out_shape=(
            jax.ShapeDtypeStruct(attn.shape, BF),
            jax.ShapeDtypeStruct(mlp.shape, BF),
            jax.ShapeDtypeStruct((4, OWN, D), F32),
        ),
        in_specs=[ANY] * 3,
        out_specs=(ANY,) * 3,
        scratch_shapes=[
            pltpu.SemaphoreType.DMA((3,)),
            pltpu.SemaphoreType.DMA((9,)),
            pltpu.SemaphoreType.DMA((9,)),
        ],
        compiler_params=pltpu.CompilerParams(collective_id=5, has_side_effects=True),
        name="gather_back",
    )(attn, mlp, ends)


SAME_CORE = [[core + 2 * chip for chip in range(16)] for core in range(2)]


def all_rows(block):
    return lax.all_gather(block, "ctx", axis=0, tiled=True, axis_index_groups=SAME_CORE)


def own_rows(block):
    return lax.psum_scatter(block, "ctx", scatter_dimension=0, tiled=True, axis_index_groups=SAME_CORE)


def unit_slices(w):
    padded = jnp.pad(w, ((0, 0), (0, 4 * UNITS - w.shape[1])))
    return padded.reshape(w.shape[0], 2, 2, UNITS).transpose(1, 2, 0, 3)


def body(ends, w_query, w_kv, w_out, w_gate_up, w_down, gains, bias_query, bias_kv):
    me = Place()
    rows = w_query.shape[1]
    mine = lax.dynamic_slice(ends[0], (me.h, me.s * OWN, 0), (1, OWN, D))[0]
    other = lax.dynamic_slice(ends[0], (me.h, (1 - me.s) * OWN, 0), (1, OWN, D))[0]
    crossed = lax.ppermute(other, "section", [(0, 1), (1, 0)])
    x = jnp.where(me.s == 0, mine, crossed)
    cotangent = jnp.where(me.s == 0, crossed, mine)

    wq = w_query[0].reshape(rows, 2, 384)
    wo = w_out[0].reshape(rows, 2, 384)
    attn_pieces = jnp.stack(
        [
            jnp.stack(
                [
                    jnp.concatenate([wq[:, s], w_kv[0, :, 0]], axis=1),
                    jnp.concatenate([wo[:, s], w_kv[0, :, 1]], axis=1),
                ]
            )
            for s in range(2)
        ]
    )
    mlp_pieces = jnp.concatenate(
        [unit_slices(w_gate_up[0, :, 0]), unit_slices(w_gate_up[0, :, 1]), unit_slices(w_down[0])], axis=3
    )
    attn_rows, mlp_rows = spread(attn_pieces, mlp_pieces)
    attn_w = [None, None]
    mlp_w = [None, None]
    for l in range(2):
        attn_w[l] = all_rows(attn_rows[l].reshape(2 * rows, QKW))
        mlp_w[l] = all_rows(mlp_rows[l].reshape(2 * rows, 3 * UNITS))

    packed = jnp.concatenate([gains[0].reshape(-1), bias_query[0].reshape(-1), bias_kv[0].reshape(-1)])[None]
    everything = lax.all_gather(packed, ("section", "ctx", "shard"), axis=0, tiled=True).astype(F32)
    everything = everything.reshape(2, 32, 2, 128)
    gain_all = everything[:, :, 0, :96].reshape(2, 32, 2, 48).transpose(0, 2, 1, 3).reshape(2, 2, 1, D)
    bias_all = everything[:, :, :, 96:].reshape(2, 32, 2, 8, 4).transpose(2, 0, 3, 1, 4).reshape(2, 2, 8, 128)
    bias_here = lax.dynamic_index_in_dim(bias_all, me.h, 0, keepdims=False)
    bias_q = lax.dynamic_slice(bias_here, (0, me.s * HEADS, 0), (2, HEADS, 128)).reshape(2, 1, 384)
    bias = jnp.concatenate([bias_q, bias_here[:, 6:8].reshape(2, 1, 256)], axis=2)

    positions = (me.ctx * TOK + jnp.arange(TOK, dtype=jnp.int32)).astype(F32)
    inverse = 1.0 / THETA ** (jnp.arange(0, HD, 2, dtype=F32) / HD)
    angles = positions[:, None] * inverse[None, :]
    cos = jnp.concatenate([jnp.cos(angles), jnp.cos(angles)], axis=1)
    sin = jnp.concatenate([-jnp.sin(angles), jnp.sin(angles)], axis=1)

    inputs, kept = [], []
    for l in range(2):
        inputs.append(x)
        mid, hid, q, kv, att, wf = attn_forward(x, gain_all[l, 0], attn_w[l], bias[l], cos, sin)
        out, hid2, gate, up, prod = mlp_forward(mid, gain_all[l, 1], mlp_w[l])
        kept.append((mid, hid, q, kv, att, wf, hid2, gate, up, prod))
        x = out.astype(BF).astype(F32)

    g = cotangent
    attn_g, mlp_g, gain_g, bias_g = [None, None], [None, None], [None, None], [None, None]
    for l in (1, 0):
        mid, hid, q, kv, att, wf, hid2, gate, up, prod = kept[l]
        gmid, ggain1, dw_mlp = mlp_backward(g, mid, gain_all[l, 1], mlp_w[l], hid2, gate, up, prod)
        mlp_g[l] = own_rows(dw_mlp)
        gin, ggain0, gbias, dw_attn = attn_backward(gmid, inputs[l], gain_all[l, 0], wf, hid, q, kv, att, cos, sin)
        attn_g[l] = own_rows(dw_attn)
        gain_g[l] = jnp.concatenate([ggain0, ggain1], axis=0)
        bias_g[l] = gbias
        g = gin.astype(BF).astype(F32) if l == 1 else gin

    small = jnp.stack(bias_g)
    small = jnp.where(jnp.arange(4)[None, :, None] == me.y, small, 0.0)
    small = jnp.concatenate([jnp.stack(gain_g).reshape(-1), small.reshape(-1)]).reshape(-1, 128)
    small = lax.psum(small, ("section", "ctx", "shard")).reshape(-1)
    gain_sum = small[: 4 * D].reshape(2, 2, 32, 48)
    bias_sum = small[4 * D :].reshape(2, 2, 2, 4, 32, 4)
    gain_sum = lax.dynamic_index_in_dim(gain_sum, me.s, 0, keepdims=False)
    gain_sum = lax.dynamic_index_in_dim(gain_sum, me.ctx, 1, keepdims=False)
    bias_sum = lax.dynamic_index_in_dim(bias_sum, me.s, 0, keepdims=False)
    bias_sum = lax.dynamic_index_in_dim(bias_sum, me.h, 0, keepdims=False)
    bias_sum = lax.dynamic_index_in_dim(bias_sum, me.ctx, 2, keepdims=False)

    attn_home, mlp_home, boundary = gather_back(
        jnp.stack(attn_g).reshape(2, 2, rows, QKW),
        jnp.stack(mlp_g).reshape(2, 2, rows, 3 * UNITS),
        jnp.stack([g, out]),
    )
    attn_home = attn_home.astype(F32)
    mlp_home = mlp_home.astype(F32).reshape(2, 2, rows, 3, UNITS).transpose(2, 3, 0, 1, 4).reshape(rows, 3, 4 * UNITS)
    mlp_home = mlp_home[:, :, : w_down.shape[2]]
    return (
        boundary.reshape(1, 2, TOK, D),
        attn_home[:, 0, :, :384].transpose(1, 0, 2).reshape(1, rows, 768),
        attn_home[:, 0, :, 384:].transpose(1, 0, 2)[None],
        attn_home[:, 1, :, :384].transpose(1, 0, 2).reshape(1, rows, 768),
        mlp_home[:, :2][None],
        mlp_home[:, 2][None],
        gain_sum[None],
        bias_sum[:, :HEADS].reshape(1, 6, 4),
        bias_sum[:, HEADS].reshape(1, 2, 1, 4),
    )


def solution(mesh):
    placed = (
        P("section", None, "ctx", None),
        P("section", "ctx", "shard"),
        P("section", "ctx", None, "shard"),
        P("section", "ctx", "shard"),
        P("section", "ctx", None, "shard"),
        P("section", "ctx", "shard"),
        P("section", None, "ctx"),
        P("section", "shard", "ctx"),
        P("section", None, "shard", "ctx"),
    )
    return jax.shard_map(
        body,
        mesh=mesh,
        in_specs=placed,
        out_specs=(
            P("section", None, "ctx", None),
            P("section", "ctx", "shard"),
            P("section", "ctx", None, "shard"),
            P("section", "ctx", "shard"),
            P("section", "ctx", None, "shard"),
            P("section", "ctx", "shard"),
            P("section", None, "ctx"),
            P("section", "shard", "ctx"),
            P("section", None, "shard", "ctx"),
        ),
        check_vma=False,
    )
```

time: 1790 us -> 1020 us (0.57)
  waiting for transfers between devices: 1110 us -> 265 us
  Pallas kernels: 0 us -> 294 us
  matrix products: 207 us -> 0 us
  other arithmetic: 86.8 us -> 9.7 us
  blocking collectives: 310 us -> 377 us
    reduce_scatter x7 -> x4, waiting for transfers between devices: 633 us -> 262 us  [own_rows(): lax.psum_scatter(block, 'ctx', scatter_dimension=0, tiled=True, axis_inde...]
    psum x11 -> x0, waiting for transfers between devices: 304 us -> none  [the longest x6 157 us: branch_total(): lax.psum(partial_value.astype(jnp.bfloat16), 'shard').astype(jnp.float32)]
    pallas_call x0 -> x10, Pallas kernels: none -> 294 us  [the longest x2 77.7 us: attn_backward(): pl.pallas_call(attn_backward_kernel, out_shape=(jax.ShapeDtypeStruct((OWN...]
    dot_general x53 -> x0, matrix products: 207 us -> none  [the longest x3 43.5 us: layer_backward(): jnp.einsum('tcf,dcf->td', grad_gate_up, w_gate_up, preferred_element_type...]
    all_gather x4, waiting for transfers between devices: 156 us -> 0.03 us  [all_rows(): lax.all_gather(block, 'ctx', axis=0, tiled=True, axis_index_groups=SAME_C...]
    all_gather x10 -> x1, blocking collectives: 247 us -> 313 us  [body(): lax.all_gather(packed, ('section', 'ctx', 'shard'), axis=0, tiled=True)]
    psum x0 -> x1, blocking collectives: none -> 64 us  [body(): small = lax.psum(small, ('section', 'ctx', 'shard')).reshape(-1)]
    unnamed x1 -> x0, blocking collectives: 62.9 us -> none
  transfers between devices with their start and end apart: 27 -> 9, of which waited for: 24 -> 4; matrix products, arithmetic and copies ran while one was open for 8% -> 1% of each run, Pallas kernels for 0% -> 9%
where the time goes in v1:
time: 1020 us
  blocking collectives  377 us (37%)
  Pallas kernels  294 us (29%)
  waiting for transfers between devices  265 us (26%)
  local copies, waits for them, and re-layouts  54.7 us (5%)
  between operations  15.1 us (1%)
    all_gather x1, blocking collectives, body(): lax.all_gather(packed, ('section', 'ctx', 'shard'), axis=0, tiled=True)  313 us
    reduce_scatter x4, waiting for transfers between devices, own_rows(): lax.psum_scatter(block, 'ctx', scatter_dimension=0, tiled=True, axis_inde...  262 us
    pallas_call x2, Pallas kernels, attn_backward(): pl.pallas_call(attn_backward_kernel, out_shape=(jax.ShapeDtypeStruct((OWN...  77.7 us
    pallas_call x2, Pallas kernels, attn_forward(): pl.pallas_call(attn_forward_kernel, out_shape=(jax.ShapeDtypeStruct((OWN,...  68.7 us
    psum x1, blocking collectives, body(): small = lax.psum(small, ('section', 'ctx', 'shard')).reshape(-1)  64 us
    pallas_call x2, Pallas kernels, mlp_backward(): pl.pallas_call(mlp_backward_kernel, out_shape=(jax.ShapeDtypeStruct((OWN,...  55.5 us
    pallas_call x2, Pallas kernels, mlp_forward(): pl.pallas_call(mlp_forward_kernel, out_shape=(jax.ShapeDtypeStruct((OWN,...  41.1 us
    pallas_call x1, Pallas kernels, gather_back(): pl.pallas_call(gather_back_kernel, out_shape=(jax.ShapeDtypeStruct(attn.s...  30.9 us
  transfers between devices with their start and end apart: 9, of which 4 were waited for; matrix products, arithmetic and copies ran while one was open for 1% of the time, Pallas kernels for 9%

profile of v1, /device:TPU:1, one launch (start us, length us, event | category | flops | bytes accessed | tf_op | source)
XLA Modules:
  0.0 1017.7 jit_solution(8838107308508815210)
XLA Ops:
  7.2 0.9 fusion.10
  8.1 0.9 reshape_squeeze.37
  9.0 1.0 reshape_squeeze.38
  10.2 1.0 pad.12
  11.4 1.2 fusion.6
  14.0 1.2 pad_maximum_fusion.mlp_ref
  15.2 20.5 %spread.1 = (bf16[2,2,48,512]{3,2,1,0:T(8,128)(2,1)}, bf16[2,2,48,3456]{3,2,1,0:T(8,128)(2,1)}) custom-call(bf16[2,2,48,512]{3,2,1,0:T(8,128)(2,1)} %pad_maximum_fusion.3.attn_ref, bf16[2,2,48,3456]{3,2,1,0:T(8,128)(2,1)} %pad_maximum_fusion.mlp_ref), custom_call_target="tpu_custom_call" | custom-call | tf_op jit(solution)/shard_map/spread/pallas_call | solution.py:536
  35.7 1.6 fusion.7
  37.5 2.5 fusion.5
  41.4 1.5 collective-permute-start
  43.3 312.6 %all-gather.1 = bf16[128,1,128]{2,1,0:T(2,128)(2,1)S(1)} all-gather(bf16[1,1,128]{2,1,0:T(2,128)(2,1)S(1)} %maximum_bitcast_fusion.6), channel_id=2, replica_groups=mesh['section'=2,'ctx'=32,'shard'=2] {'section','ctx','shard'}, dimensions={0}, use_global_device_ids=true | all-gather | bytes 33024 | tf_op jit(solution)/shard_map/all_gather | solution.py:647
  359.2 1.4 copy-done.3
  360.7 34.5 %attn_forward.2 = (f32[32,1536]{1,0:T(8,128)S(1)}, bf16[4,32,1536]{2,1,0:T(8,128)(2,1)S(1)}, bf16[2,3,64,128]{3,2,1,0:T(8,128)(2,1)S(1)}, bf16[2,2,4,4,64,256]{5...) custom-call(f32[32,1536]{1,0:T(8,128)S(1)} %get-tuple-element.138.x_ref, ...), custom_call_target="tpu_custom_call" | custom-call | tf_op jit(solution)/shard_map/attn_forward/pallas_call | solution.py:186
  396.4 19.6 %mlp_forward.2 = (f32[32,1536]{1,0:T(8,128)S(1)}, bf16[2,4,32,1536]{3,2,1,0:T(8,128)(2,1)S(1)}, f32[256,1152]{1,0:T(8,128)S(1)}, f32[256,1152]{1,0:T(8,128)S(1)}, bf16[256,1152]{1,0:T(8,128)(2,1)S(1)}) custom-call(f32[32,1536]{1,0:T(8,128)S(1)} %get-tuple-element.51.mid_ref, f32[1,1536]{1,0:T(1,128)S(1)} %get-tuple-element.152.gain_ref, ...), custom_call_target="tpu_custom_call" | custom-call | tf_op jit(solution)/shard_map/mlp_forward/pallas_call | solution.py:285
  416.1 1.0 copy-done.5
  417.1 1.0 copy-done.6
  418.2 0.9 copy-done.9
  419.1 0.8 copy-done.13
  419.9 1.4 copy-done.4
  422.7 34.2 %attn_forward.3 = (f32[32,1536]{1,0:T(8,128)S(1)}, bf16[4,32,1536]{2,1,0:T(8,128)(2,1)S(1)}, bf16[2,3,64,128]{3,2,1,0:T(8,128)(2,1)S(1)}, bf16[2,2,4,4,64,256]{5...) custom-call(f32[32,1536]{1,0:T(8,128)S(1)} %convert_convert_fusion.1.x_ref, ...), custom_call_target="tpu_custom_call" | custom-call | tf_op jit(solution)/shard_map/attn_forward/pallas_call | solution.py:186
  457.0 1.3 copy-done
  459.5 21.4 %mlp_forward.3 = (f32[32,1536]{1,0:T(8,128)S(1)}, bf16[2,4,32,1536]{3,2,1,0:T(8,128)(2,1)S(1)}, f32[256,1152]{1,0:T(8,128)S(1)}, f32[256,1152]{1,0:T(8,128)S(1)}, bf16[256,1152]{1,0:T(8,128)(2,1)S(1)}) custom-call(f32[32,1536]{1,0:T(8,128)S(1)} %get-tuple-element.54.mid_ref, f32[1,1536]{1,0:T(1,128)S(1)} %get-tuple-element.150.gain_ref, ...), custom_call_target="tpu_custom_call" | custom-call | tf_op jit(solution)/shard_map/mlp_forward/pallas_call | solution.py:285
  481.0 1.0 copy-done.7
  482.0 1.0 copy-done.8
  483.1 0.9 copy-done.10
  483.9 0.8 copy-done.14
  485.4 27.8 %mlp_backward.2 = (f32[32,1536]{1,0:T(8,128)}, f32[1,1536]{1,0:T(1,128)}, bf16[1536,3456]{1,0:T(8,128)(2,1)}) custom-call(f32[32,1536]{1,0:T(8,128)} %get-tuple-element.139.g_ref, f32[32,1536]{1,0:T(8,128)} %copy-done.12, f32[1,1536]{1,0:T(1,128)} %copy-done.28, bf16[1536,3456]{1,0:T(8,128)(2,1)} %all-gather.13.cloned.1.call-done.w_ref, ...), custom_call_target="tpu_custom_call" | custom-call | tf_op jit(solution)/shard_map/mlp_backward/pallas_call | solution.py:362
  513.3 0.9 copy-done.16
  514.2 39.6 %attn_backward.2 = (f32[32,1536]{1,0:T(8,128)S(1)}, f32[1,1536]{1,0:T(1,128)S(1)}, f32[1,512]{1,0:T(1,128)S(1)}, bf16[1536,512]{1,0:T(8,128)(2,1)}) custom-call(f32[32,1536]{1,0:T(8,128)S(1)} %copy-done.16, f32[32,1536]{1,0:T(8,128)S(1)} %convert_convert_fusion.1.x_ref, f32[1,1536]{1,0:T(1,128)S(1)} %copy-done.31, ...), custom_call_target="tpu_custom_call" | custom-call | tf_op jit(solution)/shard_map/attn_backward/pallas_call | solution.py:476
  554.5 27.7 %mlp_backward.3 = (f32[32,1536]{1,0:T(8,128)}, f32[1,1536]{1,0:T(1,128)}, bf16[1536,3456]{1,0:T(8,128)(2,1)}) custom-call(f32[32,1536]{1,0:T(8,128)} %convert_convert_fusion.g_ref, f32[32,1536]{1,0:T(8,128)} %copy-done.11, f32[1,1536]{1,0:T(1,128)} %copy-done.27, bf16[1536,3456]{1,0:T(8,128)(2,1)} %all-gather.9.cloned.1.call-done.w_ref, ...), custom_call_target="tpu_custom_call" | custom-call | tf_op jit(solution)/shard_map/mlp_backward/pallas_call | solution.py:362
  582.2 0.9 copy-done.15
  583.1 38.1 %attn_backward.3 = (f32[32,1536]{1,0:T(8,128)S(1)}, f32[1,1536]{1,0:T(1,128)S(1)}, f32[1,512]{1,0:T(1,128)S(1)}, bf16[1536,512]{1,0:T(8,128)(2,1)S(1)}) custom-call(f32[32,1536]{1,0:T(8,128)S(1)} %copy-done.15, f32[32,1536]{1,0:T(8,128)S(1)} %get-tuple-element.138.x_ref, f32[1,1536]{1,0:T(1,128)S(1)} %copy-done.30, ...), custom_call_target="tpu_custom_call" | custom-call | tf_op jit(solution)/shard_map/attn_backward/pallas_call | solution.py:476
  621.3 1.1 copy-done.2
  624.8 64.0 %psum.7 = f32[80,128]{1,0:T(8,128)S(1)} all-reduce(f32[80,128]{1,0:T(8,128)S(1)} %maximum_bitcast_fusion.2), channel_id=1, replica_groups=mesh['section'=2,'ctx'=32,'shard'=2] {'section','ctx','shard'}, use_global_device_ids=true, to_apply=%region_4.5 | all-reduce | flops 10240 | bytes 81920 | tf_op jit(solution)/shard_map/psum | solution.py:684
  692.6 76.1 %reduce-scatter.7.cloned.1.call-done = bf16[96,512]{1,0:T(8,128)(2,1)} async-done(((bf16[1536,512]{1,0:T(8,128)(2,1)}), bf16[96,512]{1,0:T(8,128)(2,1)}) %reduce-scatter.7.cloned.1.call-update) | async-done | bytes 98320 | tf_op jit(solution)/shard_map/reduce_scatter | solution.py:606
  768.7 1.6 pad_maximum_fusion.4.attn_ref
  770.3 92.3 %reduce-scatter.9.cloned.1.call-done = bf16[96,3456]{1,0:T(8,128)(2,1)} async-done(((bf16[1536,3456]{1,0:T(8,128)(2,1)}), bf16[96,3456]{1,0:T(8,128)(2,1)}) %reduce-scatter.9.cloned.1.call-update) | async-done | bytes 663568 | tf_op jit(solution)/shard_map/reduce_scatter | solution.py:606
  862.6 93.3 %reduce-scatter.11.cloned.1.call-done = bf16[96,3456]{1,0:T(8,128)(2,1)} async-done(((bf16[1536,3456]{1,0:T(8,128)(2,1)}), bf16[96,3456]{1,0:T(8,128)(2,1)}) %reduce-scatter.11.cloned.1.call-update) | async-done | bytes 663568 | tf_op jit(solution)/shard_map/reduce_scatter | solution.py:606
  955.9 2.5 pad_maximum_fusion.1.mlp_ref
  958.4 30.9 %gather_back.1 = (bf16[2,2,48,512]{3,2,1,0:T(8,128)(2,1)}, bf16[2,2,48,3456]{3,2,1,0:T(8,128)(2,1)}, f32[4,32,1536]{2,1,0:T(8,128)}) custom-call(bf16[2,2,48,512]{3,2,1,0:T(8,128)(2,1)} %pad_maximum_fusion.4.attn_ref, bf16[2,2,48,3456]{3,2,1,0:T(8,128)(2,1)} %pad_maximum_fusion.1.mlp_ref, f32[2,32,1536]{2,1,0:T(8,128)} %pad_maximum_fusion.2.ends_ref), custom_call_target="tpu_custom_call" | custom-call | tf_op jit(solution)/shard_map/gather_back/pallas_call | solution.py:579
  989.3 1.0 convert_element_type.33
  991.7 2.9 reshape.158
  994.5 3.5 copy.115
  998.1 3.5 reshape.155
  1001.5 1.0 slice_bitcast_fusion.1
  1002.5 1.3 slice_bitcast_fusion
  1006.2 3.6 copy.118
  1009.8 0.9 copy.146
  (178 shorter events, 21.8 us)
Async XLA Ops:
  7.2 352.1 %all-gather.7.cloned.1.call-start = ((), (), s32[]{:S(2)}) async-start(), calls=%async_computation.4 | async-start | bytes 1671168 | tf_op jit(solution)/shard_map/all_gather | solution.py:602
  9.0 2.4 copy-start.35
  37.4 359.0 %all-gather.9.cloned.1.call-start = ((), (), s32[]{:S(2)}) async-start(), calls=%async_computation.5 | async-start | bytes 11280384 | tf_op jit(solution)/shard_map/all_gather | solution.py:602
  37.4 3.9 copy-start.40
  37.4 5.4 copy-start.44
  37.4 5.5 copy-start.45
  37.4 5.6 copy-start.43
  40.0 379.9 %all-gather.11.cloned.1.call-start = ((), (), s32[]{:S(2)}) async-start(), calls=%async_computation.6 | async-start | bytes 1671168 | tf_op jit(solution)/shard_map/all_gather | solution.py:602
  40.7 418.8 %all-gather.13.cloned.1.call-start = ((), (), s32[]{:S(2)}) async-start(), calls=%async_computation.7 | async-start | bytes 11280384 | tf_op jit(solution)/shard_map/all_gather | solution.py:602
  41.3 651.3 %reduce-scatter.5.cloned.1.call-start = ((), (), s32[]{:S(2)}) async-start(), calls=%async_computation.8 | async-start | bytes 1671168 | tf_op jit(solution)/shard_map/reduce_scatter | solution.py:606
  41.4 317.1 %collective-permute-start = (f32[32,1536]{1,0:T(8,128)S(1)}, f32[32,1536]{1,0:T(8,128)S(1)}, u32[]{:S(2)}, u32[]{:S(2)}) collective-permute-start(f32[32,1536]{1,0:T(8,128)S(1)} %dynamic-slice_bitcast_fusion), channel_id=1, source_target_pairs={{0,64},{64,0},{1,65},{65,1},{2,66},{66,2},{3,67},{67,3},{4,68},{68... | collective-permute-start | bytes 589832 | tf_op jit(solution)/shard_map/ppermute | solution.py:619
  357.9 58.1 %copy-start.27 = (f32[1,1536]{1,0:T(1,128)}, f32[1,1536]{1,0:T(1,128)S(1)}, u32[]{:S(2)}) copy-start(f32[1,1536]{1,0:T(1,128)S(1)} %get-tuple-element.152.gain_ref) | copy-start | bytes 18436
  357.9 58.1 %copy-start.29 = (f32[1,1536]{1,0:T(1,128)}, f32[1,1536]{1,0:T(1,128)S(1)}, u32[]{:S(2)}) copy-start(f32[1,1536]{1,0:T(1,128)S(1)} %get-tuple-element.153.gain_ref) | copy-start | bytes 18436
  357.9 101.6 %copy-start.28 = (f32[1,1536]{1,0:T(1,128)}, f32[1,1536]{1,0:T(1,128)S(1)}, u32[]{:S(2)}) copy-start(f32[1,1536]{1,0:T(1,128)S(1)} %get-tuple-element.150.gain_ref) | copy-start | bytes 18436
  359.2 1.4 copy-start.3
  396.4 19.7 %copy-start.11 = (f32[32,1536]{1,0:T(8,128)}, f32[32,1536]{1,0:T(8,128)S(1)}, u32[]{:S(2)}) copy-start(f32[32,1536]{1,0:T(8,128)S(1)} %get-tuple-element.51.mid_ref) | copy-start | bytes 589828
  416.1 1.1 copy-start.5
  417.1 1.0 copy-start.6
  418.2 0.9 copy-start.9
  419.1 0.8 copy-start.13
  419.9 1.4 copy-start.4
  457.0 1.3 copy-start
  459.5 21.4 %copy-start.12 = (f32[32,1536]{1,0:T(8,128)}, f32[32,1536]{1,0:T(8,128)S(1)}, u32[]{:S(2)}) copy-start(f32[32,1536]{1,0:T(8,128)S(1)} %get-tuple-element.54.mid_ref) | copy-start | bytes 589828
  481.0 1.0 copy-start.7
  482.0 1.0 copy-start.8
  483.1 0.9 copy-start.10
  483.9 0.8 copy-start.14
  485.4 27.9 %copy-start.1 = (bf16[2,2,4,4,64,256]{5,4,3,2,1,0:T(8,128)(2,1)S(1)}, bf16[2,2,4,4,64,256]{5,4,3,2,1,0:T(8,128)(2,1)}, u32[]{:S(2)}) copy-start(bf16[2,2,4,4,64,256]{5,4,3,2,1,0:T(8,128)(2,1)} %copy-done) | copy-start | bytes 6291460
  485.4 27.9 %copy-start.24 = (bf16[2,3,64,128]{3,2,1,0:T(8,128)(2,1)S(1)}, bf16[2,3,64,128]{3,2,1,0:T(8,128)(2,1)}, u32[]{:S(2)}) copy-start(bf16[2,3,64,128]{3,2,1,0:T(8,128)(2,1)} %copy-done.23) | copy-start | bytes 294916
  485.4 27.9 %copy-start.26 = (bf16[128,384]{1,0:T(8,128)(2,1)S(1)}, bf16[128,384]{1,0:T(8,128)(2,1)}, u32[]{:S(2)}) copy-start(bf16[128,384]{1,0:T(8,128)(2,1)} %copy-done.25) | copy-start | bytes 294916
  513.3 0.9 copy-start.16
  553.8 0.7 copy-start.33
  554.5 27.7 %copy-start.20 = (bf16[2,3,64,128]{3,2,1,0:T(8,128)(2,1)S(1)}, bf16[2,3,64,128]{3,2,1,0:T(8,128)(2,1)}, u32[]{:S(2)}) copy-start(bf16[2,3,64,128]{3,2,1,0:T(8,128)(2,1)} %copy-done.19) | copy-start | bytes 294916
  554.5 27.7 %copy-start.22 = (bf16[128,384]{1,0:T(8,128)(2,1)S(1)}, bf16[128,384]{1,0:T(8,128)(2,1)}, u32[]{:S(2)}) copy-start(bf16[128,384]{1,0:T(8,128)(2,1)} %copy-done.21) | copy-start | bytes 294916
  554.5 27.7 %copy-start.30 = (f32[1,1536]{1,0:T(1,128)S(1)}, f32[1,1536]{1,0:T(1,128)}, u32[]{:S(2)}) copy-start(f32[1,1536]{1,0:T(1,128)} %copy-done.29) | copy-start | bytes 18436
  582.2 0.9 copy-start.15
  621.3 1.1 copy-start.2
  622.5 146.2 %reduce-scatter.7.cloned.1.call-start = ((), (), s32[]{:S(2)}) async-start(), calls=%async_computation.9 | async-start | bytes 1671168 | tf_op jit(solution)/shard_map/reduce_scatter | solution.py:606
  623.0 239.6 %reduce-scatter.9.cloned.1.call-start = ((), (), s32[]{:S(2)}) async-start(), calls=%async_computation.10 | async-start | bytes 11280384 | tf_op jit(solution)/shard_map/reduce_scatter | solution.py:606
  623.8 332.1 %reduce-scatter.11.cloned.1.call-start = ((), (), s32[]{:S(2)}) async-start(), calls=%async_computation.11 | async-start | bytes 11280384 | tf_op jit(solution)/shard_map/reduce_scatter | solution.py:606
  623.8 0.7 copy-start.42
  623.8 0.8 copy-start.41
  623.9 0.8 copy-start.34
  623.9 67.4 %copy-start.18 = (f32[32,1536]{1,0:T(8,128)S(1)}, f32[32,1536]{1,0:T(8,128)}, u32[]{:S(2)}) copy-start(f32[32,1536]{1,0:T(8,128)} %copy-done.17) | copy-start | bytes 589828
  1002.5 1.3 copy-start.38
  1002.5 2.2 copy-start.39
  1002.5 2.8 copy-start.37
  1006.2 3.6 copy-start.36
  (7 other events, 4.6 us)
Sparse Core Ops, SparseCore 0:
  37.5 45.0 all-gather.6
  85.3 81.3 all-gather.8
  169.5 42.6 all-gather.10
  214.7 81.3 all-gather.12
  622.6 69.9 reduce-scatter.4
  695.7 72.9 reduce-scatter.6
  772.1 90.4 reduce-scatter.8
  866.4 89.4 reduce-scatter.10

commit v2 on v1

--- a/solution.py
+++ b/solution.py
@@ -514,85 +514,379 @@
     )
 
 
-def spread_kernel(attn_ref, mlp_ref, attn_out, mlp_out, lsem, send, recv):
+def spread_kernel(attn_ref, mlp_ref, tiny_ref, ends_ref, attn_out, mlp_out, tiny_out, ends_out, lsem, send, recv):
     me = Place()
     peers = quad(me)
     greet([peer for _, _, peer in peers])
     net = Links(send, recv)
-    copies = []
-    for src, dst in ((attn_ref, attn_out), (mlp_ref, mlp_out)):
-        for core, section, peer in peers:
-            copies.append(net.go(src.at[section, core], dst.at[me.s, me.c], peer))
-    here = []
-    for i, (src, dst) in enumerate(((attn_ref, attn_out), (mlp_ref, mlp_out))):
-        copy = pltpu.make_async_copy(src.at[me.s, me.c], dst.at[me.s, me.c], lsem.at[i])
-        copy.start()
-        here.append(copy)
+    copies, here = [], []
+    away = pl.ds(pl.multiple_of((1 - me.s) * OWN, OWN), OWN)
+    home = pl.ds(pl.multiple_of(me.s * OWN, OWN), OWN)
+    for core, section, peer in peers:
+        copies.append(net.go(attn_ref.at[section, core], attn_out.at[me.s, me.c], peer))
+        copies.append(net.go(tiny_ref, tiny_out.at[me.s, me.c], peer))
+    copies.append(net.go(ends_ref.at[me.h, away], ends_out.at[me.s], {"section": 1 - me.s}))
+    for core, section, peer in peers:
+        copies.append(net.go(mlp_ref.at[section, core], mlp_out.at[me.s, me.c], peer))
+    pairs = (
+        (attn_ref.at[me.s, me.c], attn_out.at[me.s, me.c]),
+        (tiny_ref, tiny_out.at[me.s, me.c]),
+        (ends_ref.at[me.h, home], ends_out.at[me.s]),
+        (mlp_ref.at[me.s, me.c], mlp_out.at[me.s, me.c]),
+    )
+    for i, (src, dst) in enumerate(pairs):
+        here.append(pltpu.make_async_copy(src, dst, lsem.at[i]))
+        here[-1].start()
     for copy in here + copies:
         copy.wait()
 
 
-def spread(attn, mlp):
+def spread(attn, mlp, tiny, ends):
     return pl.pallas_call(
         spread_kernel,
-        out_shape=(jax.ShapeDtypeStruct(attn.shape, BF), jax.ShapeDtypeStruct(mlp.shape, BF)),
-        in_specs=[ANY, ANY],
-        out_specs=(ANY, ANY),
+        out_shape=(
+            jax.ShapeDtypeStruct(attn.shape, BF),
+            jax.ShapeDtypeStruct(mlp.shape, BF),
+            jax.ShapeDtypeStruct((2, 2) + tiny.shape, BF),
+            jax.ShapeDtypeStruct((2, OWN, D), F32),
+        ),
+        in_specs=[ANY] * 4,
+        out_specs=(ANY,) * 4,
         scratch_shapes=[
-            pltpu.SemaphoreType.DMA((2,)),
-            pltpu.SemaphoreType.DMA((6,)),
-            pltpu.SemaphoreType.DMA((6,)),
+            pltpu.SemaphoreType.DMA((4,)),
+            pltpu.SemaphoreType.DMA((10,)),
+            pltpu.SemaphoreType.DMA((10,)),
         ],
         compiler_params=pltpu.CompilerParams(collective_id=4, has_side_effects=True),
         name="spread",
-    )(attn, mlp)
-
-
-def gather_back_kernel(attn_ref, mlp_ref, ends_ref, attn_out, mlp_out, ends_out, lsem, send, recv):
+    )(attn, mlp, tiny, ends)
+
+
+def cuts(columns):
+    cut = (columns // 256) * 128
+    return (slice(0, cut), slice(cut, columns))
+
+
+SIDES = (1, 3)
+
+
+class Gather:
+    def __init__(self, net, me, src, buf, local):
+        self.net, self.me, self.src, self.buf, self.local = net, me, src, buf, local
+        self.cuts = cuts(src.shape[-1])
+        self.sent = []
+
+    def at(self, half, p, q):
+        return self.buf.at[q, p, 0] if half == 0 else self.buf.at[p, q, 1]
+
+    def axes(self, half):
+        me = self.me
+        return (me.x, me.z, me.xp, me.zp) if half == 0 else (me.z, me.x, me.zp, me.xp)
+
+    def go(self, src, dst, peer):
+        copy = self.net.go(src, dst, peer)
+        self.sent.append(copy)
+        return copy
+
+    def start(self):
+        me = self.me
+        self.own = pltpu.make_async_copy(self.src, self.buf.at[me.z, me.x], self.local)
+        self.own.start()
+        self.a, self.c = [None, None], [[None] * 4, [None] * 4]
+        for half in range(2):
+            p, q, pp, qp = self.axes(half)
+            self.a[half] = [self.go(self.src.at[half], self.at(half, p, q), pp(k)) for k in SIDES]
+        for half in range(2):
+            p, q, pp, qp = self.axes(half)
+            self.c[half][0] = [self.go(self.src.at[half], self.at(half, p, q), qp(k)) for k in SIDES]
+
+    def second(self):
+        self.f = [[], []]
+        for half in range(2):
+            p, q, pp, qp = self.axes(half)
+            for i, k in enumerate(SIDES):
+                self.a[half][i].wait_recv()
+                block = self.at(half, (p + 4 - k) % 4, q)
+                piece = block.at[:, self.cuts[i]]
+                self.f[half].append(self.go(piece, piece, pp(k)))
+        for half in range(2):
+            p, q, pp, qp = self.axes(half)
+            for i, k in enumerate(SIDES):
+                block = self.at(half, (p + 4 - k) % 4, q)
+                self.c[half][i + 1] = [self.go(block, block, qp(kk)) for kk in SIDES]
+
+    def third(self):
+        for half in range(2):
+            p, q, pp, qp = self.axes(half)
+            landed(self.f[half])
+            block = self.at(half, (p + 2) % 4, q)
+            self.c[half][3] = [self.go(block, block, qp(kk)) for kk in SIDES]
+
+    def fourth(self):
+        self.last = []
+        for j, shift in enumerate((0, 3, 1, 2)):
+            for half in range(2):
+                p, q, pp, qp = self.axes(half)
+                for i, k in enumerate(SIDES):
+                    self.c[half][j][i].wait_recv()
+                    piece = self.at(half, (p + shift) % 4, (q + 4 - k) % 4).at[:, self.cuts[i]]
+                    self.last.append(self.go(piece, piece, qp(k)))
+
+    def finish(self):
+        landed(self.last)
+        self.own.wait()
+        left(self.sent)
+
+    copies = 40
+
+
+def collect_kernel(a0, a1, m0, tiny, a0_out, a1_out, m0_out, tiny_out, lsem, send, recv):
+    me = Place()
+    greet([me.xp(1), me.xp(2), me.xp(3), me.zp(1), me.zp(2), me.zp(3)])
+    net = Links(send, recv)
+    parts = [Gather(net, me, src, dst, lsem.at[i]) for i, (src, dst) in enumerate(((a0, a0_out), (m0, m0_out), (a1, a1_out)))]
+    here = pltpu.make_async_copy(tiny, tiny_out.at[me.z, me.x], lsem.at[3])
+    here.start()
+    one = [net.go(tiny, tiny_out.at[me.z, me.x], me.xp(k)) for k in ORDER]
+    for part in parts:
+        part.start()
+    here.wait()
+    landed(one)
+    two = [net.go(tiny_out.at[me.z], tiny_out.at[me.z], me.zp(k)) for k in ORDER]
+    for part in parts:
+        part.second()
+    for part in parts:
+        part.third()
+    for part in parts:
+        part.fourth()
+    for part in parts:
+        part.finish()
+    landed(two)
+    left(one + two)
+
+
+def collect(a0, a1, m0, tiny):
+    return pl.pallas_call(
+        collect_kernel,
+        out_shape=tuple(jax.ShapeDtypeStruct((4, 4) + array.shape, BF) for array in (a0, a1, m0, tiny)),
+        in_specs=[ANY] * 4,
+        out_specs=(ANY,) * 4,
+        scratch_shapes=[
+            pltpu.SemaphoreType.DMA((4,)),
+            pltpu.SemaphoreType.DMA((3 * Gather.copies + 6,)),
+            pltpu.SemaphoreType.DMA((3 * Gather.copies + 6,)),
+        ],
+        compiler_params=pltpu.CompilerParams(collective_id=6, has_side_effects=True),
+        name="collect",
+    )(a0, a1, m0, tiny)
+
+
+class Scatter:
+    copies = 16
+
+    def __init__(self, net, me, src, buf, r1, r2, t, u1, u2, out, local):
+        self.net, self.me, self.src, self.buf, self.local = net, me, src, buf, local
+        self.r1, self.r2, self.t, self.u1, self.u2, self.out = r1, r2, t, u1, u2, out
+        self.cuts = cuts(src.shape[-1])
+        self.sent = []
+
+    @staticmethod
+    def scratch(rows, columns):
+        wide = columns - (columns // 256) * 128
+        return [
+            pltpu.VMEM((4, 4, 2, rows, columns), BF),
+            pltpu.VMEM((2, 2, 4, rows, wide), BF),
+            pltpu.VMEM((2, 2, 4, rows, columns), BF),
+            pltpu.VMEM((2, 4, rows, columns), BF),
+            pltpu.VMEM((2, 2, rows, wide), BF),
+            pltpu.VMEM((2, 2, rows, columns), BF),
+        ]
+
+    def group(self, ref, half, q):
+        return ref.at[q, :, 0] if half == 0 else ref.at[:, q, 1]
+
+    def axes(self, half):
+        me = self.me
+        return (me.x, me.z, me.xp, me.zp) if half == 0 else (me.z, me.x, me.zp, me.xp)
+
+    def go(self, src, dst, peer):
+        copy = self.net.go(src, dst, peer)
+        self.sent.append(copy)
+        return copy
+
+    def wide(self, i):
+        return slice(0, self.cuts[i].stop - self.cuts[i].start)
+
+    def start(self):
+        self.one = [[], []]
+        for half in range(2):
+            p, q, pp, qp = self.axes(half)
+            for i, k in enumerate(SIDES):
+                piece = self.group(self.src, half, (q + 2) % 4).at[:, :, self.cuts[i]]
+                self.one[half].append(self.go(piece, self.r1.at[half, i, :, :, self.wide(i)], qp(k)))
+        self.load = pltpu.make_async_copy(self.src, self.buf, self.local)
+        self.load.start()
+
+    def second(self):
+        self.load.wait()
+        self.two = [[], []]
+        for i, k in enumerate(SIDES):
+            for half in range(2):
+                p, q, pp, qp = self.axes(half)
+                self.one[half][i].wait_recv()
+                mine = self.group(self.buf, half, (q + k) % 4)
+
+                def add(j, _):
+                    mine[j, :, self.cuts[i]] = (
+                        mine[j, :, self.cuts[i]].astype(F32) + self.r1[half, i, j, :, self.wide(i)].astype(F32)
+                    ).astype(BF)
+                    return 0
+
+                lax.fori_loop(0, 4, add, 0)
+                self.two[half].append(self.go(mine, self.r2.at[half, i], qp(k)))
+
+    def third(self):
+        self.three = [[], []]
+        for half in range(2):
+            p, q, pp, qp = self.axes(half)
+            landed(self.two[half])
+            mine = self.group(self.buf, half, q)
+
+            def add(j, _):
+                self.t[half, j] = (
+                    mine[j].astype(F32) + self.r2[half, 0, j].astype(F32) + self.r2[half, 1, j].astype(F32)
+                ).astype(BF)
+                return 0
+
+            lax.fori_loop(0, 4, add, 0)
+            for i, k in enumerate(SIDES):
+                self.three[half].append(
+                    self.go(self.t.at[half, (p + 2) % 4, :, self.cuts[i]], self.u1.at[half, i, :, self.wide(i)], pp(k))
+                )
+
+    def fourth(self):
+        self.four = [[], []]
+        for half in range(2):
+            p, q, pp, qp = self.axes(half)
+            for i, k in enumerate(SIDES):
+                self.three[half][i].wait_recv()
+                place = (p + k) % 4
+                self.t[half, place, :, self.cuts[i]] = (
+                    self.t[half, place, :, self.cuts[i]].astype(F32) + self.u1[half, i, :, self.wide(i)].astype(F32)
+                ).astype(BF)
+                self.four[half].append(self.go(self.t.at[half, place], self.u2.at[half, i], pp(k)))
+
+    def fifth(self, half):
+        p, q, pp, qp = self.axes(half)
+        landed(self.four[half])
+        self.out[half] = (
+            self.t[half, p].astype(F32) + self.u2[half, 0].astype(F32) + self.u2[half, 1].astype(F32)
+        ).astype(BF)
+
+    def finish(self):
+        left(self.sent)
+
+
+def deposit_kernel(
+    a1, a0, m0, m1, small, ends,
+    attn_out, mlp_out, small_out, ends_out,
+    *scratch,
+):
     me = Place()
     peers = quad(me)
-    far = {"section": me.s, "shard": 1 - me.h}
-    cross = {"section": 1 - me.s, "shard": 1 - me.h}
-    greet([peer for _, _, peer in peers] + [far, cross])
+    greet(
+        [me.yp(1), me.yp(2), me.yp(3), me.xp(1), me.xp(2), me.xp(3), me.zp(1), me.zp(2), me.zp(3), me.cp()]
+        + [peers[2][2]]
+    )
+    res_a, res_m, sum_c, sum_got, lsem, send, recv = scratch[18:]
     net = Links(send, recv)
+    scatters = [
+        Scatter(net, me, src, *scratch[6 * i : 6 * i + 6], out, lsem.at[i])
+        for i, (src, out) in enumerate(((m0, res_m.at[0]), (a0, res_a.at[0]), (a1, res_a.at[1])))
+    ]
+    for scatter in scatters:
+        scatter.start()
     copies = []
-    for src, dst in ((attn_ref, attn_out), (mlp_ref, mlp_out)):
-        for core, section, peer in peers:
-            copies.append(net.go(src.at[section, core], dst.at[me.s, me.c], peer))
-    for k in ORDER:
-        copies.append(net.go(ends_ref.at[((me.y + k) % 4) % 2], ends_out.at[me.y], me.yp(k)))
-    here = []
-    pairs = (
-        (attn_ref.at[me.s, me.c], attn_out.at[me.s, me.c]),
-        (mlp_ref.at[me.s, me.c], mlp_out.at[me.s, me.c]),
-        (ends_ref.at[me.s], ends_out.at[me.y]),
-    )
-    for i, (src, dst) in enumerate(pairs):
-        copy = pltpu.make_async_copy(src, dst, lsem.at[i])
+    sum_c[0] = small[...]
+    rounds = ((me.yp, ORDER), (lambda k: me.cp(), (1,)), (me.xp, ORDER), (me.zp, ORDER))
+
+    def small_round(turn, slot):
+        peer, ks = rounds[turn]
+        sent = [net.go(sum_c.at[turn], sum_got.at[slot + k - 1], peer(k)) for k in ks]
+        copies.extend(sent)
+        landed(sent)
+        total = sum_c[turn]
+        for k in ks:
+            total = total + sum_got[slot + k - 1]
+        sum_c[turn + 1] = total
+
+    small_round(0, 0)
+    small_round(1, 3)
+    crossed = [net.go(ends.at[((me.y + k) % 4) % 2], ends_out.at[me.y], me.yp(k)) for k in ORDER]
+    here = [
+        pltpu.make_async_copy(ends.at[me.s], ends_out.at[me.y], lsem.at[3]),
+        pltpu.make_async_copy(m1, res_m.at[1], lsem.at[4]),
+    ]
+    for copy in here:
         copy.start()
-        here.append(copy)
-    for copy in here + copies:
-        copy.wait()
-
-
-def gather_back(attn, mlp, ends):
+    for scatter in scatters:
+        scatter.second()
+    small_round(2, 4)
+    small_round(3, 7)
+    for scatter in scatters:
+        scatter.third()
+    for scatter in scatters:
+        scatter.fourth()
+    for scatter in scatters:
+        scatter.fifth(0)
+        scatter.fifth(1)
+    here[1].wait()
+    last = []
+    for core, section, peer in peers:
+        last.append(net.go(res_a.at[section, core], attn_out.at[me.s, me.c], peer))
+        last.append(net.go(res_m.at[section, core], mlp_out.at[me.s, me.c], peer))
+    for i, (res, out) in enumerate(((res_a, attn_out), (res_m, mlp_out))):
+        here.append(pltpu.make_async_copy(res.at[me.s, me.c], out.at[me.s, me.c], lsem.at[5 + i]))
+        here[-1].start()
+    small_out[...] = sum_c[4]
+    here[0].wait()
+    here[2].wait()
+    here[3].wait()
+    landed(crossed + last)
+    left(copies + crossed + last)
+    for scatter in scatters:
+        scatter.finish()
+
+
+def deposit(a1, a0, m0, m1, small, ends):
+    rows = m1.shape[1]
+    shape = lambda array: array.reshape(4, 4, 2, rows, -1)
+    scratch = [
+        ref for columns in (3 * UNITS, QKW, QKW) for ref in Scatter.scratch(rows, columns)[:6]
+    ]
     return pl.pallas_call(
-        gather_back_kernel,
+        deposit_kernel,
         out_shape=(
-            jax.ShapeDtypeStruct(attn.shape, BF),
-            jax.ShapeDtypeStruct(mlp.shape, BF),
+            jax.ShapeDtypeStruct((2, 2, rows, QKW), BF),
+            jax.ShapeDtypeStruct((2, 2, rows, 3 * UNITS), BF),
+            jax.ShapeDtypeStruct(small.shape, F32),
             jax.ShapeDtypeStruct((4, OWN, D), F32),
         ),
-        in_specs=[ANY] * 3,
-        out_specs=(ANY,) * 3,
-        scratch_shapes=[
-            pltpu.SemaphoreType.DMA((3,)),
-            pltpu.SemaphoreType.DMA((9,)),
-            pltpu.SemaphoreType.DMA((9,)),
+        in_specs=[ANY, ANY, ANY, ANY, VM, ANY],
+        out_specs=(ANY, ANY, VM, ANY),
+        scratch_shapes=scratch
+        + [
+            pltpu.VMEM((2, 2, rows, QKW), BF),
+            pltpu.VMEM((2, 2, rows, 3 * UNITS), BF),
+            pltpu.VMEM((5,) + small.shape, F32),
+            pltpu.VMEM((10,) + small.shape, F32),
+            pltpu.SemaphoreType.DMA((7,)),
+            pltpu.SemaphoreType.DMA((3 * Scatter.copies + 19,)),
+            pltpu.SemaphoreType.DMA((3 * Scatter.copies + 19,)),
         ],
-        compiler_params=pltpu.CompilerParams(collective_id=5, has_side_effects=True),
-        name="gather_back",
-    )(attn, mlp, ends)
+        compiler_params=pltpu.CompilerParams(collective_id=5, has_side_effects=True, vmem_limit_bytes=56 << 20),
+        name="deposit",
+    )(shape(a1), shape(a0), shape(m0), m1, small, ends)
 
 
 SAME_CORE = [[core + 2 * chip for chip in range(16)] for core in range(2)]
@@ -614,12 +908,6 @@
 def body(ends, w_query, w_kv, w_out, w_gate_up, w_down, gains, bias_query, bias_kv):
     me = Place()
     rows = w_query.shape[1]
-    mine = lax.dynamic_slice(ends[0], (me.h, me.s * OWN, 0), (1, OWN, D))[0]
-    other = lax.dynamic_slice(ends[0], (me.h, (1 - me.s) * OWN, 0), (1, OWN, D))[0]
-    crossed = lax.ppermute(other, "section", [(0, 1), (1, 0)])
-    x = jnp.where(me.s == 0, mine, crossed)
-    cotangent = jnp.where(me.s == 0, crossed, mine)
-
     wq = w_query[0].reshape(rows, 2, 384)
     wo = w_out[0].reshape(rows, 2, 384)
     attn_pieces = jnp.stack(
@@ -636,19 +924,18 @@
     mlp_pieces = jnp.concatenate(
         [unit_slices(w_gate_up[0, :, 0]), unit_slices(w_gate_up[0, :, 1]), unit_slices(w_down[0])], axis=3
     )
-    attn_rows, mlp_rows = spread(attn_pieces, mlp_pieces)
-    attn_w = [None, None]
-    mlp_w = [None, None]
-    for l in range(2):
-        attn_w[l] = all_rows(attn_rows[l].reshape(2 * rows, QKW))
-        mlp_w[l] = all_rows(mlp_rows[l].reshape(2 * rows, 3 * UNITS))
-
     packed = jnp.concatenate([gains[0].reshape(-1), bias_query[0].reshape(-1), bias_kv[0].reshape(-1)])[None]
-    everything = lax.all_gather(packed, ("section", "ctx", "shard"), axis=0, tiled=True).astype(F32)
-    everything = everything.reshape(2, 32, 2, 128)
-    gain_all = everything[:, :, 0, :96].reshape(2, 32, 2, 48).transpose(0, 2, 1, 3).reshape(2, 2, 1, D)
-    bias_all = everything[:, :, :, 96:].reshape(2, 32, 2, 8, 4).transpose(2, 0, 3, 1, 4).reshape(2, 2, 8, 128)
-    bias_here = lax.dynamic_index_in_dim(bias_all, me.h, 0, keepdims=False)
+    attn_rows, mlp_rows, tiny_rows, tokens = spread(
+        attn_pieces, mlp_pieces, jnp.pad(packed, ((0, 15), (0, 0))), ends[0]
+    )
+    mlp_w1 = all_rows(mlp_rows[1].reshape(2 * rows, 3 * UNITS))
+    attn_w0, attn_w1, mlp_w0, tiny_all = collect(attn_rows[0], attn_rows[1], mlp_rows[0], tiny_rows)
+    attn_w = [attn_w0.reshape(D, QKW), attn_w1.reshape(D, QKW)]
+    mlp_w = [mlp_w0.reshape(D, 3 * UNITS), mlp_w1]
+
+    everything = tiny_all[:, :, :, :, 0].reshape(16, 2, 2, 128).astype(F32)
+    gain_all = everything[..., :96].reshape(16, 2, 2, 2, 48).transpose(1, 3, 0, 2, 4).reshape(2, 2, 1, D)
+    bias_here = everything[..., 96:].reshape(16, 2, 2, 8, 4).transpose(1, 3, 0, 2, 4).reshape(2, 8, 128)
     bias_q = lax.dynamic_slice(bias_here, (0, me.s * HEADS, 0), (2, HEADS, 128)).reshape(2, 1, 384)
     bias = jnp.concatenate([bias_q, bias_here[:, 6:8].reshape(2, 1, 256)], axis=2)
 
@@ -658,6 +945,7 @@
     cos = jnp.concatenate([jnp.cos(angles), jnp.cos(angles)], axis=1)
     sin = jnp.concatenate([-jnp.sin(angles), jnp.sin(angles)], axis=1)
 
+    x = tokens[0]
     inputs, kept = [], []
     for l in range(2):
         inputs.append(x)
@@ -666,14 +954,14 @@
         kept.append((mid, hid, q, kv, att, wf, hid2, gate, up, prod))
         x = out.astype(BF).astype(F32)
 
-    g = cotangent
+    g = tokens[1]
     attn_g, mlp_g, gain_g, bias_g = [None, None], [None, None], [None, None], [None, None]
     for l in (1, 0):
         mid, hid, q, kv, att, wf, hid2, gate, up, prod = kept[l]
-        gmid, ggain1, dw_mlp = mlp_backward(g, mid, gain_all[l, 1], mlp_w[l], hid2, gate, up, prod)
-        mlp_g[l] = own_rows(dw_mlp)
-        gin, ggain0, gbias, dw_attn = attn_backward(gmid, inputs[l], gain_all[l, 0], wf, hid, q, kv, att, cos, sin)
-        attn_g[l] = own_rows(dw_attn)
+        gmid, ggain1, mlp_g[l] = mlp_backward(g, mid, gain_all[l, 1], mlp_w[l], hid2, gate, up, prod)
+        if l == 1:
+            mlp_own1 = own_rows(mlp_g[1]).reshape(2, rows, 3 * UNITS)
+        gin, ggain0, gbias, attn_g[l] = attn_backward(gmid, inputs[l], gain_all[l, 0], wf, hid, q, kv, att, cos, sin)
         gain_g[l] = jnp.concatenate([ggain0, ggain1], axis=0)
         bias_g[l] = gbias
         g = gin.astype(BF).astype(F32) if l == 1 else gin
@@ -681,7 +969,10 @@
     small = jnp.stack(bias_g)
     small = jnp.where(jnp.arange(4)[None, :, None] == me.y, small, 0.0)
     small = jnp.concatenate([jnp.stack(gain_g).reshape(-1), small.reshape(-1)]).reshape(-1, 128)
-    small = lax.psum(small, ("section", "ctx", "shard")).reshape(-1)
+    attn_home, mlp_home, small, boundary = deposit(
+        attn_g[1], attn_g[0], mlp_g[0], mlp_own1, small, jnp.stack([g, out])
+    )
+    small = small.reshape(-1)
     gain_sum = small[: 4 * D].reshape(2, 2, 32, 48)
     bias_sum = small[4 * D :].reshape(2, 2, 2, 4, 32, 4)
     gain_sum = lax.dynamic_index_in_dim(gain_sum, me.s, 0, keepdims=False)
@@ -690,11 +981,6 @@
     bias_sum = lax.dynamic_index_in_dim(bias_sum, me.h, 0, keepdims=False)
     bias_sum = lax.dynamic_index_in_dim(bias_sum, me.ctx, 2, keepdims=False)
 
-    attn_home, mlp_home, boundary = gather_back(
-        jnp.stack(attn_g).reshape(2, 2, rows, QKW),
-        jnp.stack(mlp_g).reshape(2, 2, rows, 3 * UNITS),
-        jnp.stack([g, out]),
-    )
     attn_home = attn_home.astype(F32)
     mlp_home = mlp_home.astype(F32).reshape(2, 2, rows, 3, UNITS).transpose(2, 3, 0, 1, 4).reshape(rows, 3, 4 * UNITS)
     mlp_home = mlp_home[:, :, : w_down.shape[2]]

time: 1020 us -> 587 us (0.58)
  blocking collectives: 377 us -> 0 us
  waiting for transfers between devices: 265 us -> 0.04 us
  Pallas kernels: 294 us -> 509 us
    all_gather x1 -> x0, blocking collectives: 313 us -> none  [body(): lax.all_gather(packed, ('section', 'ctx', 'shard'), axis=0, tiled=True)]
    reduce_scatter x4 -> x1, waiting for transfers between devices: 262 us -> 0.01 us  [own_rows(): lax.psum_scatter(block, 'ctx', scatter_dimension=0, tiled=True, axis_inde...]
    pallas_call x1 -> x2, Pallas kernels: 30.9 us -> 232 us  [the longest x1 132 us: collect(): pl.pallas_call(collect_kernel, out_shape=tuple((jax.ShapeDtypeStruct((4,...]
    psum x1 -> x0, blocking collectives: 64 us -> none  [body(): small = lax.psum(small, ('section', 'ctx', 'shard')).reshape(-1)]
    unnamed x99 -> x101, local copies, waits for them, and re-layouts: 25.1 us -> 26 us
  transfers between devices with their start and end apart: 9 -> 2, of which waited for: 4 -> 0; matrix products, arithmetic and copies ran while one was open for 1% -> 1% of each run, Pallas kernels for 9% -> 58%
where the time goes in v2:
time: 587 us; the launch traced here: 581 us
  Pallas kernels  509 us (87%)
  local copies, waits for them, and re-layouts  51.4 us (9%)
  between operations  15.1 us (3%)
    pallas_call x1, Pallas kernels, collect(): pl.pallas_call(collect_kernel, out_shape=tuple((jax.ShapeDtypeStruct((4,...  132 us
    pallas_call x1, Pallas kernels, deposit(): pl.pallas_call(deposit_kernel, out_shape=(jax.ShapeDtypeStruct((2, 2, row...  100 us
    pallas_call x2, Pallas kernels, attn_backward(): pl.pallas_call(attn_backward_kernel, out_shape=(jax.ShapeDtypeStruct((OWN...  85.2 us
    pallas_call x2, Pallas kernels, attn_forward(): pl.pallas_call(attn_forward_kernel, out_shape=(jax.ShapeDtypeStruct((OWN,...  67.4 us
    pallas_call x2, Pallas kernels, mlp_backward(): pl.pallas_call(mlp_backward_kernel, out_shape=(jax.ShapeDtypeStruct((OWN,...  55.5 us
    pallas_call x2, Pallas kernels, mlp_forward(): pl.pallas_call(mlp_forward_kernel, out_shape=(jax.ShapeDtypeStruct((OWN,...  44.8 us
    unnamed x101, local copies, waits for them, and re-layouts  26 us
    pallas_call x1, Pallas kernels, spread(): pl.pallas_call(spread_kernel, out_shape=(jax.ShapeDtypeStruct(attn.shape,...  25 us
  transfers between devices with their start and end apart: 2, of which 0 were waited for; matrix products, arithmetic and copies ran while one was open for 1% of the time, Pallas kernels for 58%

profile of v2, /device:TPU:1, one launch (start us, length us, event | category | flops | bytes accessed | tf_op | source)
XLA Modules:
  0.0 581.4 jit_solution(14224102767632879112)
XLA Ops:
  7.2 1.0 reshape_squeeze.22
  8.3 0.9 fusion.9
  9.2 0.9 reshape_squeeze.23
  10.2 1.2 fusion.6
  12.0 0.7 copy-done.36
  14.1 0.7 pad_maximum_fusion.2.attn_ref
  14.8 1.2 pad_maximum_fusion.mlp_ref
  16.0 25.0 %spread.1 = (bf16[2,2,48,512]{3,2,1,0:T(8,128)(2,1)}, bf16[2,2,48,3456]{3,2,1,0:T(8,128)(2,1)}, bf16[2,2,16,128]{3,2,1,0:T(8,128)(2,1)}, f32[2,32,1536]{2,1,0:T(8,128)}) custom-call(bf16[2,2,48,512]{3,2,1,0:T(8,128)(2,1)} %pad_maximum_fusion.2.attn_ref, bf16[2,2,48,3456]{3,2,1,0:T(8,128)(2,1)} %pad_maximum_fusion.mlp_ref, bf16[16,128]{1,0:T(8,128)(2,1)} %pad.17.tiny_ref, ...), custom_call_target="tpu_custom_call" | custom-call | tf_op jit(solution)/shard_map/spread/pallas_call | solution.py:545
  41.0 2.5 fusion.5
  44.2 131.6 %collect.1 = (bf16[4,4,2,48,512]{4,3,2,1,0:T(8,128)(2,1)}, bf16[4,4,2,48,512]{4,3,2,1,0:T(8,128)(2,1)}, bf16[4,4,2,48,3456]{4,3,2,1,0:T(8,128)(2,1)}, bf16[4,4,2,2,16,128]{5,4,3,2,1,0:T(8,128)(2,1)}) custom-call(bf16[2,48,512]{2,1,0:T(8,128)(2,1)} %get-tuple-element.141.a0, bf16[2,48,512]{2,1,0:T(8,128)(2,1)} %get-tuple-element.140.a1, ...), custom_call_target="tpu_custom_call" | custom-call | tf_op jit(solution)/shard_map/collect/pallas_call | solution.py:669
  175.8 0.9 slice_convert_fusion
  178.2 0.7 slice_bitcast_fusion.3
  178.9 1.4 copy-done.3
  180.4 36.2 %attn_forward.2 = (f32[32,1536]{1,0:T(8,128)S(1)}, bf16[4,32,1536]{2,1,0:T(8,128)(2,1)S(1)}, bf16[2,3,64,128]{3,2,1,0:T(8,128)(2,1)S(1)}, bf16[2,2,4,4,64,256]{5...) custom-call(f32[32,1536]{1,0:T(8,128)S(1)} %get-tuple-element.138.x_ref, ...), custom_call_target="tpu_custom_call" | custom-call | tf_op jit(solution)/shard_map/attn_forward/pallas_call | solution.py:186
  217.9 22.5 %mlp_forward.2 = (f32[32,1536]{1,0:T(8,128)S(1)}, bf16[2,4,32,1536]{3,2,1,0:T(8,128)(2,1)S(1)}, f32[256,1152]{1,0:T(8,128)S(1)}, f32[256,1152]{1,0:T(8,128)S(1)}, bf16[256,1152]{1,0:T(8,128)(2,1)S(1)}) custom-call(f32[32,1536]{1,0:T(8,128)S(1)} %get-tuple-element.63.mid_ref, f32[1,1536]{1,0:T(1,128)S(1)} %get-tuple-element.148.gain_ref, ...), custom_call_target="tpu_custom_call" | custom-call | tf_op jit(solution)/shard_map/mlp_forward/pallas_call | solution.py:285
  240.4 1.1 copy-done.6
  241.5 1.0 copy-done.7
  242.5 0.9 copy-done.10
  243.4 0.8 copy-done.14
  244.3 31.2 %attn_forward.3 = (f32[32,1536]{1,0:T(8,128)S(1)}, bf16[4,32,1536]{2,1,0:T(8,128)(2,1)S(1)}, bf16[2,3,64,128]{3,2,1,0:T(8,128)(2,1)S(1)}, bf16[2,2,4,4,64,256]{5...) custom-call(f32[32,1536]{1,0:T(8,128)S(1)} %convert_convert_fusion.1.x_ref, ...), custom_call_target="tpu_custom_call" | custom-call | tf_op jit(solution)/shard_map/attn_forward/pallas_call | solution.py:186
  275.5 1.3 copy-done
  278.0 22.3 %mlp_forward.3 = (f32[32,1536]{1,0:T(8,128)S(1)}, bf16[2,4,32,1536]{3,2,1,0:T(8,128)(2,1)S(1)}, f32[256,1152]{1,0:T(8,128)S(1)}, f32[256,1152]{1,0:T(8,128)S(1)}, bf16[256,1152]{1,0:T(8,128)(2,1)S(1)}) custom-call(f32[32,1536]{1,0:T(8,128)S(1)} %get-tuple-element.67.mid_ref, f32[1,1536]{1,0:T(1,128)S(1)} %get-tuple-element.146.gain_ref, ...), custom_call_target="tpu_custom_call" | custom-call | tf_op jit(solution)/shard_map/mlp_forward/pallas_call | solution.py:285
  300.4 1.0 copy-done.8
  301.4 1.0 copy-done.9
  302.4 0.9 copy-done.11
  303.3 0.8 copy-done.15
  304.7 27.4 %mlp_backward.2 = (f32[32,1536]{1,0:T(8,128)}, f32[1,1536]{1,0:T(1,128)}, bf16[1536,3456]{1,0:T(8,128)(2,1)}) custom-call(f32[32,1536]{1,0:T(8,128)} %get-tuple-element.139.g_ref, f32[32,1536]{1,0:T(8,128)} %copy-done.13, f32[1,1536]{1,0:T(1,128)} %copy-done.29, bf16[1536,3456]{1,0:T(8,128)(2,1)} %all-gather.2.cloned.1.call-done.w_ref, ...), custom_call_target="tpu_custom_call" | custom-call | tf_op jit(solution)/shard_map/mlp_backward/pallas_call | solution.py:362
  332.2 0.9 copy-done.16
  333.1 1.6 copy-done.1
  334.7 0.9 copy-done.25
  335.6 0.9 copy-done.27
  336.5 46.7 %attn_backward.2 = (f32[32,1536]{1,0:T(8,128)S(1)}, f32[1,1536]{1,0:T(1,128)S(1)}, f32[1,512]{1,0:T(1,128)S(1)}, bf16[1536,512]{1,0:T(8,128)(2,1)S(1)}) custom-call(f32[32,1536]{1,0:T(8,128)S(1)} %copy-done.16, f32[32,1536]{1,0:T(8,128)S(1)} %convert_convert_fusion.1.x_ref, f32[1,1536]{1,0:T(1,128)S(1)} %copy-done.33, ...), custom_call_target="tpu_custom_call" | custom-call | tf_op jit(solution)/shard_map/attn_backward/pallas_call | solution.py:476
  383.1 1.1 copy-done.4
  384.3 0.7 convert_convert_fusion.g_ref
  385.0 28.1 %mlp_backward.3 = (f32[32,1536]{1,0:T(8,128)}, f32[1,1536]{1,0:T(1,128)}, bf16[1536,3456]{1,0:T(8,128)(2,1)}) custom-call(f32[32,1536]{1,0:T(8,128)} %convert_convert_fusion.g_ref, f32[32,1536]{1,0:T(8,128)} %copy-done.12, f32[1,1536]{1,0:T(1,128)} %copy-done.28, bf16[1536,3456]{1,0:T(8,128)(2,1)} %bitcast.141, bf16[2,4,32,1536]{3,2,1,0:T(8,128)(2,1)} %copy-done.10, ...), custom_call_target="tpu_custom_call" | custom-call | tf_op jit(solution)/shard_map/mlp_backward/pallas_call | solution.py:362
  413.1 0.9 copy-done.17
  414.0 38.5 %attn_backward.3 = (f32[32,1536]{1,0:T(8,128)S(1)}, f32[1,1536]{1,0:T(1,128)S(1)}, f32[1,512]{1,0:T(1,128)S(1)}, bf16[1536,512]{1,0:T(8,128)(2,1)S(1)}) custom-call(f32[32,1536]{1,0:T(8,128)S(1)} %copy-done.17, f32[32,1536]{1,0:T(8,128)S(1)} %get-tuple-element.138.x_ref, f32[1,1536]{1,0:T(1,128)S(1)} %copy-done.31, ...), custom_call_target="tpu_custom_call" | custom-call | tf_op jit(solution)/shard_map/attn_backward/pallas_call | solution.py:476
  452.5 1.1 copy-done.5
  454.5 0.8 pad_maximum_fusion.1.ends
  455.3 100.0 %deposit.1 = (bf16[2,2,48,512]{3,2,1,0:T(8,128)(2,1)}, bf16[2,2,48,3456]{3,2,1,0:T(8,128)(2,1)}, f32[80,128]{1,0:T(8,128)}, f32[4,32,1536]{2,1,0:T(8,128)}) custom-call(bf16[4,4,2,48,512]{4,3,2,1,0:T(8,128)(2,1)} %bitcast.134, bf16[4,4,2,48,512]{4,3,2,1,0:T(8,128)(2,1)} %bitcast.135, bf16[4,4,2,48,3456]{4,3,2,1,0:T(8,128)(2,1)} %bitcast.143, ...), custom_call_target="tpu_custom_call" | custom-call | tf_op jit(solution)/shard_map/deposit/pallas_call | solution.py:867
  555.2 3.1 reshape.167
  558.3 3.5 copy.69
  561.8 3.5 reshape.164
  565.5 1.0 slice_bitcast_fusion.1
  566.5 2.1 copy.73
  568.7 0.8 reshape.154
  569.6 0.8 reshape.155
  573.5 0.9 copy.104
  (153 shorter events, 11.8 us)
Async XLA Ops:
  7.2 3.0 copy-start.34
  7.2 270.8 %all-gather.2.cloned.1.call-start = ((), (), s32[]{:S(2)}) async-start(), calls=%async_computation.1 | async-start | bytes 11280384 | tf_op jit(solution)/shard_map/all_gather | solution.py:896
  11.7 1.0 copy-start.36
  11.9 1.0 copy-start.43
  11.9 1.2 copy-start.44
  11.9 1.3 copy-start.45
  41.0 2.6 copy-start.38
  43.5 134.8 %copy-start.37 = (f32[2,32,1536]{2,1,0:T(8,128)S(1)}, f32[2,32,1536]{2,1,0:T(8,128)}, u32[]{:S(2)}) copy-start(f32[2,32,1536]{2,1,0:T(8,128)} %get-tuple-element.57) | copy-start | bytes 1179652
  43.5 411.8 %reduce-scatter.2.cloned.1.call-start = ((), (), s32[]{:S(2)}) async-start(), calls=%async_computation.2 | async-start | bytes 11280384 | tf_op jit(solution)/shard_map/reduce_scatter | solution.py:900
  178.2 39.7 %copy-start.30 = (f32[1,1536]{1,0:T(1,128)}, f32[1,1536]{1,0:T(1,128)S(1)}, u32[]{:S(2)}) copy-start(f32[1,1536]{1,0:T(1,128)S(1)} %get-tuple-element.149.gain_ref) | copy-start | bytes 18436
  178.2 62.2 %copy-start.28 = (f32[1,1536]{1,0:T(1,128)}, f32[1,1536]{1,0:T(1,128)S(1)}, u32[]{:S(2)}) copy-start(f32[1,1536]{1,0:T(1,128)S(1)} %get-tuple-element.148.gain_ref) | copy-start | bytes 18436
  178.2 66.0 %copy-start.32 = (f32[1,1536]{1,0:T(1,128)}, f32[1,1536]{1,0:T(1,128)S(1)}, u32[]{:S(2)}) copy-start(f32[1,1536]{1,0:T(1,128)S(1)} %get-tuple-element.147.gain_ref) | copy-start | bytes 18436
  178.2 99.8 %copy-start.29 = (f32[1,1536]{1,0:T(1,128)}, f32[1,1536]{1,0:T(1,128)S(1)}, u32[]{:S(2)}) copy-start(f32[1,1536]{1,0:T(1,128)S(1)} %get-tuple-element.146.gain_ref) | copy-start | bytes 18436
  178.9 1.4 copy-start.3
  216.6 0.6 copy-start.20
  217.2 0.6 copy-start.22
  217.8 22.6 %copy-start.12 = (f32[32,1536]{1,0:T(8,128)}, f32[32,1536]{1,0:T(8,128)S(1)}, u32[]{:S(2)}) copy-start(f32[32,1536]{1,0:T(8,128)S(1)} %get-tuple-element.63.mid_ref) | copy-start | bytes 589828
  217.9 26.4 %copy-start.2 = (bf16[4,4,2,48,512]{4,3,2,1,0:T(8,128)(2,1)S(1)}, bf16[4,4,2,48,512]{4,3,2,1,0:T(8,128)(2,1)}, u32[]{:S(2)}) copy-start(bf16[4,4,2,48,512]{4,3,2,1,0:T(8,128)(2,1)} %get-tuple-element.66) | copy-start | bytes 4718596
  240.4 1.1 copy-start.6
  241.5 1.0 copy-start.7
  242.5 0.9 copy-start.10
  243.4 0.8 copy-start.14
  275.4 1.3 copy-start
  276.8 0.6 copy-start.24
  277.4 0.6 copy-start.26
  278.0 22.3 %copy-start.13 = (f32[32,1536]{1,0:T(8,128)}, f32[32,1536]{1,0:T(8,128)S(1)}, u32[]{:S(2)}) copy-start(f32[32,1536]{1,0:T(8,128)S(1)} %get-tuple-element.67.mid_ref) | copy-start | bytes 589828
  300.4 1.0 copy-start.8
  301.4 1.0 copy-start.9
  302.4 0.9 copy-start.11
  303.3 0.8 copy-start.15
  304.1 0.7 copy-start.18
  332.1 0.9 copy-start.16
  332.2 0.9 copy-start.33
  333.1 1.6 copy-start.1
  334.7 0.9 copy-start.25
  335.6 0.9 copy-start.27
  383.1 1.1 copy-start.4
  385.0 28.1 %copy-start.21 = (bf16[2,3,64,128]{3,2,1,0:T(8,128)(2,1)S(1)}, bf16[2,3,64,128]{3,2,1,0:T(8,128)(2,1)}, u32[]{:S(2)}) copy-start(bf16[2,3,64,128]{3,2,1,0:T(8,128)(2,1)} %copy-done.20) | copy-start | bytes 294916
  385.0 28.1 %copy-start.23 = (bf16[128,384]{1,0:T(8,128)(2,1)S(1)}, bf16[128,384]{1,0:T(8,128)(2,1)}, u32[]{:S(2)}) copy-start(bf16[128,384]{1,0:T(8,128)(2,1)} %copy-done.22) | copy-start | bytes 294916
  385.0 28.1 %copy-start.31 = (f32[1,1536]{1,0:T(1,128)S(1)}, f32[1,1536]{1,0:T(1,128)}, u32[]{:S(2)}) copy-start(f32[1,1536]{1,0:T(1,128)} %copy-done.30) | copy-start | bytes 18436
  413.1 0.9 copy-start.17
  414.0 39.7 %copy-start.42 = (f32[1,1536]{1,0:T(1,128)S(1)}, f32[1,1536]{1,0:T(1,128)}, u32[]{:S(2)}) copy-start(f32[1,1536]{1,0:T(1,128)} %get-tuple-element.94) | copy-start | bytes 18436
  414.0 39.7 %copy-start.41 = (f32[1,1536]{1,0:T(1,128)S(1)}, f32[1,1536]{1,0:T(1,128)}, u32[]{:S(2)}) copy-start(f32[1,1536]{1,0:T(1,128)} %get-tuple-element.96) | copy-start | bytes 18436
  414.0 40.5 %copy-start.19 = (f32[32,1536]{1,0:T(8,128)S(1)}, f32[32,1536]{1,0:T(8,128)}, u32[]{:S(2)}) copy-start(f32[32,1536]{1,0:T(8,128)} %copy-done.18) | copy-start | bytes 589828
  452.5 1.2 copy-start.5
  565.4 1.0 copy-start.39
  565.4 1.1 copy-start.40
  568.6 4.8 copy-start.35
Sparse Core Ops, SparseCore 0:
  43.6 133.6 all-gather.1
  332.3 93.1 reduce-scatter.1

commit v3 on v1

--- a/solution.py
+++ b/solution.py
@@ -1,3 +1,5 @@
+import functools
+
 import jax
 import jax.numpy as jnp
 from jax import lax
@@ -84,6 +86,254 @@
 ORDER = (1, 3, 2)
 
 
+def cuts(columns):
+    cut = (columns // 256) * 128
+    return (slice(0, cut), slice(cut, columns))
+
+
+SIDES = (1, 3)
+
+
+class Gather:
+    def __init__(self, net, me, src, buf, local):
+        self.net, self.me, self.src, self.buf, self.local = net, me, src, buf, local
+        self.cuts = cuts(src.shape[-1])
+        self.sent = []
+
+    def at(self, half, p, q):
+        return self.buf.at[q, p, 0] if half == 0 else self.buf.at[p, q, 1]
+
+    def axes(self, half):
+        me = self.me
+        return (me.x, me.z, me.xp, me.zp) if half == 0 else (me.z, me.x, me.zp, me.xp)
+
+    def go(self, src, dst, peer):
+        copy = self.net.go(src, dst, peer)
+        self.sent.append(copy)
+        return copy
+
+    def start(self):
+        me = self.me
+        self.own = pltpu.make_async_copy(self.src, self.buf.at[me.z, me.x], self.local)
+        self.own.start()
+        self.a, self.c = [None, None], [[None] * 4, [None] * 4]
+        for half in range(2):
+            p, q, pp, qp = self.axes(half)
+            self.a[half] = [self.go(self.src.at[half], self.at(half, p, q), pp(k)) for k in SIDES]
+        for half in range(2):
+            p, q, pp, qp = self.axes(half)
+            self.c[half][0] = [self.go(self.src.at[half], self.at(half, p, q), qp(k)) for k in SIDES]
+
+    def second(self):
+        self.f = [[], []]
+        for half in range(2):
+            p, q, pp, qp = self.axes(half)
+            for i, k in enumerate(SIDES):
+                self.a[half][i].wait_recv()
+                block = self.at(half, (p + 4 - k) % 4, q)
+                piece = block.at[:, self.cuts[i]]
+                self.f[half].append(self.go(piece, piece, pp(k)))
+        for half in range(2):
+            p, q, pp, qp = self.axes(half)
+            for i, k in enumerate(SIDES):
+                block = self.at(half, (p + 4 - k) % 4, q)
+                self.c[half][i + 1] = [self.go(block, block, qp(kk)) for kk in SIDES]
+
+    def third(self):
+        for half in range(2):
+            p, q, pp, qp = self.axes(half)
+            landed(self.f[half])
+            block = self.at(half, (p + 2) % 4, q)
+            self.c[half][3] = [self.go(block, block, qp(kk)) for kk in SIDES]
+        self.last = []
+        self.onward((0,))
+
+    def fourth(self):
+        self.onward((1, 2, 3))
+
+    def onward(self, turns):
+        for j in turns:
+            shift = (0, 3, 1, 2)[j]
+            for half in range(2):
+                p, q, pp, qp = self.axes(half)
+                for i, k in enumerate(SIDES):
+                    self.c[half][j][i].wait_recv()
+                    piece = self.at(half, (p + shift) % 4, (q + 4 - k) % 4).at[:, self.cuts[i]]
+                    self.last.append(self.go(piece, piece, qp(k)))
+
+    def finish(self):
+        landed(self.last)
+        self.own.wait()
+        left(self.sent)
+
+    copies = 40
+
+    def steps(self):
+        return [self.start, self.second, self.third, self.fourth, self.finish]
+
+
+class Scatter:
+    copies = 16
+
+    def __init__(self, net, me, src, buf, r1, r2, t, u1, u2, out, local):
+        self.net, self.me, self.src, self.buf, self.local = net, me, src, buf, local
+        self.r1, self.r2, self.t, self.u1, self.u2, self.out = r1, r2, t, u1, u2, out
+        self.cuts = cuts(src.shape[-1])
+        self.sent = []
+
+    @staticmethod
+    def scratch(rows, columns):
+        wide = columns - (columns // 256) * 128
+        return [
+            pltpu.VMEM((4, 4, 2, rows, columns), BF),
+            pltpu.VMEM((2, 2, 4, rows, wide), BF),
+            pltpu.VMEM((2, 2, 4, rows, columns), BF),
+            pltpu.VMEM((2, 4, rows, columns), BF),
+            pltpu.VMEM((2, 2, rows, wide), BF),
+            pltpu.VMEM((2, 2, rows, columns), BF),
+        ]
+
+    def group(self, ref, half, q):
+        return ref.at[q, :, 0] if half == 0 else ref.at[:, q, 1]
+
+    def axes(self, half):
+        me = self.me
+        return (me.x, me.z, me.xp, me.zp) if half == 0 else (me.z, me.x, me.zp, me.xp)
+
+    def go(self, src, dst, peer):
+        copy = self.net.go(src, dst, peer)
+        self.sent.append(copy)
+        return copy
+
+    def wide(self, i):
+        return slice(0, self.cuts[i].stop - self.cuts[i].start)
+
+    def start(self):
+        self.one = [[], []]
+        for half in range(2):
+            p, q, pp, qp = self.axes(half)
+            for i, k in enumerate(SIDES):
+                piece = self.group(self.src, half, (q + 2) % 4).at[:, :, self.cuts[i]]
+                self.one[half].append(self.go(piece, self.r1.at[half, i, :, :, self.wide(i)], qp(k)))
+        self.load = pltpu.make_async_copy(self.src, self.buf, self.local)
+        self.load.start()
+
+    def second(self):
+        self.load.wait()
+        self.two = [[], []]
+        for i, k in enumerate(SIDES):
+            for half in range(2):
+                p, q, pp, qp = self.axes(half)
+                self.one[half][i].wait_recv()
+                mine = self.group(self.buf, half, (q + k) % 4)
+
+                def add(j, _):
+                    mine[j, :, self.cuts[i]] = (
+                        mine[j, :, self.cuts[i]].astype(F32) + self.r1[half, i, j, :, self.wide(i)].astype(F32)
+                    ).astype(BF)
+                    return 0
+
+                lax.fori_loop(0, 4, add, 0)
+                self.two[half].append(self.go(mine, self.r2.at[half, i], qp(k)))
+
+    def third(self):
+        self.three = [[], []]
+        for half in range(2):
+            p, q, pp, qp = self.axes(half)
+            landed(self.two[half])
+            mine = self.group(self.buf, half, q)
+
+            def add(j, _):
+                self.t[half, j] = (
+                    mine[j].astype(F32) + self.r2[half, 0, j].astype(F32) + self.r2[half, 1, j].astype(F32)
+                ).astype(BF)
+                return 0
+
+            lax.fori_loop(0, 4, add, 0)
+            for i, k in enumerate(SIDES):
+                self.three[half].append(
+                    self.go(self.t.at[half, (p + 2) % 4, :, self.cuts[i]], self.u1.at[half, i, :, self.wide(i)], pp(k))
+                )
+
+    def fourth(self):
+        self.four = [[], []]
+        for half in range(2):
+            p, q, pp, qp = self.axes(half)
+            for i, k in enumerate(SIDES):
+                self.three[half][i].wait_recv()
+                place = (p + k) % 4
+                self.t[half, place, :, self.cuts[i]] = (
+                    self.t[half, place, :, self.cuts[i]].astype(F32) + self.u1[half, i, :, self.wide(i)].astype(F32)
+                ).astype(BF)
+                self.four[half].append(self.go(self.t.at[half, place], self.u2.at[half, i], pp(k)))
+
+    def fifth(self, half):
+        p, q, pp, qp = self.axes(half)
+        landed(self.four[half])
+        self.out[half] = (
+            self.t[half, p].astype(F32) + self.u2[half, 0].astype(F32) + self.u2[half, 1].astype(F32)
+        ).astype(BF)
+
+    def end(self):
+        self.fifth(0)
+        self.fifth(1)
+
+    def finish(self):
+        left(self.sent)
+
+    def steps(self):
+        return [self.start, self.second, self.third, self.fourth, self.end, self.finish]
+
+
+class Beside:
+    def __init__(self, jobs):
+        self.turns = [list(job.steps()) for job in jobs]
+
+    def step(self):
+        for turns in self.turns:
+            if turns:
+                turns.pop(0)()
+
+    def rest(self):
+        while any(self.turns):
+            self.step()
+
+
+def gather_jobs(net, me, views, bufs, lsem):
+    return Beside([Gather(net, me, src, buf, lsem.at[i]) for i, (src, buf) in enumerate(zip(views, bufs))])
+
+
+def scatter_jobs(net, me, srcs, outs, scratch, lsem):
+    return Beside(
+        [Scatter(net, me, src, *scratch[6 * i : 6 * i + 6], out, lsem.at[i]) for i, (src, out) in enumerate(zip(srcs, outs))]
+    )
+
+
+def xz(me):
+    return [me.xp(1), me.xp(2), me.xp(3), me.zp(1), me.zp(2), me.zp(3)]
+
+
+def sems(count, jobs, kind):
+    total = count + jobs * kind.copies
+    return [pltpu.SemaphoreType.DMA((max(jobs, 1),)), pltpu.SemaphoreType.DMA((total,)), pltpu.SemaphoreType.DMA((total,))]
+
+
+def params(collective_id):
+    return pltpu.CompilerParams(collective_id=collective_id, has_side_effects=True, vmem_limit_bytes=60 << 20)
+
+
+def gathered(views):
+    return tuple(jax.ShapeDtypeStruct((4, 4, 2, view[2], view[1].stop - view[1].start), BF) for view in views)
+
+
+def view_of(rows_ref, view):
+    return rows_ref.at[view[0], :, :, view[1]]
+
+
+def by_blocks(array):
+    return array.reshape(4, 4, 2, array.shape[0] // 32, -1)
+
+
 def unit_rms(u):
     scale = lax.rsqrt(jnp.mean(u * u, axis=1, keepdims=True) + EPS)
     return u * scale, scale
@@ -120,14 +370,14 @@
     return jnp.where(key_places(rows) <= query, raw * (HD**-0.5), -1e30)
 
 
-def attn_forward_kernel(
-    x_ref, gain_ref, w_ref, bias_ref, cos_ref, sin_ref,
-    mid_ref, hid_ref, q_ref, kv_ref, att_ref, wf_ref,
-    part_ref, got_ref, wsem, send, recv,
-):
+def attn_forward_kernel(views, x_ref, gain_ref, w_ref, bias_ref, cos_ref, sin_ref, rows_ref, *refs):
+    mid_ref, hid_ref, q_ref, kv_ref, att_ref, wf_ref = refs[:6]
+    bufs = refs[6 : 6 + len(views)]
+    part_ref, got_ref, wsem, lsem, send, recv = refs[6 + len(views) :]
     me = Place()
-    greet([me.yp(1), me.yp(2), me.yp(3), me.xp(1), me.xp(2), me.xp(3), me.zp(1), me.zp(2), me.zp(3), me.cp()])
+    greet([me.yp(1), me.yp(2), me.yp(3), me.cp()] + xz(me))
     net = Links(send, recv)
+    beside = gather_jobs(net, me, [view_of(rows_ref, view) for view in views], bufs, lsem)
     weights_over = net.go(w_ref, wf_ref.at[me.c], me.cp())
     weights_here = pltpu.make_async_copy(w_ref, wf_ref.at[me.c], wsem)
     weights_here.start()
@@ -135,6 +385,7 @@
     normed, _ = unit_rms(x)
     hid_ref[me.y] = (normed * gain_ref[...]).astype(BF)
     hid_copies = [net.go(hid_ref.at[me.y], hid_ref.at[me.y], me.yp(k)) for k in ORDER]
+    beside.step()
     cos, sin = twice(cos_ref[...]), twice(sin_ref[...])
     weights_here.wait()
     weights_over.wait()
@@ -153,6 +404,7 @@
         query = turned(proj[:, head * HD : (head + 1) * HD], cos, sin).astype(BF)
         for m in range(2):
             q_ref[m, head] = query[m * TOK : (m + 1) * TOK]
+    beside.step()
     landed(first0)
     second0 = [net.go(kv_ref.at[me.c, 0, me.z], kv_ref.at[me.c, 0, me.z], me.zp(k)) for k in ORDER]
     landed(first1)
@@ -161,6 +413,7 @@
     third0 = net.go(kv_ref.at[me.c, 0], kv_ref.at[me.c, 0], me.cp())
     landed(second1)
     third1 = net.go(kv_ref.at[me.c, 1], kv_ref.at[me.c, 1], me.cp())
+    beside.step()
     for m, third in ((0, third0), (1, third1)):
         third.wait_recv()
         queries = q_ref[m].reshape(HEADS * TOK, HD)
@@ -174,17 +427,20 @@
             att_ref[m * TOK : (m + 1) * TOK, head * HD : (head + 1) * HD] = out[head * TOK : (head + 1) * TOK]
     part_ref[...] = dot(att_ref[...], wf_ref[1, :, :384], 1, 1).astype(BF).reshape(4, OWN, D)
     back = [net.go(part_ref.at[(me.y + k) % 4], got_ref.at[k - 1], me.yp(k)) for k in ORDER]
+    beside.step()
     total = x + part_ref[me.y].astype(F32)
     landed(back)
     for k in range(3):
         total = total + got_ref[k].astype(F32)
     mid_ref[...] = total
+    beside.rest()
     left(hid_copies + first0 + first1 + second0 + second1 + [third0, third1] + back)
 
 
-def attn_forward(x, gain, w_half, bias, cos, sin):
+def attn_forward(x, gain, w_half, bias, cos, sin, rows, views, collective_id):
+    views = [view + (rows.shape[2],) for view in views]
     return pl.pallas_call(
-        attn_forward_kernel,
+        functools.partial(attn_forward_kernel, views),
         out_shape=(
             jax.ShapeDtypeStruct((OWN, D), F32),
             jax.ShapeDtypeStruct((4, OWN, D), BF),
@@ -192,27 +448,29 @@
             jax.ShapeDtypeStruct((2, 2, 4, 4, TOK, 2 * HD), BF),
             jax.ShapeDtypeStruct((2 * TOK, HEADS * HD), BF),
             jax.ShapeDtypeStruct((2, D, QKW), BF),
-        ),
-        in_specs=[VM, VM, ANY, VM, VM, VM],
-        out_specs=(VM,) * 6,
+        )
+        + gathered(views),
+        in_specs=[VM, VM, ANY, VM, VM, VM, ANY],
+        out_specs=(VM,) * 6 + (ANY,) * len(views),
         scratch_shapes=[
             pltpu.VMEM((4, OWN, D), BF),
             pltpu.VMEM((3, OWN, D), BF),
             pltpu.SemaphoreType.DMA,
-            pltpu.SemaphoreType.DMA((21,)),
-            pltpu.SemaphoreType.DMA((21,)),
-        ],
-        compiler_params=pltpu.CompilerParams(collective_id=0, has_side_effects=True, vmem_limit_bytes=48 << 20),
+        ]
+        + sems(21, len(views), Gather),
+        compiler_params=params(collective_id),
         name="attn_forward",
-    )(x, gain, w_half, bias, cos, sin)
-
-
-def fetch_mlp(w_ref, w_vmem, sems):
+    )(x, gain, w_half, bias, cos, sin, rows)
+
+
+def fetch_mlp(w_refs, w_vmem, sems):
     copies = []
-    for part in range(3):
-        copy = pltpu.make_async_copy(w_ref.at[:, part * UNITS : (part + 1) * UNITS], w_vmem.at[part], sems.at[part])
-        copy.start()
-        copies.append(copy)
+    part = 0
+    for ref in w_refs:
+        for i in range(ref.shape[1] // UNITS):
+            copies.append(pltpu.make_async_copy(ref.at[:, i * UNITS : (i + 1) * UNITS], w_vmem.at[part], sems.at[part]))
+            copies[-1].start()
+            part += 1
     return copies
 
 
@@ -245,21 +503,25 @@
     return total
 
 
-def mlp_forward_kernel(
-    mid_ref, gain_ref, w_ref,
-    out_ref, hid_ref, gate_ref, up_ref, prod_ref,
-    w_vmem, acc, part, mate, got, wsem, send, recv,
-):
+def mlp_forward_kernel(weight_count, views, mid_ref, gain_ref, *refs):
+    w_refs = refs[:weight_count]
+    row_refs = refs[weight_count : weight_count + len(views)]
+    refs = refs[weight_count + len(views) :]
+    out_ref, hid_ref, gate_ref, up_ref, prod_ref = refs[:5]
+    bufs = refs[5 : 5 + len(views)]
+    w_vmem, acc, part, mate, got, wsem, lsem, send, recv = refs[5 + len(views) :]
     me = Place()
-    weights = fetch_mlp(w_ref, w_vmem, wsem)
-    greet([me.yp(1), me.yp(2), me.yp(3), me.cp()])
+    weights = fetch_mlp(w_refs, w_vmem, wsem)
+    greet([me.yp(1), me.yp(2), me.yp(3), me.cp()] + (xz(me) if views else []))
     net = Links(send, recv)
+    beside = gather_jobs(net, me, [view_of(ref, view) for ref, view in zip(row_refs, views)], bufs, lsem)
     normed, _ = unit_rms(mid_ref[...])
     hid_ref[me.c, me.y] = (normed * gain_ref[...]).astype(BF)
-    gathered = gather_yc(net, me, hid_ref)
+    beside.step()
+    spread_out = gather_yc(net, me, hid_ref)
     for copy in weights:
         copy.wait()
-    hidden = hid_ref[...].reshape(256, D)
+    beside.step()
     acc[...] = jnp.zeros_like(acc)
 
     def step(i, _):
@@ -276,23 +538,28 @@
     lax.fori_loop(0, UNITS // CHUNK, step, 0)
     part[...] = acc[...].astype(BF).reshape(2, 4, OWN, D)
     swap = scatter_yc_start(net, me, part, mate)
+    beside.step()
     back = scatter_yc_middle(net, me, part, mate, got, swap)
+    beside.step()
     out_ref[...] = mid_ref[...] + scatter_yc_end(me, mate, got, back)
-    left(gathered + [swap] + back)
-
-
-def mlp_forward(mid, gain, w):
+    beside.rest()
+    left(spread_out + [swap] + back)
+
+
+def mlp_forward(mid, gain, weights, rows, views, collective_id):
+    views = [view + (ref.shape[2],) for ref, view in zip(rows, views)]
     return pl.pallas_call(
-        mlp_forward_kernel,
+        functools.partial(mlp_forward_kernel, len(weights), views),
         out_shape=(
             jax.ShapeDtypeStruct((OWN, D), F32),
             jax.ShapeDtypeStruct((2, 4, OWN, D), BF),
             jax.ShapeDtypeStruct((256, UNITS), F32),
             jax.ShapeDtypeStruct((256, UNITS), F32),
             jax.ShapeDtypeStruct((256, UNITS), BF),
-        ),
-        in_specs=[VM, VM, ANY],
-        out_specs=(VM,) * 5,
+        )
+        + gathered(views),
+        in_specs=[VM, VM] + [ANY] * (len(weights) + len(rows)),
+        out_specs=(VM,) * 5 + (ANY,) * len(views),
         scratch_shapes=[
             pltpu.VMEM((3, D, UNITS), BF),
             pltpu.VMEM((256, D), F32),
@@ -300,25 +567,30 @@
             pltpu.VMEM((4, OWN, D), BF),
             pltpu.VMEM((3, OWN, D), BF),
             pltpu.SemaphoreType.DMA((3,)),
-            pltpu.SemaphoreType.DMA((11,)),
-            pltpu.SemaphoreType.DMA((11,)),
-        ],
-        compiler_params=pltpu.CompilerParams(collective_id=1, has_side_effects=True, vmem_limit_bytes=48 << 20),
+        ]
+        + sems(11, len(views), Gather),
+        compiler_params=params(collective_id),
         name="mlp_forward",
-    )(mid, gain, w)
-
-
-def mlp_backward_kernel(
-    g_ref, mid_ref, gain_ref, w_ref, hid_ref, gate_ref, up_ref, prod_ref,
-    gmid_ref, ggain_ref, dw_ref,
-    w_vmem, low, dgate, dup, acc, part, mate, got, wsem, send, recv,
-):
+    )(mid, gain, *weights, *rows)
+
+
+def mlp_backward_kernel(weight_count, jobs, g_ref, mid_ref, gain_ref, hid_ref, gate_ref, up_ref, prod_ref, *refs):
+    w_refs = refs[:weight_count]
+    srcs = refs[weight_count : weight_count + jobs]
+    refs = refs[weight_count + jobs :]
+    gmid_ref, ggain_ref, dgu_ref, dd_ref = refs[:4]
+    outs = refs[4 : 4 + jobs]
+    w_vmem, low, dgate, dup, acc, part, mate, got, wsem = refs[4 + jobs : 13 + jobs]
+    job_scratch = refs[13 + jobs : 13 + 7 * jobs]
+    lsem, send, recv = refs[13 + 7 * jobs :]
     me = Place()
-    weights = fetch_mlp(w_ref, w_vmem, wsem)
-    greet([me.yp(1), me.yp(2), me.yp(3), me.cp()])
+    weights = fetch_mlp(w_refs, w_vmem, wsem)
+    greet([me.yp(1), me.yp(2), me.yp(3), me.cp()] + (xz(me) if jobs else []))
     net = Links(send, recv)
+    beside = scatter_jobs(net, me, srcs, outs, job_scratch, lsem)
     low[me.c, me.y] = g_ref[...].astype(BF)
-    gathered = gather_yc(net, me, low)
+    beside.step()
+    spread_out = gather_yc(net, me, low)
     for copy in weights:
         copy.wait()
     acc[...] = jnp.zeros_like(acc)
@@ -339,7 +611,9 @@
     part[...] = acc[...].astype(BF).reshape(2, 4, OWN, D)
     swap = scatter_yc_start(net, me, part, mate)
 
-    def weight_grads(index, left_ref, right_ref):
+    beside.step()
+
+    def weight_grads(dw_ref, index, left_ref, right_ref):
         def step_w(i, _):
             cols = pl.ds(pl.multiple_of(i * CHUNK, CHUNK), CHUNK)
             where = pl.ds(pl.multiple_of(index * UNITS + i * CHUNK, CHUNK), CHUNK)
@@ -349,25 +623,38 @@
         lax.fori_loop(0, UNITS // CHUNK, step_w, 0)
 
     back = scatter_yc_middle(net, me, part, mate, got, swap)
-    weight_grads(0, hid_ref, dgate)
-    weight_grads(1, hid_ref, dup)
-    weight_grads(2, low, prod_ref)
+    weight_grads(dgu_ref, 0, hid_ref, dgate)
+    beside.step()
+    weight_grads(dgu_ref, 1, hid_ref, dup)
+    beside.step()
+    weight_grads(dd_ref, 0, low, prod_ref)
     dy = scatter_yc_end(me, mate, got, back)
     du, ggain_ref[...] = norm_back(mid_ref[...], gain_ref[...], dy)
     gmid_ref[...] = g_ref[...] + du
-    left(gathered + [swap] + back)
-
-
-def mlp_backward(g, mid, gain, w, hid, gate, up, prod):
+    beside.rest()
+    left(spread_out + [swap] + back)
+
+
+def job_outs(jobs):
+    return tuple(jax.ShapeDtypeStruct((2, job.shape[0] // 32, job.shape[1]), BF) for job in jobs)
+
+
+def job_scratch(jobs):
+    return [ref for job in jobs for ref in Scatter.scratch(job.shape[0] // 32, job.shape[1])]
+
+
+def mlp_backward(g, mid, gain, weights, hid, gate, up, prod, jobs, collective_id):
     return pl.pallas_call(
-        mlp_backward_kernel,
+        functools.partial(mlp_backward_kernel, len(weights), len(jobs)),
         out_shape=(
             jax.ShapeDtypeStruct((OWN, D), F32),
             jax.ShapeDtypeStruct((1, D), F32),
-            jax.ShapeDtypeStruct((D, 3 * UNITS), BF),
-        ),
-        in_specs=[VM, VM, VM, ANY, VM, VM, VM, VM],
-        out_specs=(VM,) * 3,
+            jax.ShapeDtypeStruct((D, 2 * UNITS), BF),
+            jax.ShapeDtypeStruct((D, UNITS), BF),
+        )
+        + job_outs(jobs),
+        in_specs=[VM] * 7 + [ANY] * (len(weights) + len(jobs)),
+        out_specs=(VM,) * (4 + len(jobs)),
         scratch_shapes=[
             pltpu.VMEM((3, D, UNITS), BF),
             pltpu.VMEM((2, 4, OWN, D), BF),
@@ -378,26 +665,33 @@
             pltpu.VMEM((4, OWN, D), BF),
             pltpu.VMEM((3, OWN, D), BF),
             pltpu.SemaphoreType.DMA((3,)),
-            pltpu.SemaphoreType.DMA((11,)),
-            pltpu.SemaphoreType.DMA((11,)),
-        ],
-        compiler_params=pltpu.CompilerParams(collective_id=2, has_side_effects=True, vmem_limit_bytes=56 << 20),
+        ]
+        + job_scratch(jobs)
+        + sems(11, len(jobs), Scatter),
+        compiler_params=params(collective_id),
         name="mlp_backward",
-    )(g, mid, gain, w, hid, gate, up, prod)
+    )(g, mid, gain, hid, gate, up, prod, *weights, *[by_blocks(job) for job in jobs])
 
 
 def attn_backward_kernel(
-    gm_ref, x_ref, gain_ref, w_ref, hid_ref, q_ref, kv_ref, att_ref, cos_ref, sin_ref,
-    gin_ref, ggain_ref, gbias_ref, dw_ref,
-    low, dkv, kmate, kz, kx, k2, k3, kpair, kpair_got, dqs, dws, dw_got, part, got, send, recv,
+    jobs, gm_ref, x_ref, gain_ref, w_ref, hid_ref, q_ref, kv_ref, att_ref, cos_ref, sin_ref, *refs
 ):
+    srcs = refs[:jobs]
+    gin_ref, ggain_ref, gbias_ref, dw_ref = refs[jobs : jobs + 4]
+    outs = refs[jobs + 4 : 2 * jobs + 4]
+    refs = refs[2 * jobs + 4 :]
+    low, dkv, kmate, kz, kx, k2, k3, kpair, kpair_got, dqs, dws, dw_got, part, got = refs[:14]
+    job_refs = refs[14 : 14 + 6 * jobs]
+    lsem, send, recv = refs[14 + 6 * jobs :]
     me = Place()
-    greet([me.yp(1), me.yp(2), me.yp(3), me.xp(1), me.xp(2), me.xp(3), me.zp(1), me.zp(2), me.zp(3), me.cp()])
+    greet([me.yp(1), me.yp(2), me.yp(3), me.cp()] + xz(me))
     net = Links(send, recv)
+    beside = scatter_jobs(net, me, srcs, outs, job_refs, lsem)
     low[me.y] = gm_ref[...].astype(BF)
-    gathered = [net.go(low.at[me.y], low.at[me.y], me.yp(k)) for k in ORDER]
+    spread_out = [net.go(low.at[me.y], low.at[me.y], me.yp(k)) for k in ORDER]
+    beside.step()
     cos, sin = twice(cos_ref[...]), twice(sin_ref[...])
-    landed(gathered)
+    landed(spread_out)
     grad_mid = low[...].reshape(2 * TOK, D)
     grad_att = dot(grad_mid, w_ref[1, :, :384]).astype(BF)
     for m in range(2):
@@ -419,6 +713,7 @@
         for h in range(HEADS):
             dqs[rows, h * HD : (h + 1) * HD] = dq[h * TOK : (h + 1) * TOK]
     swap = net.go(dkv.at[1 - me.c], kmate, me.cp())
+    beside.step()
     dq_low = jnp.concatenate(
         [turned_back(dqs[:, h * HD : (h + 1) * HD], cos, sin).astype(BF) for h in range(HEADS)], axis=1
     )
@@ -430,6 +725,7 @@
     dws[0, :, :384] = dot(hidden, dq_low, 0, 0).astype(BF)
     dws[1, :, :384] = dot(grad_mid, att_ref[...], 0, 0).astype(BF)
     dws[1, :, 384:] = jnp.zeros((D, HD), BF)
+    beside.step()
     landed(first0)
     total0 = kmate[0, me.z].astype(F32)
     for k in range(3):
@@ -457,6 +753,7 @@
         (dot(dq_low, w_ref[0, :, :384], 1, 1) + dot(dk_low, w_ref[me.s, :, 384:], 1, 1)).astype(BF).reshape(4, OWN, D)
     )
     back = [net.go(part.at[(me.y + k) % 4], got.at[k - 1], me.yp(k)) for k in ORDER]
+    beside.step()
     dws[0, :, 384:] = dot(hidden, dk_low, 0, 0).astype(BF)
     dw_swap = net.go(dws.at[1 - me.c], dw_got, me.cp())
     gbias_ref[:, :384] = jnp.sum(dq_low.astype(F32), axis=0, keepdims=True)
@@ -469,20 +766,22 @@
     gin_ref[...] = gm_ref[...] + dx
     dw_swap.wait_recv()
     dw_ref[...] = (dws[me.c].astype(F32) + dw_got[...].astype(F32)).astype(BF)
-    left(gathered + [swap] + first0 + first1 + second0 + second1 + [pair] + back + [dw_swap])
-
-
-def attn_backward(gm, x, gain, w, hid, q, kv, att, cos, sin):
+    beside.rest()
+    left(spread_out + [swap] + first0 + first1 + second0 + second1 + [pair] + back + [dw_swap])
+
+
+def attn_backward(gm, x, gain, w, hid, q, kv, att, cos, sin, jobs, collective_id):
     return pl.pallas_call(
-        attn_backward_kernel,
+        functools.partial(attn_backward_kernel, len(jobs)),
         out_shape=(
             jax.ShapeDtypeStruct((OWN, D), F32),
             jax.ShapeDtypeStruct((1, D), F32),
             jax.ShapeDtypeStruct((1, QKW), F32),
             jax.ShapeDtypeStruct((D, QKW), BF),
-        ),
-        in_specs=[VM] * 10,
-        out_specs=(VM,) * 4,
+        )
+        + job_outs(jobs),
+        in_specs=[VM] * 10 + [ANY] * len(jobs),
+        out_specs=(VM,) * (4 + len(jobs)),
         scratch_shapes=[
             pltpu.VMEM((4, OWN, D), BF),
             pltpu.VMEM((2, 2, 4, 4, TOK, 2 * HD), BF),
@@ -498,12 +797,12 @@
             pltpu.VMEM((D, QKW), BF),
             pltpu.VMEM((4, OWN, D), BF),
             pltpu.VMEM((3, OWN, D), BF),
-            pltpu.SemaphoreType.DMA((21,)),
-            pltpu.SemaphoreType.DMA((21,)),
-        ],
-        compiler_params=pltpu.CompilerParams(collective_id=3, has_side_effects=True, vmem_limit_bytes=48 << 20),
+        ]
+        + job_scratch(jobs)
+        + sems(21, len(jobs), Scatter),
+        compiler_params=params(collective_id),
         name="attn_backward",
-    )(gm, x, gain, w, hid, q, kv, att, cos, sin)
+    )(gm, x, gain, w, hid, q, kv, att, cos, sin, *[by_blocks(job) for job in jobs])
 
 
 def quad(me):
@@ -514,96 +813,164 @@
     )
 
 
-def spread_kernel(attn_ref, mlp_ref, attn_out, mlp_out, lsem, send, recv):
+def open_kernel(
+    attn_ref, mlp_ref, tiny_ref, ends_ref,
+    attn_out, mlp_out, tiny_out, ends_out, tiny_all, attn_buf,
+    hsem, lsem, send, recv,
+):
     me = Place()
     peers = quad(me)
-    greet([peer for _, _, peer in peers])
+    greet([peer for _, _, peer in peers] + xz(me))
     net = Links(send, recv)
-    copies = []
-    for src, dst in ((attn_ref, attn_out), (mlp_ref, mlp_out)):
-        for core, section, peer in peers:
-            copies.append(net.go(src.at[section, core], dst.at[me.s, me.c], peer))
-    here = []
-    for i, (src, dst) in enumerate(((attn_ref, attn_out), (mlp_ref, mlp_out))):
-        copy = pltpu.make_async_copy(src.at[me.s, me.c], dst.at[me.s, me.c], lsem.at[i])
-        copy.start()
-        here.append(copy)
-    for copy in here + copies:
-        copy.wait()
-
-
-def spread(attn, mlp):
-    return pl.pallas_call(
-        spread_kernel,
-        out_shape=(jax.ShapeDtypeStruct(attn.shape, BF), jax.ShapeDtypeStruct(mlp.shape, BF)),
-        in_specs=[ANY, ANY],
-        out_specs=(ANY, ANY),
-        scratch_shapes=[
-            pltpu.SemaphoreType.DMA((2,)),
-            pltpu.SemaphoreType.DMA((6,)),
-            pltpu.SemaphoreType.DMA((6,)),
-        ],
-        compiler_params=pltpu.CompilerParams(collective_id=4, has_side_effects=True),
-        name="spread",
-    )(attn, mlp)
-
-
-def gather_back_kernel(attn_ref, mlp_ref, ends_ref, attn_out, mlp_out, ends_out, lsem, send, recv):
-    me = Place()
-    peers = quad(me)
-    far = {"section": me.s, "shard": 1 - me.h}
-    cross = {"section": 1 - me.s, "shard": 1 - me.h}
-    greet([peer for _, _, peer in peers] + [far, cross])
-    net = Links(send, recv)
-    copies = []
-    for src, dst in ((attn_ref, attn_out), (mlp_ref, mlp_out)):
-        for core, section, peer in peers:
-            copies.append(net.go(src.at[section, core], dst.at[me.s, me.c], peer))
-    for k in ORDER:
-        copies.append(net.go(ends_ref.at[((me.y + k) % 4) % 2], ends_out.at[me.y], me.yp(k)))
-    here = []
+    away = pl.ds(pl.multiple_of((1 - me.s) * OWN, OWN), OWN)
+    home = pl.ds(pl.multiple_of(me.s * OWN, OWN), OWN)
+    early, late = [], []
+    for core, section, peer in peers:
+        early.append(net.go(attn_ref.at[section, core], attn_out.at[me.s, me.c], peer))
+        early.append(net.go(tiny_ref, tiny_out.at[me.s, me.c], peer))
+    late.append(net.go(ends_ref.at[me.h, away], ends_out.at[me.s], {"section": 1 - me.s}))
+    for core, section, peer in peers:
+        late.append(net.go(mlp_ref.at[section, core], mlp_out.at[me.s, me.c], peer))
     pairs = (
         (attn_ref.at[me.s, me.c], attn_out.at[me.s, me.c]),
+        (tiny_ref, tiny_out.at[me.s, me.c]),
+        (ends_ref.at[me.h, home], ends_out.at[me.s]),
         (mlp_ref.at[me.s, me.c], mlp_out.at[me.s, me.c]),
-        (ends_ref.at[me.s], ends_out.at[me.y]),
-    )
+    )
+    here = []
     for i, (src, dst) in enumerate(pairs):
-        copy = pltpu.make_async_copy(src, dst, lsem.at[i])
-        copy.start()
-        here.append(copy)
-    for copy in here + copies:
-        copy.wait()
-
-
-def gather_back(attn, mlp, ends):
+        here.append(pltpu.make_async_copy(src, dst, hsem.at[i]))
+        here[-1].start()
+    here[0].wait()
+    here[1].wait()
+    landed(early)
+    here.append(pltpu.make_async_copy(tiny_out, tiny_all.at[me.z, me.x], hsem.at[4]))
+    here[4].start()
+    one = [net.go(tiny_out, tiny_all.at[me.z, me.x], me.xp(k)) for k in ORDER]
+    attn = Gather(net, me, attn_out.at[0], attn_buf, lsem.at[0])
+    attn.start()
+    here[4].wait()
+    landed(one)
+    two = [net.go(tiny_all.at[me.z], tiny_all.at[me.z], me.zp(k)) for k in ORDER]
+    attn.second()
+    attn.third()
+    attn.fourth()
+    attn.finish()
+    landed(two)
+    here[2].wait()
+    here[3].wait()
+    landed(late)
+    left(early + late + one + two)
+
+
+def open_up(attn, mlp, tiny, ends):
     return pl.pallas_call(
-        gather_back_kernel,
+        open_kernel,
         out_shape=(
             jax.ShapeDtypeStruct(attn.shape, BF),
             jax.ShapeDtypeStruct(mlp.shape, BF),
+            jax.ShapeDtypeStruct((2, 2) + tiny.shape, BF),
+            jax.ShapeDtypeStruct((2, OWN, D), F32),
+            jax.ShapeDtypeStruct((4, 4, 2, 2) + tiny.shape, BF),
+            jax.ShapeDtypeStruct((4, 4) + attn.shape[1:], BF),
+        ),
+        in_specs=[ANY] * 4,
+        out_specs=(ANY,) * 6,
+        scratch_shapes=[pltpu.SemaphoreType.DMA((5,))] + sems(16, 1, Gather),
+        compiler_params=params(8),
+        name="open_up",
+    )(attn, mlp, tiny, ends)
+
+
+def deposit_kernel(
+    a0, a1, d0, d1, gu0, gu1, small, ends,
+    attn_out, gu_out, d_out, small_out, ends_out,
+    *scratch,
+):
+    me = Place()
+    peers = quad(me)
+    greet([me.yp(1), me.yp(2), me.yp(3), me.cp(), peers[2][2]] + xz(me))
+    res_a, res_gu, res_d, sum_c, sum_got, hsem, lsem, send, recv = scratch[12:]
+    net = Links(send, recv)
+    beside = scatter_jobs(net, me, (d0, a0), (res_d.at[0], res_a.at[0]), scratch[:12], lsem)
+    beside.step()
+    here = []
+    for i, (src, dst) in enumerate(
+        ((gu0, res_gu.at[0]), (gu1, res_gu.at[1]), (d1, res_d.at[1]), (a1, res_a.at[1]), (ends.at[me.s], ends_out.at[me.y]))
+    ):
+        here.append(pltpu.make_async_copy(src, dst, hsem.at[i]))
+        here[-1].start()
+    copies = []
+    sum_c[0] = small[...]
+    rounds = ((me.yp, ORDER), (lambda k: me.cp(), (1,)), (me.xp, ORDER), (me.zp, ORDER))
+
+    def small_round(turn, slot):
+        peer, ks = rounds[turn]
+        sent = [net.go(sum_c.at[turn], sum_got.at[slot + k - 1], peer(k)) for k in ks]
+        copies.extend(sent)
+        landed(sent)
+        total = sum_c[turn]
+        for k in ks:
+            total = total + sum_got[slot + k - 1]
+        sum_c[turn + 1] = total
+
+    small_round(0, 0)
+    small_round(1, 3)
+    last = [net.go(ends.at[((me.y + k) % 4) % 2], ends_out.at[me.y], me.yp(k)) for k in ORDER]
+
+    def go_home(res, out, sem):
+        for core, section, peer in peers:
+            last.append(net.go(res.at[section, core], out.at[me.s, me.c], peer))
+        here.append(pltpu.make_async_copy(res.at[me.s, me.c], out.at[me.s, me.c], hsem.at[sem]))
+        here[-1].start()
+
+    here[0].wait()
+    here[1].wait()
+    go_home(res_gu, gu_out, 5)
+    beside.step()
+    small_round(2, 4)
+    small_round(3, 7)
+    beside.step()
+    beside.step()
+    beside.step()
+    here[2].wait()
+    here[3].wait()
+    go_home(res_d, d_out, 6)
+    go_home(res_a, attn_out, 7)
+    small_out[...] = sum_c[4]
+    for copy in here[4:]:
+        copy.wait()
+    landed(last)
+    left(copies + last)
+    beside.rest()
+
+
+def deposit(a0, a1, d0, d1, gu0, gu1, small, ends):
+    rows = a1.shape[1]
+    return pl.pallas_call(
+        deposit_kernel,
+        out_shape=(
+            jax.ShapeDtypeStruct((2,) + a1.shape, BF),
+            jax.ShapeDtypeStruct((2,) + gu1.shape, BF),
+            jax.ShapeDtypeStruct((2,) + d1.shape, BF),
+            jax.ShapeDtypeStruct(small.shape, F32),
             jax.ShapeDtypeStruct((4, OWN, D), F32),
         ),
-        in_specs=[ANY] * 3,
-        out_specs=(ANY,) * 3,
-        scratch_shapes=[
-            pltpu.SemaphoreType.DMA((3,)),
-            pltpu.SemaphoreType.DMA((9,)),
-            pltpu.SemaphoreType.DMA((9,)),
-        ],
-        compiler_params=pltpu.CompilerParams(collective_id=5, has_side_effects=True),
-        name="gather_back",
-    )(attn, mlp, ends)
-
-
-SAME_CORE = [[core + 2 * chip for chip in range(16)] for core in range(2)]
-
-
-def all_rows(block):
-    return lax.all_gather(block, "ctx", axis=0, tiled=True, axis_index_groups=SAME_CORE)
-
-
-def own_rows(block):
-    return lax.psum_scatter(block, "ctx", scatter_dimension=0, tiled=True, axis_index_groups=SAME_CORE)
+        in_specs=[ANY] * 6 + [VM, ANY],
+        out_specs=(ANY, ANY, ANY, VM, ANY),
+        scratch_shapes=job_scratch((d0, a0))
+        + [
+            pltpu.VMEM((2,) + a1.shape, BF),
+            pltpu.VMEM((2,) + gu1.shape, BF),
+            pltpu.VMEM((2,) + d1.shape, BF),
+            pltpu.VMEM((5,) + small.shape, F32),
+            pltpu.VMEM((10,) + small.shape, F32),
+            pltpu.SemaphoreType.DMA((8,)),
+        ]
+        + sems(22, 2, Scatter),
+        compiler_params=params(9),
+        name="deposit",
+    )(by_blocks(a0), a1, by_blocks(d0), d1, gu0, gu1, small, ends)
 
 
 def unit_slices(w):
@@ -614,12 +981,6 @@
 def body(ends, w_query, w_kv, w_out, w_gate_up, w_down, gains, bias_query, bias_kv):
     me = Place()
     rows = w_query.shape[1]
-    mine = lax.dynamic_slice(ends[0], (me.h, me.s * OWN, 0), (1, OWN, D))[0]
-    other = lax.dynamic_slice(ends[0], (me.h, (1 - me.s) * OWN, 0), (1, OWN, D))[0]
-    crossed = lax.ppermute(other, "section", [(0, 1), (1, 0)])
-    x = jnp.where(me.s == 0, mine, crossed)
-    cotangent = jnp.where(me.s == 0, crossed, mine)
-
     wq = w_query[0].reshape(rows, 2, 384)
     wo = w_out[0].reshape(rows, 2, 384)
     attn_pieces = jnp.stack(
@@ -636,19 +997,14 @@
     mlp_pieces = jnp.concatenate(
         [unit_slices(w_gate_up[0, :, 0]), unit_slices(w_gate_up[0, :, 1]), unit_slices(w_down[0])], axis=3
     )
-    attn_rows, mlp_rows = spread(attn_pieces, mlp_pieces)
-    attn_w = [None, None]
-    mlp_w = [None, None]
-    for l in range(2):
-        attn_w[l] = all_rows(attn_rows[l].reshape(2 * rows, QKW))
-        mlp_w[l] = all_rows(mlp_rows[l].reshape(2 * rows, 3 * UNITS))
-
     packed = jnp.concatenate([gains[0].reshape(-1), bias_query[0].reshape(-1), bias_kv[0].reshape(-1)])[None]
-    everything = lax.all_gather(packed, ("section", "ctx", "shard"), axis=0, tiled=True).astype(F32)
-    everything = everything.reshape(2, 32, 2, 128)
-    gain_all = everything[:, :, 0, :96].reshape(2, 32, 2, 48).transpose(0, 2, 1, 3).reshape(2, 2, 1, D)
-    bias_all = everything[:, :, :, 96:].reshape(2, 32, 2, 8, 4).transpose(2, 0, 3, 1, 4).reshape(2, 2, 8, 128)
-    bias_here = lax.dynamic_index_in_dim(bias_all, me.h, 0, keepdims=False)
+    attn_rows, mlp_rows, _, tokens, tiny_all, attn_w0 = open_up(
+        attn_pieces, mlp_pieces, jnp.pad(packed, ((0, 15), (0, 0))), ends[0]
+    )
+
+    everything = tiny_all[:, :, :, :, 0].reshape(16, 2, 2, 128).astype(F32)
+    gain_all = everything[..., :96].reshape(16, 2, 2, 2, 48).transpose(1, 3, 0, 2, 4).reshape(2, 2, 1, D)
+    bias_here = everything[..., 96:].reshape(16, 2, 2, 8, 4).transpose(1, 3, 0, 2, 4).reshape(2, 8, 128)
     bias_q = lax.dynamic_slice(bias_here, (0, me.s * HEADS, 0), (2, HEADS, 128)).reshape(2, 1, 384)
     bias = jnp.concatenate([bias_q, bias_here[:, 6:8].reshape(2, 1, 256)], axis=2)
 
@@ -658,30 +1014,47 @@
     cos = jnp.concatenate([jnp.cos(angles), jnp.cos(angles)], axis=1)
     sin = jnp.concatenate([-jnp.sin(angles), jnp.sin(angles)], axis=1)
 
-    inputs, kept = [], []
-    for l in range(2):
-        inputs.append(x)
-        mid, hid, q, kv, att, wf = attn_forward(x, gain_all[l, 0], attn_w[l], bias[l], cos, sin)
-        out, hid2, gate, up, prod = mlp_forward(mid, gain_all[l, 1], mlp_w[l])
-        kept.append((mid, hid, q, kv, att, wf, hid2, gate, up, prod))
-        x = out.astype(BF).astype(F32)
-
-    g = cotangent
-    attn_g, mlp_g, gain_g, bias_g = [None, None], [None, None], [None, None], [None, None]
-    for l in (1, 0):
-        mid, hid, q, kv, att, wf, hid2, gate, up, prod = kept[l]
-        gmid, ggain1, dw_mlp = mlp_backward(g, mid, gain_all[l, 1], mlp_w[l], hid2, gate, up, prod)
-        mlp_g[l] = own_rows(dw_mlp)
-        gin, ggain0, gbias, dw_attn = attn_backward(gmid, inputs[l], gain_all[l, 0], wf, hid, q, kv, att, cos, sin)
-        attn_g[l] = own_rows(dw_attn)
-        gain_g[l] = jnp.concatenate([ggain0, ggain1], axis=0)
-        bias_g[l] = gbias
-        g = gin.astype(BF).astype(F32) if l == 1 else gin
+    def whole(blocks):
+        return blocks.reshape(D, -1)
+
+    gate, up_down, every = slice(0, UNITS), slice(UNITS, 3 * UNITS), slice(0, 3 * UNITS)
+    x0 = tokens[0]
+    mid0, hid, q, kv, att, wf, mlp_w0 = attn_forward(
+        x0, gain_all[0, 0], whole(attn_w0), bias[0], cos, sin, mlp_rows, [(0, every)], 0
+    )
+    kept0 = (hid, q, kv, att)
+    wf0 = wf
+    mlp_w0 = [whole(mlp_w0)]
+    out, *mlp0, attn_w1, gate_w1 = mlp_forward(
+        mid0, gain_all[0, 1], mlp_w0, [attn_rows, mlp_rows], [(1, slice(0, QKW)), (1, gate)], 1
+    )
+    x1 = out.astype(BF).astype(F32)
+    mid1, hid, q, kv, att, wf, up_down_w1 = attn_forward(
+        x1, gain_all[1, 0], whole(attn_w1), bias[1], cos, sin, mlp_rows, [(1, up_down)], 2
+    )
+    kept1 = (hid, q, kv, att)
+    mlp_w1 = [whole(gate_w1), whole(up_down_w1)]
+    out, *mlp1 = mlp_forward(mid1, gain_all[1, 1], mlp_w1, [], [], 3)
+
+    gmid, ggain11, dgu1, dd1 = mlp_backward(tokens[1], mid1, gain_all[1, 1], mlp_w1, *mlp1, [], 4)
+    gin, ggain10, gbias1, da1, dgu1 = attn_backward(
+        gmid, x1, gain_all[1, 0], wf, *kept1, cos, sin, [dgu1], 5
+    )
+    g = gin.astype(BF).astype(F32)
+    gmid, ggain01, dgu0, dd0, dd1, da1 = mlp_backward(g, mid0, gain_all[0, 1], mlp_w0, *mlp0, [dd1, da1], 6)
+    gin, ggain00, gbias0, da0, dgu0 = attn_backward(
+        gmid, x0, gain_all[0, 0], wf0, *kept0, cos, sin, [dgu0], 7
+    )
+    bias_g = [gbias0, gbias1]
+    gain_g = [ggain00, ggain01, ggain10, ggain11]
 
     small = jnp.stack(bias_g)
     small = jnp.where(jnp.arange(4)[None, :, None] == me.y, small, 0.0)
     small = jnp.concatenate([jnp.stack(gain_g).reshape(-1), small.reshape(-1)]).reshape(-1, 128)
-    small = lax.psum(small, ("section", "ctx", "shard")).reshape(-1)
+    attn_home, gu_home, d_home, small, boundary = deposit(
+        da0, da1, dd0, dd1, dgu0, dgu1, small, jnp.stack([gin, out])
+    )
+    small = small.reshape(-1)
     gain_sum = small[: 4 * D].reshape(2, 2, 32, 48)
     bias_sum = small[4 * D :].reshape(2, 2, 2, 4, 32, 4)
     gain_sum = lax.dynamic_index_in_dim(gain_sum, me.s, 0, keepdims=False)
@@ -690,21 +1063,16 @@
     bias_sum = lax.dynamic_index_in_dim(bias_sum, me.h, 0, keepdims=False)
     bias_sum = lax.dynamic_index_in_dim(bias_sum, me.ctx, 2, keepdims=False)
 
-    attn_home, mlp_home, boundary = gather_back(
-        jnp.stack(attn_g).reshape(2, 2, rows, QKW),
-        jnp.stack(mlp_g).reshape(2, 2, rows, 3 * UNITS),
-        jnp.stack([g, out]),
-    )
     attn_home = attn_home.astype(F32)
-    mlp_home = mlp_home.astype(F32).reshape(2, 2, rows, 3, UNITS).transpose(2, 3, 0, 1, 4).reshape(rows, 3, 4 * UNITS)
-    mlp_home = mlp_home[:, :, : w_down.shape[2]]
+    gu_home = gu_home.astype(F32).reshape(2, 2, rows, 2, UNITS).transpose(2, 3, 0, 1, 4).reshape(rows, 2, 4 * UNITS)
+    d_home = d_home.astype(F32).transpose(2, 0, 1, 3).reshape(rows, 4 * UNITS)
     return (
         boundary.reshape(1, 2, TOK, D),
         attn_home[:, 0, :, :384].transpose(1, 0, 2).reshape(1, rows, 768),
         attn_home[:, 0, :, 384:].transpose(1, 0, 2)[None],
         attn_home[:, 1, :, :384].transpose(1, 0, 2).reshape(1, rows, 768),
-        mlp_home[:, :2][None],
-        mlp_home[:, 2][None],
+        gu_home[:, :, : w_down.shape[2]][None],
+        d_home[:, : w_down.shape[2]][None],
         gain_sum[None],
         bias_sum[:, :HEADS].reshape(1, 6, 4),
         bias_sum[:, HEADS].reshape(1, 2, 1, 4),

time: 1020 us -> 510 us (0.50)
  blocking collectives: 377 us -> 0 us
  waiting for transfers between devices: 265 us -> 0 us
  Pallas kernels: 294 us -> 468 us
  local copies, waits for them, and re-layouts: 54.7 us -> 20.6 us
  between operations: 15.1 us -> 1.4 us
    all_gather x1 -> x0, blocking collectives: 313 us -> none  [body(): lax.all_gather(packed, ('section', 'ctx', 'shard'), axis=0, tiled=True)]
    reduce_scatter x4 -> x0, waiting for transfers between devices: 262 us -> none  [own_rows(): lax.psum_scatter(block, 'ctx', scatter_dimension=0, tiled=True, axis_inde...]
    pallas_call x10, Pallas kernels: 294 us -> 468 us  [the longest x2 122 us: attn_forward(): pl.pallas_call(functools.partial(attn_forward_kernel, views), out_shape=(...]
    psum x1 -> x0, blocking collectives: 64 us -> none  [body(): small = lax.psum(small, ('section', 'ctx', 'shard')).reshape(-1)]
    unnamed x99 -> x36, local copies, waits for them, and re-layouts: 25.1 us -> 2.99 us
  transfers between devices with their start and end apart: 9 -> 0, of which waited for: 4 -> 0; matrix products, arithmetic and copies ran while one was open for 1% -> 0% of each run, Pallas kernels for 9% -> 0%
where the time goes in v3:
time: 510 us; the launch traced here: 503 us
  Pallas kernels  468 us (92%)
  local copies, waits for them, and re-layouts  20.6 us (4%)
  other arithmetic  13.7 us (3%)
    pallas_call x2, Pallas kernels, attn_forward(): pl.pallas_call(functools.partial(attn_forward_kernel, views), out_shape=(...  122 us
    pallas_call x2, Pallas kernels, attn_backward(): pl.pallas_call(functools.partial(attn_backward_kernel, len(jobs)), out_sh...  117 us
    pallas_call x2, Pallas kernels, mlp_backward(): pl.pallas_call(functools.partial(mlp_backward_kernel, len(weights), len(j...  75.2 us
    pallas_call x2, Pallas kernels, mlp_forward(): pl.pallas_call(functools.partial(mlp_forward_kernel, len(weights), views)...  64.1 us
    pallas_call x1, Pallas kernels, deposit(): pl.pallas_call(deposit_kernel, out_shape=(jax.ShapeDtypeStruct((2,) + a1....  51.1 us
    pallas_call x1, Pallas kernels, open_up(): pl.pallas_call(open_kernel, out_shape=(jax.ShapeDtypeStruct(attn.shape, B...  38.4 us

profile of v3, /device:TPU:1, one launch (start us, length us, event | category | flops | bytes accessed | tf_op | source)
XLA Modules:
  0.0 503.4 jit_solution(3959378396997094082)
XLA Ops:
  0.7 1.0 reshape_squeeze.19
  1.8 0.9 fusion.10
  2.7 0.9 reshape_squeeze.20
  3.8 0.7 pad_maximum_fusion.2.attn_ref
  4.5 1.2 fusion.7
  5.7 0.1 copy_bitcast_fusion.3
  6.2 0.6 copy-done.3
  7.1 1.2 pad_maximum_fusion.mlp_ref
  8.7 0.6 pad.17.tiny_ref
  9.3 38.4 %open_up.1 = (bf16[2,2,48,512]{3,2,1,0:T(8,128)(2,1)}, bf16[2,2,48,3456]{3,2,1,0:T(8,128)(2,1)}, bf16[2,2,16,128]{3,2,1,0:T(8,128)(2,1)}, f32[2,32,1536]{2,1,0:T...) custom-call(bf16[2,2,48,512]{3,2,1,0:T(8,128)(2,1)} %pad_maximum_fusion.2.attn_ref, ...), custom_call_target="tpu_custom_call" | custom-call | tf_op jit(solution)/shard_map/open_up/pallas_call | solution.py:867
  47.8 0.9 slice_convert_fusion
  48.9 0.1 copy.65
  49.4 0.6 slice_bitcast_fusion.11
  50.2 0.1 reshape.153
  50.4 0.6 slice_bitcast_fusion.7
  51.0 1.8 slice_bitcast_fusion.2
  52.8 0.2 fusion.6
  53.0 0.7 pad_maximum_fusion.7
  53.7 67.7 %attn_forward.2 = (f32[32,1536]{1,0:T(8,128)}, bf16[4,32,1536]{2,1,0:T(8,128)(2,1)}, bf16[2,3,64,128]{3,2,1,0:T(8,128)(2,1)}, bf16[2,2,4,4,64,256]{5,4,3,2,1,0:T...) custom-call(f32[32,1536]{1,0:T(8,128)} %get-tuple-element.152.x_ref, ...), custom_call_target="tpu_custom_call" | custom-call | tf_op jit(solution)/shard_map/attn_forward/pallas_call | solution.py:442
  121.4 40.9 %mlp_forward.2 = (f32[32,1536]{1,0:T(8,128)}, bf16[2,4,32,1536]{3,2,1,0:T(8,128)(2,1)}, f32[256,1152]{1,0:T(8,128)}, f32[256,1152]{1,0:T(8,128)}, bf16[256,1152]...) custom-call(f32[32,1536]{1,0:T(8,128)} %get-tuple-element.69.mid_ref, ...), custom_call_target="tpu_custom_call" | custom-call | tf_op jit(solution)/shard_map/mlp_forward/pallas_call | solution.py:551
  162.3 1.6 convert_convert_fusion.1.x_ref
  163.9 53.9 %attn_forward.3 = (f32[32,1536]{1,0:T(8,128)}, bf16[4,32,1536]{2,1,0:T(8,128)(2,1)}, bf16[2,3,64,128]{3,2,1,0:T(8,128)(2,1)}, bf16[2,2,4,4,64,256]{5,4,3,2,1,0:T...) custom-call(f32[32,1536]{1,0:T(8,128)} %convert_convert_fusion.1.x_ref, ...), custom_call_target="tpu_custom_call" | custom-call | tf_op jit(solution)/shard_map/attn_forward/pallas_call | solution.py:442
  217.8 23.2 %mlp_forward.3 = (f32[32,1536]{1,0:T(8,128)}, bf16[2,4,32,1536]{3,2,1,0:T(8,128)(2,1)}, f32[256,1152]{1,0:T(8,128)}, f32[256,1152]{1,0:T(8,128)}, bf16[256,1152]{1,0:T(8,128)(2,1)}) custom-call(f32[32,1536]{1,0:T(8,128)} %get-tuple-element.74.mid_ref, f32[1,1536]{1,0:T(1,128)} %get-tuple-element.158.gain_ref, bf16[1536,1152]{1,0:T(8,128)(2,1)} %bitcast.139, ...), custom_call_target="tpu_custom_call" | custom-call | tf_op jit(solution)/shard_map/mlp_forward/pallas_call | solution.py:551
  241.1 28.3 %mlp_backward.2 = (f32[32,1536]{1,0:T(8,128)}, f32[1,1536]{1,0:T(1,128)}, bf16[1536,2304]{1,0:T(8,128)(2,1)}, bf16[1536,1152]{1,0:T(8,128)(2,1)}) custom-call(f32[32,1536]{1,0:T(8,128)} %get-tuple-element.153.g_ref, f32[32,1536]{1,0:T(8,128)} %get-tuple-element.74.mid_ref, f32[1,1536]{1,0:T(1,128)} %get-tuple-element.158.gain_ref, ...), custom_call_target="tpu_custom_call" | custom-call | tf_op jit(solution)/shard_map/mlp_backward/pallas_call | solution.py:647
  269.4 58.2 %attn_backward.2 = (f32[32,1536]{1,0:T(8,128)}, f32[1,1536]{1,0:T(1,128)}, f32[1,512]{1,0:T(1,128)}, bf16[1536,512]{1,0:T(8,128)(2,1)}, bf16[2,48,2304]{2,1,0:T(8,128)(2,1)}) custom-call(f32[32,1536]{1,0:T(8,128)} %get-tuple-element.81.gm_ref, f32[32,1536]{1,0:T(8,128)} %convert_convert_fusion.1.x_ref, f32[1,1536]{1,0:T(1,128)} %get-tuple-element.159.gain_ref, ...), custom_call_target="tpu_custom_call" | custom-call | tf_op jit(solution)/shard_map/attn_backward/pallas_call | solution.py:774
  327.6 1.6 convert_convert_fusion.g_ref
  329.2 46.9 %mlp_backward.3 = (f32[32,1536]{1,0:T(8,128)}, f32[1,1536]{1,0:T(1,128)}, bf16[1536,2304]{1,0:T(8,128)(2,1)}, bf16[1536,1152]{1,0:T(8,128)(2,1)}, bf16[2,48,1152...) custom-call(f32[32,1536]{1,0:T(8,128)} %convert_convert_fusion.g_ref, f32[32,1536]{1,0:T(8,128)} %get-tuple-element.69.mid_ref, ...), custom_call_target="tpu_custom_call" | custom-call | tf_op jit(solution)/shard_map/mlp_backward/pallas_call | solution.py:647
  376.2 59.1 %attn_backward.3 = (f32[32,1536]{1,0:T(8,128)}, f32[1,1536]{1,0:T(1,128)}, f32[1,512]{1,0:T(1,128)}, bf16[1536,512]{1,0:T(8,128)(2,1)}, bf16[2,48,2304]{2,1,0:T(8,128)(2,1)}) custom-call(f32[32,1536]{1,0:T(8,128)} %get-tuple-element.95.gm_ref, f32[32,1536]{1,0:T(8,128)} %get-tuple-element.152.x_ref, f32[1,1536]{1,0:T(1,128)} %get-tuple-element.161.gain_ref, ...), custom_call_target="tpu_custom_call" | custom-call | tf_op jit(solution)/shard_map/attn_backward/pallas_call | solution.py:774
  435.2 1.7 pad_maximum_fusion.1.ends
  436.9 0.7 pad_maximum_fusion.9
  437.7 0.7 maximum_bitcast_fusion.3
  438.5 0.6 maximum_bitcast_fusion.2.small
  439.1 51.1 %deposit.1 = (bf16[2,2,48,512]{3,2,1,0:T(8,128)(2,1)}, bf16[2,2,48,2304]{3,2,1,0:T(8,128)(2,1)}, bf16[2,2,48,1152]{3,2,1,0:T(8,128)(2,1)}, f32[80,128]{1,0:T(8,128)}, f32[4,32,1536]{2,1,0:T(8,128)}) custom-call(bf16[4,4,2,48,512]{4,3,2,1,0:T(8,128)(2,1)} %bitcast.151, bf16[2,48,512]{2,1,0:T(8,128)(2,1)} %get-tuple-element.103.a1, ...), custom_call_target="tpu_custom_call" | custom-call | tf_op jit(solution)/shard_map/deposit/pallas_call | solution.py:950
  490.2 2.4 reshape.174
  492.7 0.7 copy.70
  493.4 0.6 reshape.175
  493.9 1.8 fusion
  495.7 0.3 copy.71
  496.1 0.3 reshape.176
  496.4 1.0 fusion.1
  497.5 0.8 reshape.172
  498.4 0.8 reshape.173
  499.1 0.5 reshape.178
  499.7 0.7 copy.76
  500.4 0.6 slice_bitcast_fusion.13
  501.0 0.6 copy.74
  501.7 0.6 constant_dynamic-slice_fusion.1
  502.3 0.9 copy.105
  (78 shorter events, 2.5 us)
Async XLA Ops:
  0.6 3.8 copy-start
  5.8 1.0 copy-start.3
  6.9 1.4 copy-start.11
  6.9 1.5 copy-start.12
  6.9 1.6 copy-start.13
  376.1 59.1 %copy-start.4 = (f32[32,1536]{1,0:T(8,128)S(1)}, f32[32,1536]{1,0:T(8,128)}, u32[]{:S(2)}) copy-start(f32[32,1536]{1,0:T(8,128)} %get-tuple-element.115) | copy-start | bytes 589828
  376.1 60.8 %copy-start.7 = (f32[1,1536]{1,0:T(1,128)S(1)}, f32[1,1536]{1,0:T(1,128)}, u32[]{:S(2)}) copy-start(f32[1,1536]{1,0:T(1,128)} %get-tuple-element.111) | copy-start | bytes 18436
  376.1 60.8 %copy-start.8 = (f32[1,1536]{1,0:T(1,128)S(1)}, f32[1,1536]{1,0:T(1,128)}, u32[]{:S(2)}) copy-start(f32[1,1536]{1,0:T(1,128)} %get-tuple-element.110) | copy-start | bytes 18436
  376.1 60.8 %copy-start.9 = (f32[1,1536]{1,0:T(1,128)S(1)}, f32[1,1536]{1,0:T(1,128)}, u32[]{:S(2)}) copy-start(f32[1,1536]{1,0:T(1,128)} %get-tuple-element.109) | copy-start | bytes 18436
  376.1 61.5 %copy-start.10 = (f32[1,512]{1,0:T(1,128)S(1)}, f32[1,512]{1,0:T(1,128)}, u32[]{:S(2)}) copy-start(f32[1,512]{1,0:T(1,128)} %get-tuple-element.113) | copy-start | bytes 6148
  493.3 2.4 copy-start.2
  495.7 1.6 copy-start.5
  496.1 3.1 copy-start.6
  496.4 5.9 %copy-start.1 = (f32[4,32,1536]{2,1,0:T(8,128)S(1)}, f32[4,32,1536]{2,1,0:T(8,128)}, u32[]{:S(2)}) copy-start(f32[4,32,1536]{2,1,0:T(8,128)} %get-tuple-element.116) | copy-start | bytes 2359300

commit v4 on v1

v4 whole, which is shorter than its diff:
```python
import functools
import types

import jax
import jax.numpy as jnp
from jax import lax
from jax.experimental import pallas as pl
from jax.experimental.pallas import tpu as pltpu
from jax.sharding import PartitionSpec as P

MESH = pl.DeviceIdType.MESH
BF = jnp.bfloat16
F32 = jnp.float32
EPS = 1e-06
THETA = 1000000.0
D = 1536
HD = 128
HEADS = 3
UNITS = 1152
CHUNK = 384
TOK = 64
OWN = 32
ROWS = 48
QKW = 512
ORDER = (1, 3, 2)
SIDES = (1, 3)


class Place:
    def __init__(self):
        self.ctx = lax.axis_index("ctx")
        self.s = lax.axis_index("section")
        self.h = lax.axis_index("shard")
        self.z = self.ctx // 8
        self.x = (self.ctx // 2) % 4
        self.c = self.ctx % 2
        self.y = self.h * 2 + self.s

    def yp(self, k):
        other = (self.y + k) % 4
        return {"section": other % 2, "shard": other // 2}

    def xp(self, k):
        return {"ctx": self.z * 8 + ((self.x + k) % 4) * 2 + self.c}

    def zp(self, k):
        return {"ctx": (self.ctx + 8 * k) % 32}

    def cp(self):
        return {"ctx": self.ctx + 1 - 2 * self.c}

    def quad(self):
        return (
            (self.c, 1 - self.s, {"section": 1 - self.s}),
            (1 - self.c, self.s, self.cp()),
            (1 - self.c, 1 - self.s, {"section": 1 - self.s, "ctx": self.ctx + 1 - 2 * self.c}),
        )

    def greet(self):
        peers = [self.yp(k) for k in ORDER] + [self.cp(), self.quad()[2][2]]
        peers += [self.xp(k) for k in ORDER] + [self.zp(k) for k in ORDER]
        barrier = pltpu.get_barrier_semaphore()
        for peer in peers:
            pl.semaphore_signal(barrier, 1, device_id=peer, device_id_type=MESH)
        pl.semaphore_wait(barrier, len(peers))


class Links:
    def __init__(self, send, recv):
        self.send, self.recv, self.count = send, recv, 0
        self.free = list(range(send.shape[0]))

    def go(self, src, dst, peer):
        index = self.count
        self.count += 1
        slot = self.free.pop(0)
        copy = pltpu.make_async_remote_copy(
            src, dst, self.send.at[slot], self.recv.at[index], device_id=peer, device_id_type=MESH
        )
        copy.start()
        return copy, slot

    def left(self, copies):
        for copy, slot in copies:
            copy.wait_send()
            self.free.append(slot)


def landed(copies):
    for copy, _ in copies:
        copy.wait_recv()


class Local:
    def __init__(self, sems):
        self.sems, self.count = sems, 0

    def go(self, src, dst):
        copy = pltpu.make_async_copy(src, dst, self.sems.at[self.count])
        self.count += 1
        copy.start()
        return copy


def cuts(columns):
    cut = (columns // 256) * 128
    return (slice(0, cut), slice(cut, columns))


class Gather:
    copies = 40

    def __init__(self, me, net, local, src, buf, ready=()):
        self.me, self.net, self.local, self.src, self.buf, self.ready = me, net, local, src, buf, ready
        self.cuts = cuts(src.shape[-1])
        self.sent = []

    def steps(self):
        return [self.start, self.second, self.third, self.fourth, self.finish]

    def at(self, half, p, q):
        return self.buf.at[q, p, 0] if half == 0 else self.buf.at[p, q, 1]

    def axes(self, half):
        me = self.me
        return (me.x, me.z, me.xp, me.zp) if half == 0 else (me.z, me.x, me.zp, me.xp)

    def go(self, src, dst, peer):
        copy = self.net.go(src, dst, peer)
        self.sent.append(copy)
        return copy

    def start(self):
        me = self.me
        for wait in self.ready:
            wait()
        self.own = self.local.go(self.src, self.buf.at[me.z, me.x])
        self.a, self.c = [None, None], [[None] * 4, [None] * 4]
        for half in range(2):
            p, q, pp, qp = self.axes(half)
            self.a[half] = [self.go(self.src.at[half], self.at(half, p, q), pp(k)) for k in SIDES]
        for half in range(2):
            p, q, pp, qp = self.axes(half)
            self.c[half][0] = [self.go(self.src.at[half], self.at(half, p, q), qp(k)) for k in SIDES]

    def second(self):
        self.f = [[], []]
        for half in range(2):
            p, q, pp, qp = self.axes(half)
            for i, k in enumerate(SIDES):
                landed([self.a[half][i]])
                piece = self.at(half, (p + 4 - k) % 4, q).at[:, self.cuts[i]]
                self.f[half].append(self.go(piece, piece, pp(k)))
        for half in range(2):
            p, q, pp, qp = self.axes(half)
            for i, k in enumerate(SIDES):
                block = self.at(half, (p + 4 - k) % 4, q)
                self.c[half][i + 1] = [self.go(block, block, qp(kk)) for kk in SIDES]

    def third(self):
        for half in range(2):
            p, q, pp, qp = self.axes(half)
            landed(self.f[half])
            block = self.at(half, (p + 2) % 4, q)
            self.c[half][3] = [self.go(block, block, qp(kk)) for kk in SIDES]
        self.last = []
        self.onward((0,))

    def fourth(self):
        self.onward((1, 2, 3))

    def onward(self, turns):
        for j in turns:
            shift = (0, 3, 1, 2)[j]
            for half in range(2):
                p, q, pp, qp = self.axes(half)
                for i, k in enumerate(SIDES):
                    landed([self.c[half][j][i]])
                    piece = self.at(half, (p + shift) % 4, (q + 4 - k) % 4).at[:, self.cuts[i]]
                    self.last.append(self.go(piece, piece, qp(k)))

    def finish(self):
        landed(self.last)
        self.own.wait()
        self.net.left(self.sent)


class Scatter:
    copies = 16

    def __init__(self, me, net, part, scratch, out, then=None):
        self.me, self.net, self.part, self.out, self.then = me, net, part, out, then
        self.r1, self.r2, self.u1, self.u2 = scratch
        self.cuts = cuts(part.shape[-1])
        self.sent = []

    def steps(self):
        return [self.start, self.second, self.third, self.fourth, self.finish]

    @staticmethod
    def scratch(columns):
        wide = columns - (columns // 256) * 128
        return [
            pltpu.VMEM((2, 2, 4, ROWS, wide), BF),
            pltpu.VMEM((2, 2, 4, ROWS, columns), BF),
            pltpu.VMEM((2, 2, ROWS, wide), BF),
            pltpu.VMEM((2, 2, ROWS, columns), BF),
        ]

    def group(self, half, q):
        return self.part.at[q, :, 0] if half == 0 else self.part.at[:, q, 1]

    def axes(self, half):
        me = self.me
        return (me.x, me.z, me.xp, me.zp) if half == 0 else (me.z, me.x, me.zp, me.xp)

    def go(self, src, dst, peer):
        copy = self.net.go(src, dst, peer)
        self.sent.append(copy)
        return copy

    def wide(self, i):
        return slice(0, self.cuts[i].stop - self.cuts[i].start)

    def start(self):
        self.one = [[], []]
        for half in range(2):
            p, q, pp, qp = self.axes(half)
            for i, k in enumerate(SIDES):
                piece = self.group(half, (q + 2) % 4).at[:, :, self.cuts[i]]
                self.one[half].append(self.go(piece, self.r1.at[half, i, :, :, self.wide(i)], qp(k)))

    def second(self):
        self.two = [[], []]
        for i, k in enumerate(SIDES):
            for half in range(2):
                p, q, pp, qp = self.axes(half)
                landed([self.one[half][i]])
                mine = self.group(half, (q + k) % 4)

                def add(j, _):
                    mine[j, :, self.cuts[i]] = (
                        mine[j, :, self.cuts[i]].astype(F32) + self.r1[half, i, j, :, self.wide(i)].astype(F32)
                    ).astype(BF)
                    return 0

                lax.fori_loop(0, 4, add, 0)
                self.two[half].append(self.go(mine, self.r2.at[half, i], qp(k)))

    def third(self):
        self.three = [[], []]
        for half in range(2):
            p, q, pp, qp = self.axes(half)
            landed(self.two[half])
            mine = self.group(half, q)

            def add(j, _):
                mine[j] = (
                    mine[j].astype(F32) + self.r2[half, 0, j].astype(F32) + self.r2[half, 1, j].astype(F32)
                ).astype(BF)
                return 0

            lax.fori_loop(0, 4, add, 0)
            for i, k in enumerate(SIDES):
                self.three[half].append(
                    self.go(mine.at[(p + 2) % 4, :, self.cuts[i]], self.u1.at[half, i, :, self.wide(i)], pp(k))
                )

    def fourth(self):
        self.four = [[], []]
        for half in range(2):
            p, q, pp, qp = self.axes(half)
            for i, k in enumerate(SIDES):
                landed([self.three[half][i]])
                block = self.group(half, q).at[(p + k) % 4]
                block[:, self.cuts[i]] = (
                    block[:, self.cuts[i]].astype(F32) + self.u1[half, i, :, self.wide(i)].astype(F32)
                ).astype(BF)
                self.four[half].append(self.go(block, self.u2.at[half, i], pp(k)))

    def finish(self):
        for half in range(2):
            p, q, pp, qp = self.axes(half)
            landed(self.four[half])
            self.out[half] = (
                self.group(half, q)[p].astype(F32) + self.u2[half, 0].astype(F32) + self.u2[half, 1].astype(F32)
            ).astype(BF)
        self.net.left(self.sent)
        if self.then is not None:
            self.then()


class Beside:
    def __init__(self, lag):
        self.lag, self.turn, self.jobs = lag, 0, []

    def add(self, job):
        first = self.turn
        if self.jobs:
            first = max(first, self.jobs[-1][0] + self.lag)
        self.jobs.append((first, list(job.steps()), job))
        return job

    def step(self, count=1):
        for _ in range(count):
            for first, steps, _ in reversed(self.jobs):
                if self.turn >= first and steps:
                    steps.pop(0)()
            self.turn += 1

    def until(self, *jobs):
        while any(steps for _, steps, job in self.jobs if job in jobs):
            self.step()

    def rest(self):
        while any(steps for _, steps, _ in self.jobs):
            self.step()


def dot(a, b, ca=1, cb=0):
    return lax.dot_general(a, b, (((ca,), (cb,)), ((), ())), preferred_element_type=F32)


def unit_rms(u):
    scale = lax.rsqrt(jnp.mean(u * u, axis=1, keepdims=True) + EPS)
    return u * scale, scale


def norm_back(u, gain, dy):
    n, scale = unit_rms(u)
    sd = dy * gain
    return scale * (sd - n * jnp.mean(sd * n, axis=1, keepdims=True)), jnp.sum(dy * n, axis=0, keepdims=True)


def turned(u, cos, sin):
    return u * cos + pltpu.roll(u, 64, 1) * sin


def turned_back(w, cos, sin):
    return w * cos - pltpu.roll(w, 64, 1) * sin


def twice(table):
    return jnp.concatenate([table, table], axis=0)


def key_places(rows):
    j = lax.broadcasted_iota(jnp.int32, (rows, 2048), 1)
    core = j // 1024
    chip = (j % 1024) // TOK
    return chip * (2 * TOK) + core * TOK + j % TOK


def masked(raw, ctx):
    rows = raw.shape[0]
    query = ctx * TOK + lax.broadcasted_iota(jnp.int32, (rows, 2048), 0) % TOK
    return jnp.where(key_places(rows) <= query, raw * (HD**-0.5), -1e30)


def columns_of(i, base=0):
    return pl.ds(pl.multiple_of(base + i * CHUNK, CHUNK), CHUNK)


def attn_forward(me, net, beside, x_ref, gain, bias, cos_ref, sin_ref, wf, weights, hid, q, kv, att, part, got, mid):
    x = x_ref[...]
    normed, _ = unit_rms(x)
    hid[me.y] = (normed * gain).astype(BF)
    hid_copies = [net.go(hid.at[me.y], hid.at[me.y], me.yp(k)) for k in ORDER]
    cos, sin = twice(cos_ref[...]), twice(sin_ref[...])
    weights()
    landed(hid_copies)
    hidden = hid[...].reshape(2 * TOK, D)
    proj = dot(hidden, whole(wf.at[0], slice(0, QKW))) + bias[:, :QKW]
    key = turned(proj[:, 384:], cos, sin).astype(BF)
    value = (dot(hidden, whole(wf.at[1], slice(384, QKW))) + bias[:, QKW:]).astype(BF)
    keyval = jnp.concatenate([key, value], axis=1)
    for m in range(2):
        kv[me.c, m, me.z, me.x] = keyval[m * TOK : (m + 1) * TOK]
    mine0, mine1 = kv.at[me.c, 0, me.z, me.x], kv.at[me.c, 1, me.z, me.x]
    first0 = [net.go(mine0, mine0, me.xp(k)) for k in ORDER]
    first1 = [net.go(mine1, mine1, me.zp(k)) for k in ORDER]
    for head in range(HEADS):
        query = turned(proj[:, head * HD : (head + 1) * HD], cos, sin).astype(BF)
        for m in range(2):
            q[m, head] = query[m * TOK : (m + 1) * TOK]
    beside.step()
    landed(first0)
    second0 = [net.go(kv.at[me.c, 0, me.z], kv.at[me.c, 0, me.z], me.zp(k)) for k in ORDER]
    landed(first1)
    second1 = [net.go(kv.at[me.c, 1, :, me.x], kv.at[me.c, 1, :, me.x], me.xp(k)) for k in ORDER]
    beside.step()
    landed(second0)
    third0 = net.go(kv.at[me.c, 0], kv.at[me.c, 0], me.cp())
    landed(second1)
    third1 = net.go(kv.at[me.c, 1], kv.at[me.c, 1], me.cp())
    for m, third in ((0, third0), (1, third1)):
        beside.step()
        landed([third])
        queries = q[m].reshape(HEADS * TOK, HD)
        keys = kv[:, m, :, :, :, :HD].reshape(2048, HD)
        values = kv[:, m, :, :, :, HD:].reshape(2048, HD)
        scores = masked(dot(queries, keys, 1, 1), me.ctx)
        weight = jnp.exp(scores - jnp.max(scores, axis=1, keepdims=True))
        total = jnp.sum(weight, axis=1, keepdims=True)
        out = (dot(weight.astype(BF), values) / total).astype(BF)
        for head in range(HEADS):
            att[m * TOK : (m + 1) * TOK, head * HD : (head + 1) * HD] = out[head * TOK : (head + 1) * TOK]
    beside.step()
    part[...] = dot(att[...], whole(wf.at[1], slice(0, 384)), 1, 1).astype(BF).reshape(4, OWN, D)
    back = [net.go(part.at[(me.y + k) % 4], got.at[k - 1], me.yp(k)) for k in ORDER]
    beside.step()
    total = x + part[me.y].astype(F32)
    landed(back)
    for k in range(3):
        total = total + got[k].astype(F32)
    mid[...] = total
    net.left(hid_copies + first0 + first1 + second0 + second1 + [third0, third1] + back)


def gather_yc(me, net, buf):
    own = buf.at[me.c, me.y]
    sent = [net.go(own, own, me.yp(k)) for k in ORDER]
    crossed = [net.go(own, own, me.cp())]

    def rest():
        for k, copy in zip(ORDER, sent):
            landed([copy])
            block = buf.at[me.c, (me.y + 4 - k) % 4]
            crossed.append(net.go(block, block, me.cp()))
        landed(crossed)
        return sent + crossed

    return rest


class ScatterYC:
    def __init__(self, me, net, part, mate, got):
        self.me, self.net, self.part, self.mate, self.got = me, net, part, mate, got
        self.swap = net.go(part.at[1 - me.c], mate, me.cp())

    def middle(self):
        me, mate = self.me, self.mate
        landed([self.swap])
        mate[...] = (self.part[me.c].astype(F32) + mate[...].astype(F32)).astype(BF)
        self.back = [self.net.go(mate.at[(me.y + k) % 4], self.got.at[k - 1], me.yp(k)) for k in ORDER]

    def end(self):
        total = self.mate[self.me.y].astype(F32)
        landed(self.back)
        for k in range(3):
            total = total + self.got[k].astype(F32)
        self.net.left([self.swap] + self.back)
        return total


def whole(ref, columns):
    return ref[:, :, :, :, columns].reshape(D, -1)


def mlp_forward(me, net, beside, mid, gain, wg, wu, wd, weights, hid, gate, up, prod, acc, part, mate, got, out):
    normed, _ = unit_rms(mid[...])
    hid[me.c, me.y] = (normed * gain).astype(BF)
    rest = gather_yc(me, net, hid)
    beside.step()
    copies = rest()
    weights(0)
    weights(1)

    def first(i, _):
        cols = columns_of(i)
        gate_part = dot(hid[...].reshape(256, D), whole(wg, cols))
        up_part = dot(hid[...].reshape(256, D), whole(wu, cols))
        gate[:, cols] = gate_part
        up[:, cols] = up_part
        prod[:, cols] = (gate_part * jax.nn.sigmoid(gate_part) * up_part).astype(BF)
        return 0

    lax.fori_loop(0, UNITS // CHUNK, first, 0)
    beside.step()
    weights(2)
    acc[...] = jnp.zeros_like(acc)

    def second(i, _):
        cols = columns_of(i)
        acc[...] += dot(prod[:, cols], whole(wd, cols), 1, 1)
        return 0

    lax.fori_loop(0, UNITS // CHUNK, second, 0)
    part[...] = acc[...].astype(BF).reshape(2, 4, OWN, D)
    scatter = ScatterYC(me, net, part, mate, got)
    beside.step()
    scatter.middle()
    beside.step()
    out[...] = mid[...] + scatter.end()
    return copies


def call(kernel, name, collective_id, ins, outs, scratch):
    names = list(ins) + list(outs) + list(scratch)

    def body(*refs):
        kernel(types.SimpleNamespace(**dict(zip(names, refs))))

    def spec(here):
        return pl.BlockSpec(memory_space=pltpu.VMEM if here else pl.ANY)

    results = pl.pallas_call(
        body,
        out_shape=tuple(jax.ShapeDtypeStruct(shape, dtype) for shape, dtype, _ in outs.values()),
        in_specs=[spec(here) for _, here in ins.values()],
        out_specs=tuple(spec(here) for _, _, here in outs.values()),
        scratch_shapes=list(scratch.values()),
        compiler_params=pltpu.CompilerParams(
            collective_id=collective_id, has_side_effects=True, vmem_limit_bytes=63 << 20
        ),
        name=name,
    )(*[array for array, _ in ins.values()])
    return dict(zip(outs, results))


def sems(local, send, recv):
    return {
        "lsem": pltpu.SemaphoreType.DMA((local,)),
        "send": pltpu.SemaphoreType.DMA((send,)),
        "recv": pltpu.SemaphoreType.DMA((recv,)),
    }


KEPT = {
    "hid": ((4, OWN, D), BF),
    "q": ((2, HEADS, TOK, HD), BF),
    "kv": ((2, 2, 4, 4, TOK, 2 * HD), BF),
    "att": ((2 * TOK, HEADS * HD), BF),
    "wf": ((2, 4, 4, 2, ROWS, QKW), BF),
    "x": ((OWN, D), F32),
    "mid": ((OWN, D), F32),
    "hid2": ((2, 4, OWN, D), BF),
    "gate": ((256, UNITS), F32),
    "up": ((256, UNITS), F32),
    "prod": ((256, UNITS), BF),
    "wg": ((4, 4, 2, ROWS, UNITS), BF),
    "wu": ((4, 4, 2, ROWS, UNITS), BF),
    "wd": ((4, 4, 2, ROWS, UNITS), BF),
}
MLP_PARTS = ("wg", "wu", "wd")


def vmem(shape_dtype):
    return pltpu.VMEM(*shape_dtype)


def forward_kernel(r):
    me = Place()
    me.greet()
    net, local = Links(r.send, r.recv), Local(r.lsem)
    peers = me.quad()
    early, late, arrivals = [], [], []
    for core, section, peer in peers:
        early.append(net.go(r.attn_pieces.at[section, core], r.attn_rows.at[me.s, me.c], peer))
        early.append(net.go(r.tiny, r.tiny_quad.at[me.s, me.c], peer))
    here = [
        local.go(r.attn_pieces.at[me.s, me.c], r.attn_rows.at[me.s, me.c]),
        local.go(r.tiny, r.tiny_quad.at[me.s, me.c]),
    ]
    away = pl.ds(pl.multiple_of((1 - me.s) * OWN, OWN), OWN)
    home = pl.ds(pl.multiple_of(me.s * OWN, OWN), OWN)
    tokens_over = net.go(r.ends.at[me.h, away], r.tokens.at[me.s], {"section": 1 - me.s})
    tokens_here = local.go(r.ends.at[me.h, home], r.tokens.at[me.s])
    for part in range(3):
        over = [
            net.go(r.mlp_pieces.at[part, section, core], r.mlp_rows.at[part, me.s, me.c], peer)
            for core, section, peer in peers
        ]
        kept = local.go(r.mlp_pieces.at[part, me.s, me.c], r.mlp_rows.at[part, me.s, me.c])
        arrivals.append((functools.partial(landed, over), kept.wait))
        late.extend(over)

    beside = Beside(2)
    attn_jobs = [None, None]
    mlp_jobs = [[None] * 3, [None] * 3]

    def add_attn(l):
        buf = getattr(r, f"wf{l}").at[me.c]
        attn_jobs[l] = beside.add(Gather(me, net, local, r.attn_rows.at[l], buf))

    def add_mlp(l, part):
        ready = arrivals[part] if l == 0 else ()
        buf = getattr(r, MLP_PARTS[part] + str(l))
        mlp_jobs[l][part] = beside.add(Gather(me, net, local, r.mlp_rows.at[part, l], buf, ready))

    for copy in here:
        copy.wait()
    landed(early)
    r.tiny_mine[...] = (r.tiny_quad[:, 0].astype(F32) + r.tiny_quad[:, 1].astype(F32)).astype(BF)
    one = [net.go(r.tiny_mine, r.tiny_x.at[k - 1], me.xp(k)) for k in ORDER]
    for l in range(2):
        add_attn(l)
        for part in range(3):
            add_mlp(l, part)
    beside.step()
    landed(one)
    r.tiny_row[...] = (
        r.tiny_mine[...].astype(F32) + r.tiny_x[0].astype(F32) + r.tiny_x[1].astype(F32) + r.tiny_x[2].astype(F32)
    ).astype(BF)
    two = [net.go(r.tiny_row, r.tiny_z.at[k - 1], me.zp(k)) for k in ORDER]
    beside.step()
    landed(two)
    r.small[...] = (
        r.tiny_row[...].astype(F32) + r.tiny_z[0].astype(F32) + r.tiny_z[1].astype(F32) + r.tiny_z[2].astype(F32)
    )

    def gain(l, which):
        return jnp.concatenate([r.small[l, 12 * which + i : 12 * which + i + 1, :] for i in range(12)], axis=1)

    def bias(l):
        rows = [r.small[l, pl.ds(24 + HEADS * me.s + i, 1), :] for i in range(HEADS)]
        rows += [r.small[l, 30 + i : 31 + i, :] for i in range(2)]
        return jnp.concatenate(rows, axis=1)

    for l in range(2):
        for which in range(2):
            r.gains[l, which] = gain(l, which)
    tokens_here.wait()
    landed([tokens_over])
    r.low[me.c, me.y] = r.tokens[1].astype(BF)
    low_rest = []

    saved = []

    def save(l, *names):
        for name in names:
            saved.append(local.go(getattr(r, name + str(l)), getattr(r, "out_" + name + str(l))))

    done = []
    for l in range(2):
        kept = types.SimpleNamespace(**{name: getattr(r, name + str(l)) for name in KEPT})
        if l == 0:
            kept.x[...] = r.tokens[0]

        def attn_weights():
            if l == 0:
                low_rest.append(gather_yc(me, net, r.low))
            beside.until(attn_jobs[l])
            swap = net.go(kept.wf.at[me.c], kept.wf.at[me.c], me.cp())
            landed([swap])
            done.append(swap)

        attn_forward(
            me, net, beside, kept.x, r.gains[l, 0], bias(l), r.cos, r.sin, kept.wf, attn_weights,
            kept.hid, kept.q, kept.kv, kept.att, getattr(r, f"part{l}"), getattr(r, f"got{l}"), kept.mid,
        )
        if l == 0:
            done += low_rest[0]()
        save(l, "hid", "q", "kv", "att", "wf", "x", "mid")
        out = r.out1 if l == 1 else r.out0
        done += mlp_forward(
            me, net, beside, kept.mid, r.gains[l, 1], kept.wg, kept.wu, kept.wd,
            lambda part: beside.until(mlp_jobs[l][part]),
            kept.hid2, kept.gate, kept.up, kept.prod, r.acc, getattr(r, f"wide{l}"), getattr(r, f"mate{l}"),
            getattr(r, f"got2{l}"), out,
        )
        save(l, "hid2", "gate", "up", "prod", "wg", "wu", "wd")
        if l == 0:
            r.x1[...] = out[...].astype(BF).astype(F32)
    beside.rest()
    for copy in saved:
        copy.wait()
    net.left(early + late + [tokens_over] + one + two + done)


def forward(attn_pieces, mlp_pieces, tiny, ends, cos, sin):
    ins = {
        "attn_pieces": (attn_pieces, False), "mlp_pieces": (mlp_pieces, False), "tiny": (tiny, False), "ends": (ends, False),
        "cos": (cos, True), "sin": (sin, True),
    }
    outs = {f"out_{name}{l}": (*KEPT[name], False) for l in range(2) for name in KEPT}
    outs["gains"] = ((2, 2, 1, D), F32, True)
    outs["out1"] = ((OWN, D), F32, True)
    outs["low"] = ((2, 4, OWN, D), BF, True)
    outs["tokens"] = ((2, OWN, D), F32, True)
    scratch = {f"{name}{l}": vmem(KEPT[name]) for l in range(2) for name in KEPT}
    scratch |= {
        "attn_rows": pltpu.VMEM((2, 2, ROWS, QKW), BF),
        "mlp_rows": pltpu.VMEM((3, 2, 2, ROWS, UNITS), BF),
        "tiny_quad": pltpu.VMEM((2, 2, 32, 128), BF),
        "tiny_mine": pltpu.VMEM((2, 32, 128), BF),
        "tiny_x": pltpu.VMEM((3, 2, 32, 128), BF),
        "tiny_row": pltpu.VMEM((2, 32, 128), BF),
        "tiny_z": pltpu.VMEM((3, 2, 32, 128), BF),
        "small": pltpu.VMEM((2, 32, 128), F32),
        "out0": pltpu.VMEM((OWN, D), F32),
        "acc": pltpu.VMEM((256, D), F32),
    }
    for l in range(2):
        scratch |= {
            f"part{l}": pltpu.VMEM((4, OWN, D), BF),
            f"got{l}": pltpu.VMEM((3, OWN, D), BF),
            f"wide{l}": pltpu.VMEM((2, 4, OWN, D), BF),
            f"mate{l}": pltpu.VMEM((4, OWN, D), BF),
            f"got2{l}": pltpu.VMEM((3, OWN, D), BF),
        }
    return call(forward_kernel, "forward", 0, ins, outs, scratch | sems(48, 200, 413))


def attn_backward(me, net, beside, r, gm, load_weights):
    wf, dws = r.wg, r.wu
    r.low2[me.y] = gm.astype(BF)
    own = r.low2.at[me.y]
    gathered = [net.go(own, own, me.yp(k)) for k in ORDER]
    beside.step()
    cos, sin = twice(r.cos[...]), twice(r.sin[...])
    load_weights()
    landed(gathered)
    grad_mid = r.low2[...].reshape(2 * TOK, D)
    grad_att = dot(grad_mid, whole(wf, slice(512, 896))).astype(BF)
    for m in range(2):
        rows = slice(m * TOK, (m + 1) * TOK)
        queries = r.q[m].reshape(HEADS * TOK, HD)
        keys = r.kv[:, m, :, :, :, :HD].reshape(2048, HD)
        values = r.kv[:, m, :, :, :, HD:].reshape(2048, HD)
        grad_out = jnp.concatenate([grad_att[rows, h * HD : (h + 1) * HD] for h in range(HEADS)], axis=0)
        scores = masked(dot(queries, keys, 1, 1), me.ctx)
        weight = jnp.exp(scores - jnp.max(scores, axis=1, keepdims=True))
        soft = weight / jnp.sum(weight, axis=1, keepdims=True)
        grad_soft = dot(grad_out, values, 1, 1)
        delta = jnp.sum(soft * grad_soft, axis=1, keepdims=True)
        grad_scores = (soft * (grad_soft - delta)).astype(BF)
        grad_values = dot(soft.astype(BF), grad_out, 0, 0)
        grad_keys = dot(grad_scores, queries, 0, 0) * (HD**-0.5)
        r.dkv[:, m] = jnp.concatenate([grad_keys, grad_values], axis=1).astype(BF).reshape(2, 4, 4, TOK, 2 * HD)
        dq = dot(grad_scores, keys) * (HD**-0.5)
        for h in range(HEADS):
            r.dqs[rows, h * HD : (h + 1) * HD] = dq[h * TOK : (h + 1) * TOK]
        beside.step()
    swap = net.go(r.dkv.at[1 - me.c], r.kmate, me.cp())
    dq_low = jnp.concatenate(
        [turned_back(r.dqs[:, h * HD : (h + 1) * HD], cos, sin).astype(BF) for h in range(HEADS)], axis=1
    )
    hidden = r.hid[...].reshape(2 * TOK, D)
    landed([swap])
    kmate, kz, kx, k2, k3 = r.kmate, r.kz, r.kx, r.k2, r.k3
    kmate[...] = (kmate[...].astype(F32) + r.dkv[me.c].astype(F32)).astype(BF)
    first0 = [net.go(kmate.at[0, (me.z + k) % 4], kz.at[k - 1], me.zp(k)) for k in ORDER]
    first1 = [net.go(kmate.at[1, :, (me.x + k) % 4], kx.at[k - 1], me.xp(k)) for k in ORDER]

    def blocks(value):
        return value.astype(BF).reshape(4, 4, 2, ROWS, -1)

    dws[:, :, :, :, :384] = blocks(dot(hidden, dq_low, 0, 0))
    dws[:, :, :, :, 512:896] = blocks(dot(grad_mid, r.att[...], 0, 0))
    dws[:, :, :, :, 896:1024] = jnp.zeros((4, 4, 2, ROWS, HD), BF)
    beside.step()
    landed(first0)
    total0 = kmate[0, me.z].astype(F32)
    for k in range(3):
        total0 = total0 + kz[k].astype(F32)
    k2[0] = total0.astype(BF)
    second0 = [net.go(k2.at[0, (me.x + k) % 4], k3.at[0, k - 1], me.xp(k)) for k in ORDER]
    landed(first1)
    total1 = kmate[1, :, me.x].astype(F32)
    for k in range(3):
        total1 = total1 + kx[k].astype(F32)
    k2[1] = total1.astype(BF)
    second1 = [net.go(k2.at[1, (me.z + k) % 4], k3.at[1, k - 1], me.zp(k)) for k in ORDER]
    beside.step()
    landed(second0 + second1)
    for m, place in ((0, me.x), (1, me.z)):
        total = k2[m, place].astype(F32)
        for k in range(3):
            total = total + k3[m, k].astype(F32)
        r.kpair[0, m * TOK : (m + 1) * TOK] = total[:, :HD].astype(BF)
        r.kpair[1, m * TOK : (m + 1) * TOK] = total[:, HD:].astype(BF)
    pair = net.go(r.kpair.at[1 - me.s], r.kpair_got, {"section": 1 - me.s})
    landed([pair])
    total = r.kpair[me.s].astype(F32) + r.kpair_got[...].astype(F32)
    dk_low = jnp.where(me.s == 0, turned_back(total, cos, sin), total).astype(BF)
    w_own = jnp.where(me.s == 0, whole(wf, slice(384, 512)), whole(wf, slice(896, 1024)))
    r.part[...] = (
        (dot(dq_low, whole(wf, slice(0, 384)), 1, 1) + dot(dk_low, w_own, 1, 1)).astype(BF).reshape(4, OWN, D)
    )
    back = [net.go(r.part.at[(me.y + k) % 4], r.got.at[k - 1], me.yp(k)) for k in ORDER]
    dws[:, :, :, :, 384:512] = blocks(dot(hidden, dk_low, 0, 0))

    def half(core):
        return pl.ds(pl.multiple_of(core * QKW, QKW), QKW)

    dw_swap = net.go(dws.at[:, :, :, :, half(1 - me.c)], r.da, me.cp())
    beside.step()
    gbias = jnp.concatenate(
        [jnp.sum(dq_low.astype(F32), axis=0, keepdims=True), jnp.sum(dk_low.astype(F32), axis=0, keepdims=True)], axis=1
    )
    dy = r.part[me.y].astype(F32)
    landed(back)
    for k in range(3):
        dy = dy + r.got[k].astype(F32)
    dx, ggain = norm_back(r.x[...], r.gains[0], dy)
    r.gin[...] = gm + dx
    landed([dw_swap])

    def add(j, _):
        r.da[j] = (dws[j, :, :, :, half(me.c)].astype(F32) + r.da[j].astype(F32)).astype(BF)
        return 0

    lax.fori_loop(0, 4, add, 0)
    net.left(gathered + [swap] + first0 + first1 + second0 + second1 + [pair] + back + [dw_swap])
    return ggain, gbias


def mlp_backward(me, net, beside, r, g, loaded, scatter):
    loaded("prod")

    def weight_grad(dw, left_ref, right_ref):
        def step(i, _):
            cols = columns_of(i)
            dw[:, :, :, :, cols] = (
                dot(left_ref[...].reshape(256, D), right_ref[:, cols], 0, 0).astype(BF).reshape(4, 4, 2, ROWS, CHUNK)
            )
            return 0

        lax.fori_loop(0, UNITS // CHUNK, step, 0)

    weight_grad(r.dd, r.low, r.prod)
    scatter(2)
    beside.step()
    loaded("gate", "up", "wd", "wg", "wu", "hid2")
    r.acc[...] = jnp.zeros_like(r.acc)

    def step(i, _):
        cols = columns_of(i)
        dprod = dot(r.low[...].reshape(256, D), whole(r.wd, cols))
        gate, up = r.gate[:, cols], r.up[:, cols]
        sigma = jax.nn.sigmoid(gate)
        dg = (dprod * up * sigma * (1.0 + gate * (1.0 - sigma))).astype(BF)
        du = (dprod * gate * sigma).astype(BF)
        r.dgate[:, cols] = dg
        r.dup[:, cols] = du
        r.acc[...] += dot(dg, whole(r.wg, cols), 1, 1) + dot(du, whole(r.wu, cols), 1, 1)
        return 0

    lax.fori_loop(0, UNITS // CHUNK, step, 0)
    r.wide[...] = r.acc[...].astype(BF).reshape(2, 4, OWN, D)
    sums = ScatterYC(me, net, r.wide, r.mate, r.got2)
    beside.step()
    weight_grad(r.dg, r.hid2, r.dgate)
    sums.middle()
    scatter(0)
    beside.step()
    weight_grad(r.du, r.hid2, r.dup)
    scatter(1)
    beside.step()
    dy = sums.end()
    du, ggain = norm_back(r.mid[...], r.gains[1], dy)
    return g + du, ggain


def put_small(r, base, y, ggain0, ggain1, gbias):
    r.sums[0, base + 24 : base + 40] = jnp.zeros((16, 128), F32)
    for which, ggain in enumerate((ggain0, ggain1)):
        for i in range(12):
            r.sums[0, base + 12 * which + i : base + 12 * which + i + 1] = ggain[:, i * 128 : (i + 1) * 128]
    for i in range(4):
        r.sums[0, pl.ds(base + 24 + 4 * y + i, 1)] = gbias[:, i * 128 : (i + 1) * 128]


def backward_kernel(last, r):
    me = Place()
    local = Local(r.lsem)
    names = ("prod", "low", "gate", "up", "wd", "wg", "wu", "hid2", "mid", "hid", "q", "kv", "att", "x")
    pending = {}

    def load(name):
        pending[name] = local.go(getattr(r, "in_" + name), getattr(r, name))

    def loaded(*wanted):
        for name in wanted:
            pending.pop(name).wait()

    for name in names:
        if not (last and name == "low"):
            load(name)
    me.greet()
    net = Links(r.send, r.recv)
    beside = Beside(2)
    extra = []
    g = r.g[...]
    if last:
        g = g.astype(BF).astype(F32)
        r.low[me.c, me.y] = g.astype(BF)
        rest = gather_yc(me, net, r.low)
        res = [local.go(r.in_sums1, r.res_m.at[:, 1]), local.go(r.in_out1, r.ends2.at[1])]
        da1 = local.go(r.in_da1, r.da1)
        crossed = []

        def go_home(src, dst):
            for core, section, peer in me.quad():
                crossed.append(net.go(src.at[section, core], dst.at[me.s, me.c], peer))
            extra.append(local.go(src.at[me.s, me.c], dst.at[me.s, me.c]))

        da1.wait()
        beside.add(Scatter(me, net, r.da1, (r.a1_r1, r.a1_r2, r.a1_u1, r.a1_u2), r.res_a.at[1]))
        beside.step()

    def scatter(part):
        dw = (r.dg, r.du, r.dd)[part]
        job = tuple(getattr(r, f"m{part}_{name}") for name in ("r1", "r2", "u1", "u2"))
        if last:
            out = r.res_m.at[part, 0]
            beside.add(Scatter(me, net, dw, job, out, lambda: go_home(r.res_m.at[part], r.m_home.at[part])))
        else:
            beside.add(Scatter(me, net, dw, job, r.sums1.at[part]))

    if last:
        low_copies = rest()
        for copy in res:
            copy.wait()
    loaded("mid", *(() if last else ("low",)))
    gm, ggain1 = mlp_backward(me, net, beside, r, g, loaded, scatter)

    wf_copies = [
        local.go(r.in_wf.at[0], r.wg.at[:, :, :, :, :QKW]), local.go(r.in_wf.at[1], r.wg.at[:, :, :, :, QKW : 2 * QKW])
    ]

    def load_weights():
        for copy in wf_copies:
            copy.wait()
        loaded("hid", "q", "kv", "att", "x")

    ggain0, gbias = attn_backward(me, net, beside, r, gm, load_weights)
    if not last:
        put_small(r, 0, me.y, ggain0, ggain1, gbias)
        r.small1[...] = r.sums[0]
        da_out = local.go(r.da, r.out_da)
        beside.rest()
        da_out.wait()
        return
    beside.add(
        Scatter(
            me, net, r.da, (r.a0_r1, r.a0_r2, r.a0_u1, r.a0_u2), r.res_a.at[0],
            lambda: go_home(r.res_a, r.a_home),
        )
    )
    beside.step()
    r.ends2[0] = r.gin[...]
    for k in ORDER:
        crossed.append(net.go(r.ends2.at[((me.y + k) % 4) % 2], r.boundary.at[me.y], me.yp(k)))
    r.boundary[me.y] = r.ends2[me.s]
    put_small(r, 0, me.y, ggain0, ggain1, gbias)
    r.sums[0, 40:] = r.small1[...]
    rounds = ((me.yp, ORDER, 0), (lambda k: me.cp(), (1,), 3), (me.xp, ORDER, 4), (me.zp, ORDER, 7))
    small = []
    for turn, (peer, ks, slot) in enumerate(rounds):
        sent = [net.go(r.sums.at[turn], r.sums_got.at[slot + k - 1], peer(k)) for k in ks]
        beside.step()
        landed(sent)
        total = r.sums[turn]
        for k in ks:
            total = total + r.sums_got[slot + k - 1]
        r.sums[turn + 1] = total
        small.extend(sent)
    r.small[...] = r.sums[4]
    beside.rest()
    landed(crossed)
    for copy in extra:
        copy.wait()
    net.left(low_copies + crossed + small)


def backward(last, kept, g, gains, cos, sin, more):
    ins = {"in_" + name: (kept[name], False) for name in KEPT}
    ins |= {"g": (g, True), "gains": (gains, True), "cos": (cos, True), "sin": (sin, True)}
    if last:
        ins |= {
            "in_sums1": (more["sums1"], False), "in_out1": (more["out1"], False), "in_da1": (more["out_da"], False),
            "small1": (more["small1"], True),
        }
        outs = {
            "m_home": ((3, 2, 2, ROWS, UNITS), BF, False),
            "a_home": ((2, 2, ROWS, QKW), BF, False),
            "boundary": ((4, OWN, D), F32, True),
            "small": ((80, 128), F32, True),
        }
    else:
        ins["in_low"] = (more["low"], False)
        outs = {
            "sums1": ((3, 2, ROWS, UNITS), BF, True),
            "out_da": ((4, 4, 2, ROWS, QKW), BF, False),
            "small1": ((40, 128), F32, True),
            "gin": ((OWN, D), F32, True),
        }
    scratch = {name: vmem(KEPT[name]) for name in KEPT if name != "wf"}
    blocks = (4, 4, 2, ROWS, UNITS)
    scratch |= {
        "low": pltpu.VMEM((2, 4, OWN, D), BF),
        "dgate": pltpu.VMEM((256, UNITS), BF),
        "dup": pltpu.VMEM((256, UNITS), BF),
        "acc": pltpu.VMEM((256, D), F32),
        "wide": pltpu.VMEM((2, 4, OWN, D), BF),
        "mate": pltpu.VMEM((4, OWN, D), BF),
        "got2": pltpu.VMEM((3, OWN, D), BF),
        "dg": pltpu.VMEM(blocks, BF),
        "du": pltpu.VMEM(blocks, BF),
        "dd": pltpu.VMEM(blocks, BF),
        "low2": pltpu.VMEM((4, OWN, D), BF),
        "dkv": pltpu.VMEM((2, 2, 4, 4, TOK, 2 * HD), BF),
        "kmate": pltpu.VMEM((2, 4, 4, TOK, 2 * HD), BF),
        "kz": pltpu.VMEM((3, 4, TOK, 2 * HD), BF),
        "kx": pltpu.VMEM((3, 4, TOK, 2 * HD), BF),
        "k2": pltpu.VMEM((2, 4, TOK, 2 * HD), BF),
        "k3": pltpu.VMEM((2, 3, TOK, 2 * HD), BF),
        "kpair": pltpu.VMEM((2, 2 * TOK, HD), BF),
        "kpair_got": pltpu.VMEM((2 * TOK, HD), BF),
        "dqs": pltpu.VMEM((2 * TOK, HEADS * HD), F32),
        "da": pltpu.VMEM((4, 4, 2, ROWS, QKW), BF),
        "part": pltpu.VMEM((4, OWN, D), BF),
        "got": pltpu.VMEM((3, OWN, D), BF),
        "sums": pltpu.VMEM((5, 80, 128) if last else (1, 40, 128), F32),
    }
    jobs = {f"m{part}": UNITS for part in range(3)}
    if last:
        jobs |= {"a0": QKW, "a1": QKW}
        scratch |= {
            "gin": pltpu.VMEM((OWN, D), F32),
            "da1": pltpu.VMEM((4, 4, 2, ROWS, QKW), BF),
            "res_m": pltpu.VMEM((3, 2, 2, ROWS, UNITS), BF),
            "res_a": pltpu.VMEM((2, 2, ROWS, QKW), BF),
            "ends2": pltpu.VMEM((2, OWN, D), F32),
            "sums_got": pltpu.VMEM((10, 80, 128), F32),
        }
    for job, columns in jobs.items():
        for name, ref in zip(("r1", "r2", "u1", "u2"), Scatter.scratch(columns)):
            scratch[f"{job}_{name}"] = ref
    return call(
        functools.partial(backward_kernel, last), "backward", 1 + last, ins, outs,
        scratch | (sems(28, 140, 144) if last else sems(28, 80, 84)),
    )


def unit_slices(w):
    padded = jnp.pad(w, ((0, 0), (0, 4 * UNITS - w.shape[1])))
    return padded.reshape(w.shape[0], 2, 2, UNITS).transpose(1, 2, 0, 3)


def body(ends, w_query, w_kv, w_out, w_gate_up, w_down, gains, bias_query, bias_kv):
    me = Place()
    rows = w_query.shape[1]
    wq = w_query[0].reshape(rows, 2, 384)
    wo = w_out[0].reshape(rows, 2, 384)
    attn_pieces = jnp.stack(
        [
            jnp.stack(
                [
                    jnp.concatenate([wq[:, s], w_kv[0, :, 0]], axis=1),
                    jnp.concatenate([wo[:, s], w_kv[0, :, 1]], axis=1),
                ]
            )
            for s in range(2)
        ]
    )
    mlp_pieces = jnp.stack(
        [unit_slices(w_gate_up[0, :, 0]), unit_slices(w_gate_up[0, :, 1]), unit_slices(w_down[0])]
    )
    tiny = jnp.concatenate(
        [
            lax.dynamic_update_slice(jnp.zeros((2, D), BF), gains[0], (0, me.ctx * 48)).reshape(24, 128),
            lax.dynamic_update_slice(
                jnp.zeros((8, 128), BF),
                jnp.concatenate([bias_query[0], bias_kv[0].reshape(2, 4)], axis=0),
                (0, me.ctx * 4),
            ),
        ],
        axis=0,
    )
    positions = (me.ctx * TOK + jnp.arange(TOK, dtype=jnp.int32)).astype(F32)
    inverse = 1.0 / THETA ** (jnp.arange(0, HD, 2, dtype=F32) / HD)
    angles = positions[:, None] * inverse[None, :]
    cos = jnp.concatenate([jnp.cos(angles), jnp.cos(angles)], axis=1)
    sin = jnp.concatenate([-jnp.sin(angles), jnp.sin(angles)], axis=1)

    ahead = forward(attn_pieces, mlp_pieces, tiny, ends[0], cos, sin)
    kept = [{name: ahead[f"out_{name}{l}"] for name in KEPT} for l in range(2)]
    gain_all = ahead["gains"]
    upper = backward(False, kept[1], ahead["tokens"][1], gain_all[1], cos, sin, ahead)
    done = backward(True, kept[0], upper["gin"], gain_all[0], cos, sin, upper | {"out1": ahead["out1"]})

    small = done["small"].reshape(2, 40, 128)
    small = lax.dynamic_index_in_dim(small, me.s, 0, keepdims=False)
    gain_sum = lax.dynamic_index_in_dim(small[:24].reshape(2, 32, 48), me.ctx, 1, keepdims=False)
    bias_sum = small[24:].reshape(2, 2, 4, 32, 4)
    bias_sum = lax.dynamic_index_in_dim(bias_sum, me.h, 0, keepdims=False)
    bias_sum = lax.dynamic_index_in_dim(bias_sum, me.ctx, 2, keepdims=False)

    attn_home = done["a_home"].astype(F32)
    mlp_home = done["m_home"].astype(F32).transpose(3, 0, 1, 2, 4).reshape(rows, 3, 4 * UNITS)
    mlp_home = mlp_home[:, :, : w_down.shape[2]]
    return (
        done["boundary"].reshape(1, 2, TOK, D),
        attn_home[:, 0, :, :384].transpose(1, 0, 2).reshape(1, rows, 768),
        attn_home[:, 0, :, 384:].transpose(1, 0, 2)[None],
        attn_home[:, 1, :, :384].transpose(1, 0, 2).reshape(1, rows, 768),
        mlp_home[:, :2][None],
        mlp_home[:, 2][None],
        gain_sum[None],
        bias_sum[:, :HEADS].reshape(1, 6, 4),
        bias_sum[:, HEADS].reshape(1, 2, 1, 4),
    )


def solution(mesh):
    placed = (
        P("section", None, "ctx", None),
        P("section", "ctx", "shard"),
        P("section", "ctx", None, "shard"),
        P("section", "ctx", "shard"),
        P("section", "ctx", None, "shard"),
        P("section", "ctx", "shard"),
        P("section", None, "ctx"),
        P("section", "shard", "ctx"),
        P("section", None, "shard", "ctx"),
    )
    return jax.shard_map(
        body,
        mesh=mesh,
        in_specs=placed,
        out_specs=(
            P("section", None, "ctx", None),
            P("section", "ctx", "shard"),
            P("section", "ctx", None, "shard"),
            P("section", "ctx", "shard"),
            P("section", "ctx", None, "shard"),
            P("section", "ctx", "shard"),
            P("section", None, "ctx"),
            P("section", "shard", "ctx"),
            P("section", None, "shard", "ctx"),
        ),
        check_vma=False,
    )
```

time: 1020 us -> 456 us (0.45)
  blocking collectives: 377 us -> 0 us
  waiting for transfers between devices: 265 us -> 0 us
  Pallas kernels: 294 us -> 414 us
  local copies, waits for them, and re-layouts: 54.7 us -> 26.2 us
  between operations: 15.1 us -> 1.12 us
    all_gather x1 -> x0, blocking collectives: 313 us -> none  [body(): lax.all_gather(packed, ('section', 'ctx', 'shard'), axis=0, tiled=True)]
    reduce_scatter x4 -> x0, waiting for transfers between devices: 262 us -> none  [own_rows(): lax.psum_scatter(block, 'ctx', scatter_dimension=0, tiled=True, axis_inde...]
    pallas_call x10 -> x3, Pallas kernels: 294 us -> 414 us  [call(): pl.pallas_call(body, out_shape=tuple((jax.ShapeDtypeStruct(shape, dtype)...]
    psum x1 -> x0, blocking collectives: 64 us -> none  [body(): small = lax.psum(small, ('section', 'ctx', 'shard')).reshape(-1)]
    unnamed x99 -> x14, local copies, waits for them, and re-layouts: 25.1 us -> 4.82 us
  transfers between devices with their start and end apart: 9 -> 0, of which waited for: 4 -> 0; matrix products, arithmetic and copies ran while one was open for 1% -> 0% of each run, Pallas kernels for 9% -> 0%
where the time goes in v4:
time: 456 us; the launch traced here: 447 us
  Pallas kernels  414 us (91%)
  local copies, waits for them, and re-layouts  26.2 us (6%)
  other arithmetic  5.74 us (1%)
    pallas_call x3, Pallas kernels, call(): pl.pallas_call(body, out_shape=tuple((jax.ShapeDtypeStruct(shape, dtype)...  414 us

profile of v4, /device:TPU:1, one launch (start us, length us, event | category | flops | bytes accessed | tf_op | source)
XLA Modules:
  0.0 447.5 jit_solution(4953627288042060454)
XLA Ops:
  0.6 0.0 copy-start
  0.7 0.9 dynamic_update_slice.6
  1.6 0.8 copy.35
  2.4 0.7 pad_maximum_fusion.9
  3.1 0.2 dynamic_update_slice.7
  3.3 0.6 pad_maximum_fusion.8.refs_2_
  3.9 0.9 reshape_squeeze.12
  4.8 0.1 fusion.6
  5.0 0.9 fusion.8
  5.9 0.9 reshape_squeeze.13
  6.8 0.1 fusion.7
  7.0 0.7 pad_maximum_fusion.1.refs_0_
  7.7 0.2 fusion.4
  7.9 0.7 pad_maximum_fusion.6
  8.6 0.0 copy-done
  8.6 1.2 fusion.5
  9.8 0.1 copy_bitcast_fusion.3
  10.0 0.0 copy-start.2
  10.0 0.1 reshape.76
  10.2 0.1 reshape.75
  10.4 0.6 copy-done.2
  11.0 0.1 reshape.77
  11.2 1.2 pad_maximum_fusion.refs_1_
  12.4 197.6 %forward.1 = (bf16[4,32,1536]{2,1,0:T(8,128)(2,1)}, bf16[2,3,64,128]{3,2,1,0:T(8,128)(2,1)}, bf16[2,2,4,4,64,256]{5,4,3,2,1,0:T(8,128)(2,1)}, bf16[128,384]{1,0:...) custom-call(bf16[2,2,48,512]{3,2,1,0:T(8,128)(2,1)} %pad_maximum_fus, ...), custom_call_target="tpu_custom_call" | custom-call | tf_op jit(solution)/shard_map/forward/pallas_call | solution.py:507
  210.1 1.3 slice_bitcast_fusion.6
  211.4 1.6 slice_bitcast_fusion.2.refs_14_
  213.0 92.5 %backward.2 = (bf16[3,2,48,1152]{3,2,1,0:T(8,128)(2,1)}, bf16[4,4,2,48,512]{4,3,2,1,0:T(8,128)(2,1)}, f32[40,128]{1,0:T(8,128)}, f32[32,1536]{1,0:T(8,128)}) custom-call(bf16[4,32,1536]{2,1,0:T(8,128)(2,1)} %get-tuple-element.63.refs_0_, bf16[2,3,64,128]{3,2,1,0:T(8,128)(2,1)} %get-tuple-element.64.refs_1_, ...), custom_call_target="tpu_custom_call" | custom-call | tf_op jit(solution)/shard_map/backward/pallas_call | solution.py:507
  305.6 124.2 %backward.3 = (bf16[3,2,2,48,1152]{4,3,2,1,0:T(8,128)(2,1)}, bf16[2,2,48,512]{3,2,1,0:T(8,128)(2,1)}, f32[4,32,1536]{2,1,0:T(8,128)}, f32[80,128]{1,0:T(8,128)}) custom-call(bf16[4,32,1536]{2,1,0:T(8,128)(2,1)} %get-tuple-element.49.refs_0_, bf16[2,3,64,128]{3,2,1,0:T(8,128)(2,1)} %get-tuple-element.50.refs_1_, ...), custom_call_target="tpu_custom_call" | custom-call | tf_op jit(solution)/shard_map/backward/pallas_call | solution.py:507
  429.8 1.5 convert_bitcast_fusion
  431.3 1.4 copy.38
  432.7 3.2 reshape.89
  435.9 1.6 slice_bitcast_fusion
  437.5 0.0 copy-start.3
  437.5 2.1 copy.41
  439.6 2.2 slice_bitcast_fusion.1
  441.8 0.0 copy-done.3
  441.8 0.1 copy.36
  441.9 0.8 reshape.80
  442.7 0.1 copy.37
  442.8 0.8 reshape.81
  443.6 0.6 copy.40
  444.2 0.0 copy-done.4
  444.2 0.3 reshape.86
  444.5 0.7 copy.43
  445.2 0.6 slice_bitcast_fusion.8
  445.8 0.1 reshape.85
  445.9 0.6 constant_dynamic-slice_fusion.2
  446.4 0.9 copy.69
  (28 shorter events, 0.5 us)
Async XLA Ops:
  0.6 8.0 %copy-start = (bf16[1,48,2,4480]{3,2,1,0:T(2,128)(2,1)S(1)}, bf16[1,48,2,4480]{3,2,1,0:T(2,128)(2,1)}, u32[]{:S(2)}) copy-start(bf16[1,48,2,4480]{3,2,1,0:T(2,128)(2,1)} %param.13) | copy-start | bytes 2580484
  10.0 1.0 copy-start.2
  437.5 4.3 copy-start.3
  439.6 4.7 %copy-start.4 = (f32[80,128]{1,0:T(8,128)S(1)}, f32[80,128]{1,0:T(8,128)}, u32[]{:S(2)}) copy-start(f32[80,128]{1,0:T(8,128)} %get-tuple-element.88) | copy-start | bytes 122884
  439.6 6.9 %copy-start.1 = (f32[4,32,1536]{2,1,0:T(8,128)S(1)}, f32[4,32,1536]{2,1,0:T(8,128)}, u32[]{:S(2)}) copy-start(f32[4,32,1536]{2,1,0:T(8,128)} %get-tuple-element.85) | copy-start | bytes 2359300
